TPU v7x, 128 devices: a whole 4x4x4 slice. The times are simulated.
128 devices in a mesh: row: 8 (over y, core), col: 16 (over z, x).
Axes of the slice: x: 4, y: 4, z: 4, core: 2. Of those that a mesh axis runs over, the one named last changes fastest.
Arguments:
- hamiltonian: bfloat16 [2048, 200704], P('row', 'col'), may hold values from -0.0546875 to 0.0546875
- term_now: bfloat16 [100352, 4096], P('row', 'col'), may hold values from -6 to 6
- hamiltonian_ids: int32 [8, 16, 78], P('row', 'col'), may hold values from 0 to 196, as said below
- term_ids: int32 [8, 16, 78], P('row', 'col'), may hold values from 0 to 196, as said below
- product_filter: int32 [4, 16, 32], P(None, 'row', 'col'), may hold values 0 or 1
- term_before: bfloat16 [2048, 4096], P('row', 'col'), may hold values from -6 to 6
- density_in: float32 [2048, 4096], P('row', 'col'), may hold values from -6 to 6
- coefficient: float32 [1], replicated, may hold values from 0.5 to 1.5
Outputs:
- term_next: bfloat16 [2048, 4096], P('row', 'col')
- density_out: float32 [2048, 4096], P('row', 'col')
Inputs may be any that keep to these rules, and one draw needn't show every extreme that they name: `hamiltonian_ids`: in each cell's list the first entries are distinct block positions below 196 and the remaining entries equal 196, meaning no block; each list stores at most 78 blocks, and some list stores exactly 78. `term_ids`: likewise for the term's panels.
All inputs are finite; a program needn't handle non-finite values. No bound on the sum of `product_filter` on one device may be relied on, other than what follows from the above.
Results may differ from a plain program's by a relative error of at most 0.006.
Values may be sent and summed in bfloat16 or wider, within the bound.
No kernel may reach another device: no remote copies, remote signals or barrier semaphores. Data moves between devices by JAX's collectives and lax.ppermute only.
A program may use at most 128 MiB of HBM per device.

v0:
```python
import jax
import jax.numpy as jnp
from jax import lax
from jax.sharding import PartitionSpec as P

BS = 128
KB = 98
WB = 2
STEPS = 4


def from_behind(value, axis, steps):
    count = lax.axis_size(axis)
    pairs = [(source, (source + steps) % count) for source in range(count)]
    return lax.ppermute(value, axis, pairs)


def block_flags(block_list):
    positions = jnp.arange(WB * KB, dtype=jnp.int32)
    return jnp.any(block_list[:, None] == positions[None, :], axis=0)


def masked_panel(panel, block_list, outer, inner_count):
    height, breadth = panel.shape
    blocks = panel.reshape(outer, BS, inner_count, BS)
    keep = block_flags(block_list).reshape(outer, 1, inner_count, 1)
    return jnp.where(keep, blocks, jnp.zeros((), panel.dtype)).reshape(height, breadth)


def step_product(left_side, right_side, filt):
    height = left_side.shape[0]
    result = jnp.dot(left_side, right_side, preferred_element_type=jnp.float32).reshape(
        WB, BS, WB, BS
    )
    keep = filt.reshape(WB, 1, WB, 1) == 1
    return jnp.where(keep, result, jnp.zeros((), jnp.float32)).reshape(height, height)


def per_device(
    hamiltonian,
    term_now,
    hamiltonian_ids,
    term_ids,
    product_filter,
    term_before,
    density_in,
    coefficient,
):
    height = hamiltonian.shape[0]
    left_list = hamiltonian_ids.reshape(-1)
    right_list = term_ids.reshape(-1)
    total = jnp.zeros((height, height), jnp.float32)
    left_panel = hamiltonian
    right_panel = term_now
    for step in range(STEPS):
        if step > 0:
            left_panel, left_list = from_behind((left_panel, left_list), "col", 1)
            right_panel, right_list = from_behind((right_panel, right_list), "row", 1)
        left_side = masked_panel(left_panel, left_list, WB, KB)
        right_side = masked_panel(right_panel, right_list, KB, WB)
        total = total + step_product(left_side, right_side, product_filter[step])
    term_next = (2.0 * total - term_before.astype(jnp.float32)).astype(jnp.bfloat16)
    density_out = density_in + coefficient[0] * term_next.astype(jnp.float32)
    return (term_next, density_out)


def solution(mesh):
    return jax.shard_map(
        per_device,
        mesh=mesh,
        in_specs=(
            P("row", "col"),
            P("row", "col"),
            P("row", "col", None),
            P("row", "col", None),
            P(None, "row", "col"),
            P("row", "col"),
            P("row", "col"),
            P(),
        ),
        out_specs=(P("row", "col"), P("row", "col")),
        check_vma=False,
    )
```

profile of v0, /device:TPU:0, one launch (start us, length us, event | category | flops | bytes accessed | tf_op | source)
XLA Modules:
  0.0 464.4 jit_solution(14885162647364204741)
XLA Ops:
  0.6 1.6 collective-permute-start.1
  2.3 1.5 collective-permute-start
  3.8 9.4 %copy.22 = bf16[12544,256]{0,1:T(8,128)(2,1)} copy(bf16[12544,256]{1,0:T(8,128)(2,1)} %param.9) | data formatting | bytes 12845056 | tf_op args[1]
  13.2 1.7 collective-permute-start.2
  15.1 0.9 broadcast_in_dim.138
  16.0 7.1 %bitcast_select_fusion.7 = bf16[256,12544]{1,0:T(8,128)(2,1)} fusion(bf16[256,12544]{1,0:T(8,128)(2,1)} %param.8, pred[32,8,98,128]{3,2,1,0:T(8,128)(4,1)S(1)} %bitcast.101), kind=kLoop, calls=%fused_computation.7 | loop fusion | flops 3211264 | bytes 16056320 | tf_op jit(solution)/shard_map/jit(_where)/select_n | solution.py:27
  23.8 0.9 broadcast_in_dim.142
  24.8 7.5 %bitcast_select_fusion.6 = bf16[12544,256]{0,1:T(8,128)(2,1)} fusion(bf16[12544,256]{0,1:T(8,128)(2,1)} %copy.22, pred[32,8,98,128]{3,2,1,0:T(8,128)(4,1)S(1)} %bitcast.102), kind=kLoop, calls=%fused_computation.6 | loop fusion | flops 3211264 | bytes 16056320 | tf_op jit(solution)/shard_map/jit(_where)/select_n | solution.py:27
  32.3 5.6 %convolution_select_fusion.3 = f32[2,128,2,128]{3,1,2,0:T(8,128)S(1)} fusion(bf16[2,128,12544,1]{2,1,3,0:T(8,128)(2,1)S(1)} %bitcast.109, bf16[2,128,12544,1]{2,1,0,3:T(8,128)(2,1)} %bitcast.118, pred[2,2]{1,0:T(4,128)(4,1)S(1)} %get-tuple-element.4), kind=kOutput, calls=%fused_computation.15 | convolution fusion | flops 1644232704 | bytes 13107204 | tf_op jit(solution)/shard_map/dot_general | solution.py:32
  38.5 107.1 %collective-permute-done = s32[78]{0:T(128)S(1)} collective-permute-done((s32[78]{0:T(128)}, s32[78]{0:T(128)S(1)}, u32[]{:S(2)}, u32[]{:S(2)}) %collective-permute-start) | collective-permute-done | bytes 344 | tf_op jit(solution)/shard_map/ppermute | solution.py:15
  146.3 6.4 %collective-permute-done.4 = s32[78]{0:T(128)S(1)} collective-permute-done((s32[78]{0:T(128)S(1)}, s32[78]{0:T(128)S(1)}, u32[]{:S(2)}, u32[]{:S(2)}) %collective-permute-start.4) | collective-permute-done | bytes 344 | tf_op jit(solution)/shard_map/ppermute | solution.py:15
  153.3 6.4 %collective-permute-done.8 = s32[78]{0:T(128)S(1)} collective-permute-done((s32[78]{0:T(128)S(1)}, s32[78]{0:T(128)S(1)}, u32[]{:S(2)}, u32[]{:S(2)}) %collective-permute-start.8) | collective-permute-done | bytes 344 | tf_op jit(solution)/shard_map/ppermute | solution.py:15
  160.5 0.9 broadcast_in_dim.148
  161.5 7.2 %bitcast_select_fusion.5 = bf16[256,12544]{1,0:T(8,128)(2,1)} fusion(bf16[256,12544]{1,0:T(8,128)(2,1)} %collective-permute-done.1, pred[32,8,98,128]{3,2,1,0:T(8,128)(4,1)S(1)} %bitcast.103), kind=kLoop, calls=%fused_computation.5 | loop fusion | flops 3211264 | bytes 16056320 | tf_op jit(solution)/shard_map/jit(_where)/select_n | solution.py:27
  169.6 7.2 %bitcast_select_fusion.4 = bf16[12544,256]{0,1:T(8,128)(2,1)} fusion(bf16[12544,256]{0,1:T(8,128)(2,1)} %collective-permute-done.3, pred[32,8,98,128]{3,2,1,0:T(8,128)(4,1)S(1)} %bitcast.104), kind=kLoop, calls=%fused_computation.4 | loop fusion | flops 3211264 | bytes 16056320 | tf_op jit(solution)/shard_map/jit(_where)/select_n | solution.py:27
  176.8 7.5 %fusion.3 = f32[2,128,2,128]{3,1,2,0:T(8,128)S(1)} fusion(f32[2,128,2,128]{3,1,2,0:T(8,128)S(1)} %convolution_select_fusion.3, bf16[2,128,12544,1]{2,1,3,0:T(8,128)(2,1)} %bitcast.113, bf16[2,128,12544,1]{2,1,0,3:T(8,128)(2,1)} %bitcast.116, pred[2,2]{1,0:T(4,128)(4,1)S(1)} %get-tuple-element.3), kind=kOutput, calls=%fused_computation.14 | convolution fusion | flops 1644298240 | bytes 13369348 | tf_op jit(solution)/shard_map/dot_general | solution.py:32
  184.3 117.0 %collective-permute-done.5 = bf16[256,12544]{1,0:T(8,128)(2,1)} collective-permute-done((bf16[256,12544]{1,0:T(8,128)(2,1)}, bf16[256,12544]{1,0:T(8,128)(2,1)}, u32[]{:S(2)}, u32[]{:S(2)}) %collective-permute-start.5) | collective-permute-done | bytes 6422560 | tf_op jit(solution)/shard_map/ppermute | solution.py:15
  302.3 7.2 %bitcast_select_fusion.3 = bf16[256,12544]{1,0:T(8,128)(2,1)} fusion(bf16[256,12544]{1,0:T(8,128)(2,1)} %collective-permute-done.5, pred[32,8,98,128]{3,2,1,0:T(8,128)(4,1)S(1)} %bitcast.105), kind=kLoop, calls=%fused_computation.3 | loop fusion | flops 3211264 | bytes 16056320 | tf_op jit(solution)/shard_map/jit(_where)/select_n | solution.py:27
  310.4 4.4 bitcast_select_fusion.2
  314.8 7.5 %fusion.2 = f32[2,128,2,128]{3,1,2,0:T(8,128)S(1)} fusion(f32[2,128,2,128]{3,1,2,0:T(8,128)S(1)} %fusion.3, bf16[2,128,12544,1]{2,1,3,0:T(8,128)(2,1)} %bitcast.114, bf16[2,128,12544,1]{2,1,0,3:T(8,128)(2,1)} %bitcast.117, pred[2,2]{1,0:T(4,128)(4,1)S(1)} %get-tuple-element.5), kind=kOutput, calls=%fused_computation.12 | convolution fusion | flops 1644298240 | bytes 13369348 | tf_op jit(solution)/shard_map/dot_general | solution.py:32
  322.3 119.0 %collective-permute-done.9 = bf16[256,12544]{1,0:T(8,128)(2,1)} collective-permute-done((bf16[256,12544]{1,0:T(8,128)(2,1)}, bf16[256,12544]{1,0:T(8,128)(2,1)}, u32[]{:S(2)}, u32[]{:S(2)}) %collective-permute-start.9) | collective-permute-done | bytes 6422560 | tf_op jit(solution)/shard_map/ppermute | solution.py:15
  442.2 7.1 %bitcast_select_fusion.1 = bf16[256,12544]{1,0:T(8,128)(2,1)} fusion(bf16[256,12544]{1,0:T(8,128)(2,1)} %collective-permute-done.9, pred[32,8,98,128]{3,2,1,0:T(8,128)(4,1)S(1)} %bitcast.99), kind=kLoop, calls=%fused_computation.1 | loop fusion | flops 3211264 | bytes 16056320 | tf_op jit(solution)/shard_map/jit(_where)/select_n | solution.py:27
  450.3 7.5 %bitcast_select_fusion = bf16[12544,256]{0,1:T(8,128)(2,1)} fusion(bf16[12544,256]{0,1:T(8,128)(2,1)} %collective-permute-done.11, pred[32,8,98,128]{3,2,1,0:T(8,128)(4,1)S(1)} %bitcast.100), kind=kLoop, calls=%fused_computation | loop fusion | flops 3211264 | bytes 16056320 | tf_op jit(solution)/shard_map/jit(_where)/select_n | solution.py:27
  457.8 5.6 %fusion.1 = f32[2,128,2,128]{3,1,2,0:T(8,128)S(1)} fusion(f32[2,128,2,128]{3,1,2,0:T(8,128)S(1)} %fusion.2, bf16[2,128,12544,1]{2,1,3,0:T(8,128)(2,1)S(1)} %bitcast.112, bf16[2,128,12544,1]{2,1,0,3:T(8,128)(2,1)} %bitcast.115, pred[2,2]{1,0:T(4,128)(4,1)S(1)} %get-tuple-element.2), kind=kOutput, calls=%fused_computation.10 | convolution fusion | flops 1644363776 | bytes 13369348 | tf_op jit(solution)/shard_map/dot_general | solution.py:32
  (64 shorter events, 8.6 us)
Async XLA Ops:
  0.6 159.6 %collective-permute-start.1 = (bf16[256,12544]{1,0:T(8,128)(2,1)}, bf16[256,12544]{1,0:T(8,128)(2,1)}, u32[]{:S(2)}, u32[]{:S(2)}) collective-permute-start(bf16[256,12544]{1,0:T(8,128)(2,1)} %param.8), channel_id=1, source_target_pairs={{0,1},{1,2},{2,3},{3,4},{4,5},{5,6},{6,7},{7,8},{8,9},{9,10},{10,1... | collective-permute-start | bytes 19267592 | tf_op jit(solution)/shard_map/ppermute | solution.py:15
  2.3 10.9 %copy-start.4 = (s32[1,1,78]{2,1,0:T(1,128)S(1)}, s32[1,1,78]{2,1,0:T(1,128)}, u32[]{:S(2)}) copy-start(s32[1,1,78]{2,1,0:T(1,128)} %param.11) | copy-start | bytes 940
  2.3 12.6 %copy-start.3 = (s32[1,1,78]{2,1,0:T(1,128)S(1)}, s32[1,1,78]{2,1,0:T(1,128)}, u32[]{:S(2)}) copy-start(s32[1,1,78]{2,1,0:T(1,128)} %param.10) | copy-start | bytes 940
  2.3 143.4 %collective-permute-start = (s32[78]{0:T(128)}, s32[78]{0:T(128)S(1)}, u32[]{:S(2)}, u32[]{:S(2)}) collective-permute-start(s32[78]{0:T(128)} %bitcast.120), channel_id=1, source_target_pairs={{0,1},{1,2},{2,3},{3,4},{4,5},{5,6},{6,7},{7,8},{8,9},{9,10},{10,1... | collective-permute-start | bytes 944 | tf_op jit(solution)/shard_map/ppermute | solution.py:15
  13.2 147.3 %collective-permute-start.3 = (bf16[12544,256]{0,1:T(8,128)(2,1)}, bf16[12544,256]{0,1:T(8,128)(2,1)}, u32[]{:S(2)}, u32[]{:S(2)}) collective-permute-start(bf16[12544,256]{0,1:T(8,128)(2,1)} %copy.22), channel_id=1, source_target_pairs={{0,16},{16,32},{32,48},{48,64},{64,80},{80,96},{96,112},{112,0},{1... | collective-permute-start | bytes 19267592 | tf_op jit(solution)/shard_map/ppermute | solution.py:15
  13.2 132.7 %collective-permute-start.2 = (s32[78]{0:T(128)S(1)}, s32[78]{0:T(128)S(1)}, u32[]{:S(2)}, u32[]{:S(2)}) collective-permute-start(s32[78]{0:T(128)S(1)} %bitcast.122), channel_id=1, source_target_pairs={{0,16},{16,32},{32,48},{48,64},{64,80},{80,96},{96,112},{112,0},{1... | collective-permute-start | bytes 944 | tf_op jit(solution)/shard_map/ppermute | solution.py:15
  16.0 7.5 %copy-start.2 = (s32[4,2,2]{0,2,1:T(2,128)S(1)}, s32[4,2,2]{0,2,1:T(2,128)}, u32[]{:S(2)}) copy-start(s32[4,2,2]{0,2,1:T(2,128)} %param.12) | copy-start | bytes 196
  23.8 8.5 %slice-start = ((s8[6422528]{0:T(1024)(128)(4,1)}), s8[4194304]{0:T(1024)(128)(4,1)S(1)}, s32[]{:S(2)}) async-start(s8[6422528]{0:T(1024)(128)(4,1)} %bitcast.107), calls=%async_computation | async-start | bytes 8388608
  24.8 7.5 %slice-start.1 = ((s8[6422528]{0:T(1024)(128)(4,1)}), s8[2228224]{0:T(1024)(128)(4,1)S(1)}, s32[]{:S(2)}) async-start(s8[6422528]{0:T(1024)(128)(4,1)} %bitcast.107), calls=%async_computation.1 | async-start | bytes 4456448
  145.8 6.9 %collective-permute-start.4 = (s32[78]{0:T(128)S(1)}, s32[78]{0:T(128)S(1)}, u32[]{:S(2)}, u32[]{:S(2)}) collective-permute-start(s32[78]{0:T(128)S(1)} %collective-permute-done), channel_id=1, source_target_pairs={{0,1},{1,2},{2,3},{3,4},{4,5},{5,6},{6,7},{7,8},{8,9},{9,10},{10,1... | collective-permute-start | bytes 944 | tf_op jit(solution)/shard_map/ppermute | solution.py:15
  146.3 6.6 %collective-permute-start.6 = (s32[78]{0:T(128)S(1)}, s32[78]{0:T(128)S(1)}, u32[]{:S(2)}, u32[]{:S(2)}) collective-permute-start(s32[78]{0:T(128)S(1)} %collective-permute-done.2), channel_id=1, source_target_pairs={{0,16},{16,32},{32,48},{48,64},{64,80},{80,96},{96,112},{112,0},{1... | collective-permute-start | bytes 944 | tf_op jit(solution)/shard_map/ppermute | solution.py:15
  152.8 6.9 %collective-permute-start.8 = (s32[78]{0:T(128)S(1)}, s32[78]{0:T(128)S(1)}, u32[]{:S(2)}, u32[]{:S(2)}) collective-permute-start(s32[78]{0:T(128)S(1)} %collective-permute-done.4), channel_id=1, source_target_pairs={{0,1},{1,2},{2,3},{3,4},{4,5},{5,6},{6,7},{7,8},{8,9},{9,10},{10,1... | collective-permute-start | bytes 944 | tf_op jit(solution)/shard_map/ppermute | solution.py:15
  153.3 6.6 %collective-permute-start.10 = (s32[78]{0:T(128)S(1)}, s32[78]{0:T(128)S(1)}, u32[]{:S(2)}, u32[]{:S(2)}) collective-permute-start(s32[78]{0:T(128)S(1)} %collective-permute-done.6), channel_id=1, source_target_pairs={{0,16},{16,32},{32,48},{48,64},{64,80},{80,96},{96,112},{112,0},{1... | collective-permute-start | bytes 944 | tf_op jit(solution)/shard_map/ppermute | solution.py:15
  160.2 141.1 %collective-permute-start.5 = (bf16[256,12544]{1,0:T(8,128)(2,1)}, bf16[256,12544]{1,0:T(8,128)(2,1)}, u32[]{:S(2)}, u32[]{:S(2)}) collective-permute-start(bf16[256,12544]{1,0:T(8,128)(2,1)} %collective-permute-done.1), channel_id=1, source_target_pairs={{0,1},{1,2},{2,3},{3,4},{4,5},{5,6},{6,7},{7,8},{8,9},{9,10},{10,1... | collective-permute-start | bytes 19267592 | tf_op jit(solution)/shard_map/ppermute | solution.py:15
  160.5 140.8 %collective-permute-start.7 = (bf16[12544,256]{0,1:T(8,128)(2,1)}, bf16[12544,256]{0,1:T(8,128)(2,1)S(1)}, u32[]{:S(2)}, u32[]{:S(2)}) collective-permute-start(bf16[12544,256]{0,1:T(8,128)(2,1)} %collective-permute-done.3), channel_id=1, source_target_pairs={{0,16},{16,32},{32,48},{48,64},{64,80},{80,96},{96,112},{112,0},{1... | collective-permute-start | bytes 19267592 | tf_op jit(solution)/shard_map/ppermute | solution.py:15
  301.3 139.9 %collective-permute-start.9 = (bf16[256,12544]{1,0:T(8,128)(2,1)}, bf16[256,12544]{1,0:T(8,128)(2,1)}, u32[]{:S(2)}, u32[]{:S(2)}) collective-permute-start(bf16[256,12544]{1,0:T(8,128)(2,1)} %collective-permute-done.5), channel_id=1, source_target_pairs={{0,1},{1,2},{2,3},{3,4},{4,5},{5,6},{6,7},{7,8},{8,9},{9,10},{10,1... | collective-permute-start | bytes 19267592 | tf_op jit(solution)/shard_map/ppermute | solution.py:15
  301.3 148.0 %collective-permute-start.11 = (bf16[12544,256]{0,1:T(8,128)(2,1)S(1)}, bf16[12544,256]{0,1:T(8,128)(2,1)}, u32[]{:S(2)}, u32[]{:S(2)}) collective-permute-start(bf16[12544,256]{0,1:T(8,128)(2,1)S(1)} %collective-permute-done.7), channel_id=1, source_target_pairs={{0,16},{16,32},{32,48},{48,64},{64,80},{80,96},{96,112},{112,0},{1... | collective-permute-start | bytes 19267592 | tf_op jit(solution)/shard_map/ppermute | solution.py:15
  449.3 8.5 %slice-start.2 = ((s8[6422528]{0:T(1024)(128)(4,1)}), s8[4194304]{0:T(1024)(128)(4,1)S(1)}, s32[]{:S(2)}) async-start(s8[6422528]{0:T(1024)(128)(4,1)} %bitcast.110), calls=%async_computation.2 | async-start | bytes 8388608
  450.2 7.5 %slice-start.3 = ((s8[6422528]{0:T(1024)(128)(4,1)}), s8[2228224]{0:T(1024)(128)(4,1)S(1)}, s32[]{:S(2)}) async-start(s8[6422528]{0:T(1024)(128)(4,1)} %bitcast.110), calls=%async_computation.3 | async-start | bytes 4456448
  457.7 5.9 %copy-start = (f32[256,256]{1,0:T(8,128)S(1)}, f32[256,256]{1,0:T(8,128)}, u32[]{:S(2)}) copy-start(f32[256,256]{1,0:T(8,128)} %param.14) | copy-start | bytes 786436
  457.8 5.9 %copy-start.1 = (bf16[256,256]{1,0:T(8,128)(2,1)S(1)}, bf16[256,256]{1,0:T(8,128)(2,1)}, u32[]{:S(2)}) copy-start(bf16[256,256]{1,0:T(8,128)(2,1)} %param.13) | copy-start | bytes 393220
where the time goes:
time: 465 us; the launch traced here: 464 us
  waiting for transfers between devices  356 us (77%)
  other arithmetic  57 us (12%)
  matrix products  26.1 us (6%)
  local copies, waits for them, and re-layouts  18.6 us (4%)
  starting transfers between devices  5.23 us (1%)
    ppermute x12, waiting for transfers between devices, from_behind(): return lax.ppermute(value, axis, pairs)  356 us
    select_n x8, other arithmetic, masked_panel(): jnp.where(keep, blocks, jnp.zeros((), panel.dtype)).reshape(height, breadth)  55.1 us
    dot_general x4, matrix products, step_product(): jnp.dot(left_side, right_side, preferred_element_type=jnp.float32)  26.1 us
    unnamed x19, local copies, waits for them, and re-layouts  9.45 us
  transfers between devices with their start and end apart: 12, of which 5 were waited for; matrix products, arithmetic and copies ran while one was open for 19% of the time, Pallas kernels for 0%

commit v1 on v0

v1 whole, which is shorter than its diff:
```python
import functools

import jax
import jax.numpy as jnp
from jax import lax
from jax.experimental import pallas as pl
from jax.experimental.pallas import tpu as pltpu
from jax.sharding import PartitionSpec as P

BS = 128
KB = 98
WB = 2
STEPS = 4
MAXB = 78
N_ROW = 8
N_COL = 16
AXES = ("row", "col")
GROUP = 4
LISTED = 100
ZERO = 4 * MAXB


def left_near(i, j):
    if i % 2 == 1:
        return i - 1, j + 1
    return i - 1, j + 3 if j % 4 == 0 else j - 1


def right_near(i, j):
    if i % 2 == 1:
        return i + 1, j - 1
    return i + 1, j + 1 if j % 4 == 2 else j - 3


def left_far(i, j):
    if i % 2 == 1:
        return i - 2, j + 4 if j % 4 == 3 else j
    return None


def right_far(i, j):
    if i % 2 == 1:
        return i + 2, j if j % 4 == 3 else j - 4
    return None


def home_two(i, j):
    if i % 2 == 1:
        return i + 1, j - 1 if j % 4 == 3 else j + 3
    return i + 1, j + 1


def home_three(i, j):
    if i % 2 == 1:
        return i + 2, j - 1 if j % 4 == 3 else j + 3
    return i, j + 1


def home_one(i, j):
    if i % 2 == 1:
        return i + 1, j if j % 4 == 3 else j + 4
    return i + 1, j


def move(value, target):
    pairs = []
    for i in range(N_ROW):
        for j in range(N_COL):
            to = target(i, j)
            if to is not None:
                pairs.append((i * N_COL + j, (to[0] % N_ROW) * N_COL + to[1] % N_COL))
    return lax.ppermute(value, AXES, pairs)


def sources(target):
    found = [0] * (N_ROW * N_COL)
    for i in range(N_ROW):
        for j in range(N_COL):
            to = target(i, j)
            if to is not None:
                found[(to[0] % N_ROW) * N_COL + to[1] % N_COL] = i * N_COL + j
    return found


def gather_blocks_kernel(by_rows, ids_ref, panel_ref, out_ref, sem):
    def start(n, carry):
        place = jnp.minimum(ids_ref[n], WB * KB - 1)
        if by_rows:
            r, k = place // KB, place % KB
        else:
            r, k = place // WB, place % WB
        pltpu.make_async_copy(
            panel_ref.at[
                pl.ds(pl.multiple_of(r * BS, BS), BS), pl.ds(pl.multiple_of(k * BS, BS), BS)
            ],
            out_ref.at[pl.ds(pl.multiple_of(n * BS, BS), BS), :],
            sem,
        ).start()
        return carry

    lax.fori_loop(0, MAXB, start, 0)
    pltpu.make_async_copy(out_ref, out_ref, sem).wait()


def gather_blocks(panel, ids, by_rows):
    return pl.pallas_call(
        functools.partial(gather_blocks_kernel, by_rows),
        out_shape=jax.ShapeDtypeStruct((MAXB * BS, BS), panel.dtype),
        in_specs=[
            pl.BlockSpec(memory_space=pltpu.SMEM),
            pl.BlockSpec(memory_space=pl.ANY),
        ],
        out_specs=pl.BlockSpec(memory_space=pl.ANY),
        scratch_shapes=[pltpu.SemaphoreType.DMA],
        cost_estimate=pl.CostEstimate(
            flops=0, bytes_accessed=2 * MAXB * BS * BS * 2, transcendentals=0
        ),
    )(ids, panel)


def slots_of(ids, base):
    positions = jnp.arange(WB * KB, dtype=jnp.int32)
    hit = ids[:, None] == positions[None, :]
    slot = jnp.min(jnp.where(hit, jnp.arange(MAXB, dtype=jnp.int32)[:, None], MAXB), axis=0)
    return jnp.where(slot == MAXB, ZERO, slot + base)


def matched(left_slots, right_slots):
    left = left_slots.reshape(WB, KB)
    right = right_slots.reshape(KB, WB).T
    both = jnp.any(left != ZERO, axis=0) & jnp.any(right != ZERO, axis=0)
    inner = jnp.arange(KB, dtype=jnp.int32)
    rank = jnp.sum(both[:, None] & (inner[:, None] < inner[None, :]), axis=0)
    chosen = both[:, None] & (rank[:, None] == jnp.arange(LISTED, dtype=jnp.int32)[None, :])
    four = jnp.concatenate([left, right], axis=0)
    listed = ZERO + jnp.sum(jnp.where(chosen[None], four[:, :, None] - ZERO, 0), axis=1)
    count = jnp.sum(both.astype(jnp.int32))
    return listed, (count + GROUP - 1) // GROUP


def multiply(listed_ref, count_ref, product, held, out_ref):
    def block(which, at):
        slot = listed_ref[product, which, at]
        return held[pl.ds(pl.multiple_of(slot * BS, BS), BS), :]

    out_ref[product] = jnp.zeros((WB * BS, WB * BS), jnp.float32)

    def step(t, carry):
        ks = [t * GROUP + q for q in range(GROUP)]
        left = jnp.concatenate(
            [jnp.concatenate([block(r, k) for k in ks], axis=1) for r in range(WB)], axis=0
        )
        right = jnp.concatenate(
            [jnp.concatenate([block(WB + c, k) for k in ks], axis=0) for c in range(WB)], axis=1
        )
        out_ref[product] += jnp.dot(left, right, preferred_element_type=jnp.float32)
        return carry

    lax.fori_loop(0, count_ref[product], step, 0)


def own_kernel(listed_ref, count_ref, left_ref, right_ref, out_ref, held, sems):
    size = MAXB * BS
    held[pl.ds(ZERO * BS, BS), :] = jnp.zeros((BS, BS), held.dtype)
    copies = [
        pltpu.make_async_copy(ref, held.at[pl.ds(n * size, size), :], sems.at[n])
        for n, ref in ((0, left_ref), (2, right_ref))
    ]
    for copy in copies:
        copy.start()
    for copy in copies:
        copy.wait()
    multiply(listed_ref, count_ref, 0, held, out_ref)


def products_kernel(
    odd_ref,
    listed_ref,
    count_ref,
    left_own_ref,
    right_own_ref,
    left_near_ref,
    right_near_ref,
    left_far_ref,
    right_far_ref,
    out_ref,
    held,
    sems,
):
    size = MAXB * BS

    def load(refs):
        for n, ref in enumerate(refs):
            pltpu.make_async_copy(ref, held.at[pl.ds(n * size, size), :], sems.at[n]).start()

    @pl.when(odd_ref[0] == 1)
    def _():
        load((left_far_ref, left_near_ref, right_near_ref, right_far_ref))

    @pl.when(odd_ref[0] == 0)
    def _():
        load((left_near_ref, left_own_ref, right_own_ref, right_near_ref))

    held[pl.ds(ZERO * BS, BS), :] = jnp.zeros((BS, BS), held.dtype)
    for n in range(4):
        part = held.at[pl.ds(n * size, size), :]
        pltpu.make_async_copy(part, part, sems.at[n]).wait()
    for product in range(3):
        multiply(listed_ref, count_ref, product, held, out_ref)


def run_products(kernel, scalars, panels, count):
    return pl.pallas_call(
        kernel,
        out_shape=jax.ShapeDtypeStruct((count, WB * BS, WB * BS), jnp.float32),
        in_specs=[pl.BlockSpec(memory_space=pltpu.SMEM)] * len(scalars)
        + [pl.BlockSpec(memory_space=pl.ANY)] * len(panels),
        out_specs=pl.BlockSpec(memory_space=pltpu.VMEM),
        scratch_shapes=[
            pltpu.VMEM(((ZERO + 1) * BS, BS), jnp.bfloat16),
            pltpu.SemaphoreType.DMA((4,)),
        ],
        compiler_params=pltpu.CompilerParams(vmem_limit_bytes=32 * 1024 * 1024),
        cost_estimate=pl.CostEstimate(
            flops=count * 2 * WB * WB * BS * BS * BS * 40,
            bytes_accessed=len(panels) * MAXB * BS * BS * 2,
            transcendentals=0,
        ),
    )(*scalars, *panels)


def per_device(
    hamiltonian,
    term_now,
    hamiltonian_ids,
    term_ids,
    product_filter,
    term_before,
    density_in,
    coefficient,
):
    left_ids = hamiltonian_ids.reshape(-1)
    right_ids = term_ids.reshape(-1)
    all_ids = lax.all_gather(jnp.stack([left_ids, right_ids]), AXES)

    left_own = gather_blocks(hamiltonian, left_ids, True)
    left_n = move(left_own, left_near)
    left_f = move(left_own, left_far)
    right_own = gather_blocks(term_now, right_ids, False)
    right_n = move(right_own, right_near)
    right_f = move(right_own, right_far)

    me = lax.axis_index("row") * N_COL + lax.axis_index("col")
    odd = lax.axis_index("row") % 2

    def ids_from(target, side):
        return all_ids[jnp.asarray(sources(target), jnp.int32)[me], side]

    near_l, near_r = ids_from(left_near, 0), ids_from(right_near, 1)
    far_l, far_r = ids_from(left_far, 0), ids_from(right_far, 1)
    is_odd = odd == 1
    l1 = slots_of(jnp.where(is_odd, far_l, near_l), 0)
    l2 = slots_of(jnp.where(is_odd, near_l, left_ids), MAXB)
    r1 = slots_of(jnp.where(is_odd, near_r, right_ids), 2 * MAXB)
    r2 = slots_of(jnp.where(is_odd, far_r, near_r), 3 * MAXB)
    lists = [
        matched(jnp.where(is_odd, l2, l1), jnp.where(is_odd, r1, r2)),
        matched(jnp.where(is_odd, l1, l2), jnp.where(is_odd, r1, r2)),
        matched(jnp.where(is_odd, l2, l1), jnp.where(is_odd, r2, r1)),
    ]
    listed = jnp.stack([entry[0] for entry in lists])
    counts = jnp.stack([entry[1] for entry in lists])
    own_listed, own_count = matched(slots_of(left_ids, 0), slots_of(right_ids, 2 * MAXB))

    own = run_products(
        own_kernel, (own_listed[None], own_count[None]), (left_own, right_own), 1
    )
    results = run_products(
        products_kernel,
        (odd.astype(jnp.int32)[None], listed, counts),
        (left_own, right_own, left_n, right_n, left_f, right_f),
        3,
    )
    home = [
        move(results[0], home_two),
        move(results[1], home_three),
        move(results[2], home_one),
    ]
    height = WB * BS

    def kept(result, filt):
        keep = filt.reshape(WB, 1, WB, 1) == 1
        return jnp.where(keep, result.reshape(WB, BS, WB, BS), 0.0).reshape(height, height)

    third = jnp.where(is_odd, product_filter[3], product_filter[1])
    first = jnp.where(is_odd, product_filter[1], product_filter[3])
    total = (
        kept(own[0], product_filter[0])
        + kept(home[0], product_filter[2])
        + kept(home[1], third)
        + kept(home[2], first)
    )
    term_next = (2.0 * total - term_before.astype(jnp.float32)).astype(jnp.bfloat16)
    density_out = density_in + coefficient[0] * term_next.astype(jnp.float32)
    return (term_next, density_out)


def solution(mesh):
    return jax.shard_map(
        per_device,
        mesh=mesh,
        in_specs=(
            P("row", "col"),
            P("row", "col"),
            P("row", "col", None),
            P("row", "col", None),
            P(None, "row", "col"),
            P("row", "col"),
            P("row", "col"),
            P(),
        ),
        out_specs=(P("row", "col"), P("row", "col")),
        check_vma=False,
    )
```

time: 465 us -> 314 us (0.68)
  waiting for transfers between devices: 356 us -> 11.2 us
  Pallas kernels: 0 us -> 172 us
  blocking collectives: 0 us -> 91.2 us
  other arithmetic: 57 us -> 4.32 us
  matrix products: 26.1 us -> 0 us
  starting transfers between devices: 5.23 us -> 15.5 us
  between operations: 1.53 us -> 11.7 us
  local copies, waits for them, and re-layouts: 18.6 us -> 8.68 us
    ppermute x12 -> x7, waiting for transfers between devices: 356 us -> 11.2 us  [move(): return lax.ppermute(value, AXES, pairs)]
    pallas_call x0 -> x4, Pallas kernels: none -> 172 us  [the longest x2 159 us: gather_blocks(): pl.pallas_call(functools.partial(gather_blocks_kernel, by_rows), out_shap...]
    all_gather x0 -> x1, blocking collectives: none -> 91.2 us  [per_device(): all_ids = lax.all_gather(jnp.stack([left_ids, right_ids]), AXES)]
    select_n x8 -> x5, other arithmetic: 55.1 us -> 0.03 us  [the longest x1 0.02 us: per_device(): r2 = slots_of(jnp.where(is_odd, far_r, near_r), 3 * MAXB)]
    dot_general x4 -> x0, matrix products: 26.1 us -> none  [step_product(): jnp.dot(left_side, right_side, preferred_element_type=jnp.float32)]
    ppermute x12 -> x7, starting transfers between devices: 5.23 us -> 15.5 us  [move(): return lax.ppermute(value, AXES, pairs)]
    broadcast_in_dim x20 -> x4, local copies, waits for them, and re-layouts: 8.9 us -> 0.56 us  [kept(): jnp.where(keep, result.reshape(WB, BS, WB, BS), 0.0).reshape(height, height)]
    unnamed x19 -> x24, local copies, waits for them, and re-layouts: 9.45 us -> 3.47 us
  transfers between devices with their start and end apart: 12 -> 7, of which waited for: 5 -> 3; matrix products, arithmetic and copies ran while one was open for 19% -> 2% of each run, Pallas kernels for 0% -> 26%
where the time goes in v1:
time: 314 us
  Pallas kernels  172 us (55%)
  blocking collectives  91.2 us (29%)
  starting transfers between devices  15.5 us (5%)
  between operations  11.7 us (4%)
  waiting for transfers between devices  11.2 us (4%)
  local copies, waits for them, and re-layouts  8.68 us (3%)
  other arithmetic  4.32 us (1%)
    pallas_call x2, Pallas kernels, gather_blocks(): pl.pallas_call(functools.partial(gather_blocks_kernel, by_rows), out_shap...  159 us
    all_gather x1, blocking collectives, per_device(): all_ids = lax.all_gather(jnp.stack([left_ids, right_ids]), AXES)  91.2 us
    ppermute x7, starting transfers between devices, move(): return lax.ppermute(value, AXES, pairs)  15.5 us
    pallas_call x2, Pallas kernels, run_products(): pl.pallas_call(kernel, out_shape=jax.ShapeDtypeStruct((count, WB * BS, WB...  13 us
    ppermute x7, waiting for transfers between devices, move(): return lax.ppermute(value, AXES, pairs)  11.2 us
  transfers between devices with their start and end apart: 7, of which 3 were waited for; matrix products, arithmetic and copies ran while one was open for 2% of the time, Pallas kernels for 26%

profile of v1, /device:TPU:0, one launch (start us, length us, event | category | flops | bytes accessed | tf_op | source)
XLA Modules:
  0.0 314.2 jit_solution(14591908284106255385)
XLA Ops:
  0.6 79.2 %shard_map.131.left_ref.left_own_ref = bf16[9984,128]{1,0:T(8,128)(2,1)} custom-call(s32[78]{0:T(128)} %bitcast.101, bf16[256,12544]{1,0:T(8,128)(2,1)} %panel_ref.2), custom_call_target="tpu_custom_call" | custom-call | bytes 5111808 | tf_op jit(solution)/shard_map/pallas_call | solution.py:106
  79.9 4.8 %collective-permute-start = (bf16[9984,128]{1,0:T(8,128)(2,1)}, bf16[9984,128]{1,0:T(8,128)(2,1)}, u32[]{:S(2)}, u32[]{:S(2)}) collective-permute-start(bf16[9984,128]{1,0:T(8,128)(2,1)} %shard_map.131.left_ref.left_own_ref), channel_id=1, source_target_pairs={{0,115},{1,112},{2,113},{3,114},{4,119},{5,116},{6,117},{7,118},{8... | collective-permute-start | bytes 7667720 | tf_op jit(solution)/shard_map/ppermute | solution.py:72
  84.7 2.2 collective-permute-start.2
  86.9 79.3 %shard_map.132.right_ref.right_own_ref = bf16[9984,128]{1,0:T(8,128)(2,1)} custom-call(s32[78]{0:T(128)} %bitcast.98, bf16[12544,256]{1,0:T(8,128)(2,1)} %panel_ref.3), custom_call_target="tpu_custom_call" | custom-call | bytes 5111808 | tf_op jit(solution)/shard_map/pallas_call | solution.py:106
  166.2 4.1 %collective-permute-start.1 = (bf16[9984,128]{1,0:T(8,128)(2,1)}, bf16[9984,128]{1,0:T(8,128)(2,1)}, u32[]{:S(2)}, u32[]{:S(2)}) collective-permute-start(bf16[9984,128]{1,0:T(8,128)(2,1)} %shard_map.132.right_ref.right_own_ref), channel_id=1, source_target_pairs={{0,29},{1,30},{2,19},{3,16},{4,17},{5,18},{6,23},{7,20},{8,21},{9,... | collective-permute-start | bytes 7667720 | tf_op jit(solution)/shard_map/ppermute | solution.py:72
  170.3 2.1 collective-permute-start.3
  172.5 0.6 dynamic_slice.24
  174.3 0.6 dynamic_slice.26
  176.3 0.6 dynamic_slice.28
  178.0 0.6 dynamic_slice.30
  180.1 91.2 %all-gather.1 = s32[128,2,78]{2,1,0:T(2,128)S(1)} all-gather(s32[1,2,78]{2,1,0:T(2,128)S(1)} %add_bitcast_fusion.4), channel_id=2, replica_groups=mesh['row'=8,'col'=16] {'row','col'}, dimensions={0}, use_global_device_ids=true | all-gather | bytes 80496 | tf_op jit(solution)/shard_map/all_gather | solution.py:244
  275.3 0.7 convert_reduce_fusion.6
  279.0 0.2 select_reduce_fusion.2
  280.2 1.7 copy-done.1
  281.9 9.6 %shard_map.134 = f32[3,256,256]{2,1,0:T(8,128)S(1)} custom-call(s32[1]{0:T(128)} %bitcast.6.odd_ref, s32[3,4,100]{2,1,0:T(4,128)S(1)} %pad_add_fusion.listed_ref, s32[3]{0:T(128)S(1)} %pad_add_fusion.4.count_ref, bf16[9984,128]{1,0:T(8,128)(2,1)S(1)} %copy-done, bf16[9984,128]{1,0:T(8,128)(2,1)S(1)} %copy-done.1, ...), custom_call_target="tpu_custom_call" | custom-call | flops 2013265920 | bytes 15335424 | tf_op jit(solution)/shard_map/pallas_call | solution.py:213
  291.6 0.9 slice_bitcast_fusion.2
  292.5 2.3 collective-permute-start.5
  296.1 1.7 copy-done.2
  297.8 3.4 %shard_map.133 = f32[1,256,256]{2,1,0:T(8,128)S(1)} custom-call(s32[1,4,100]{2,1,0:T(4,128)S(1)} %add_bitcast_fusion.3.listed_ref, s32[1]{0:T(128)} %bitcast.4.count_ref, bf16[9984,128]{1,0:T(8,128)(2,1)S(1)} %copy-done, bf16[9984,128]{1,0:T(8,128)(2,1)S(1)} %copy-done.2), custom_call_target="tpu_custom_call" | custom-call | flops 671088640 | bytes 5111808 | tf_op jit(solution)/shard_map/pallas_call | solution.py:213
  301.1 0.3 compare_reduce_fusion.3
  301.4 4.1 %collective-permute-done.4 = f32[256,256]{1,0:T(8,128)S(1)} collective-permute-done((f32[256,256]{1,0:T(8,128)}, f32[256,256]{1,0:T(8,128)S(1)}, u32[]{:S(2)}, u32[]{:S(2)}) %collective-permute-start.4) | collective-permute-done | bytes 262176 | tf_op jit(solution)/shard_map/ppermute | solution.py:72
  305.5 3.3 %collective-permute-done.5 = f32[256,256]{1,0:T(8,128)S(1)} collective-permute-done((f32[256,256]{1,0:T(8,128)}, f32[256,256]{1,0:T(8,128)S(1)}, u32[]{:S(2)}, u32[]{:S(2)}) %collective-permute-start.5) | collective-permute-done | bytes 262176 | tf_op jit(solution)/shard_map/ppermute | solution.py:72
  308.8 3.9 %collective-permute-done.6 = f32[256,256]{1,0:T(8,128)S(1)} collective-permute-done((f32[256,256]{1,0:T(8,128)}, f32[256,256]{1,0:T(8,128)S(1)}, u32[]{:S(2)}, u32[]{:S(2)}) %collective-permute-start.6) | collective-permute-done | bytes 262176 | tf_op jit(solution)/shard_map/ppermute | solution.py:72
  313.2 1.0 multiply_add_fusion
  (81 shorter events, 4.1 us)
Async XLA Ops:
  79.9 200.3 %collective-permute-start = (bf16[9984,128]{1,0:T(8,128)(2,1)}, bf16[9984,128]{1,0:T(8,128)(2,1)}, u32[]{:S(2)}, u32[]{:S(2)}) collective-permute-start(bf16[9984,128]{1,0:T(8,128)(2,1)} %shard_map.131.left_ref.left_own_ref), channel_id=1, source_target_pairs={{0,115},{1,112},{2,113},{3,114},{4,119},{5,116},{6,117},{7,118},{8... | collective-permute-start | bytes 7667720 | tf_op jit(solution)/shard_map/ppermute | solution.py:72
  84.7 195.5 %collective-permute-start.2 = (bf16[9984,128]{1,0:T(8,128)(2,1)}, bf16[9984,128]{1,0:T(8,128)(2,1)}, u32[]{:S(2)}, u32[]{:S(2)}) collective-permute-start(bf16[9984,128]{1,0:T(8,128)(2,1)} %shard_map.131.left_ref.left_own_ref), channel_id=1, source_target_pairs={{16,112},{17,113},{18,114},{19,119},{20,116},{21,117},{22,118},{23... | collective-permute-start | bytes 7667720 | tf_op jit(solution)/shard_map/ppermute | solution.py:72
  86.8 85.6 %copy-start.11 = (s32[128]{0:T(128)S(1)}, s32[128]{0:T(128)}, u32[]{:S(2)}) copy-start(s32[128]{0:T(128)} %constant.104.clone) | copy-start | bytes 1540
  86.8 87.5 %copy-start.10 = (s32[128]{0:T(128)S(1)}, s32[128]{0:T(128)}, u32[]{:S(2)}) copy-start(s32[128]{0:T(128)} %constant.106.clone) | copy-start | bytes 1540
  86.8 89.4 %copy-start.9 = (s32[128]{0:T(128)S(1)}, s32[128]{0:T(128)}, u32[]{:S(2)}) copy-start(s32[128]{0:T(128)} %constant.105.clone) | copy-start | bytes 1540
  86.8 91.1 %copy-start.8 = (s32[128]{0:T(128)S(1)}, s32[128]{0:T(128)}, u32[]{:S(2)}) copy-start(s32[128]{0:T(128)} %constant.107.clone) | copy-start | bytes 1540
  86.8 93.0 %copy-start.6 = (s32[1,1,78]{2,1,0:T(1,128)S(1)}, s32[1,1,78]{2,1,0:T(1,128)}, u32[]{:S(2)}) copy-start(s32[1,1,78]{2,1,0:T(1,128)} %param.15) | copy-start | bytes 940
  86.9 93.1 %copy-start.7 = (s32[1,1,78]{2,1,0:T(1,128)S(1)}, s32[1,1,78]{2,1,0:T(1,128)}, u32[]{:S(2)}) copy-start(s32[1,1,78]{2,1,0:T(1,128)} %param.14) | copy-start | bytes 940
  86.9 193.3 %copy-start = (bf16[9984,128]{1,0:T(8,128)(2,1)S(1)}, bf16[9984,128]{1,0:T(8,128)(2,1)}, u32[]{:S(2)}) copy-start(bf16[9984,128]{1,0:T(8,128)(2,1)} %shard_map.131.left_ref.left_own_ref) | copy-start | bytes 7667716
  166.2 114.0 %collective-permute-start.1 = (bf16[9984,128]{1,0:T(8,128)(2,1)}, bf16[9984,128]{1,0:T(8,128)(2,1)}, u32[]{:S(2)}, u32[]{:S(2)}) collective-permute-start(bf16[9984,128]{1,0:T(8,128)(2,1)} %shard_map.132.right_ref.right_own_ref), channel_id=1, source_target_pairs={{0,29},{1,30},{2,19},{3,16},{4,17},{5,18},{6,23},{7,20},{8,21},{9,... | collective-permute-start | bytes 7667720 | tf_op jit(solution)/shard_map/ppermute | solution.py:72
  170.3 109.9 %collective-permute-start.3 = (bf16[9984,128]{1,0:T(8,128)(2,1)}, bf16[9984,128]{1,0:T(8,128)(2,1)}, u32[]{:S(2)}, u32[]{:S(2)}) collective-permute-start(bf16[9984,128]{1,0:T(8,128)(2,1)} %shard_map.132.right_ref.right_own_ref), channel_id=1, source_target_pairs={{16,60},{17,61},{18,62},{19,51},{20,48},{21,49},{22,50},{23,55},{2... | collective-permute-start | bytes 7667720 | tf_op jit(solution)/shard_map/ppermute | solution.py:72
  280.2 1.7 copy-start.1
  292.5 13.0 %collective-permute-start.4 = (f32[256,256]{1,0:T(8,128)}, f32[256,256]{1,0:T(8,128)S(1)}, u32[]{:S(2)}, u32[]{:S(2)}) collective-permute-start(f32[256,256]{1,0:T(8,128)} %get-tuple-element.20), channel_id=1, source_target_pairs={{0,17},{1,18},{2,19},{3,20},{4,21},{5,22},{6,23},{7,24},{8,25},{9,... | collective-permute-start | bytes 786440 | tf_op jit(solution)/shard_map/ppermute | solution.py:72
  292.5 16.3 %collective-permute-start.5 = (f32[256,256]{1,0:T(8,128)}, f32[256,256]{1,0:T(8,128)S(1)}, u32[]{:S(2)}, u32[]{:S(2)}) collective-permute-start(f32[256,256]{1,0:T(8,128)} %get-tuple-element.22), channel_id=1, source_target_pairs={{0,1},{1,2},{2,3},{3,4},{4,5},{5,6},{6,7},{7,8},{8,9},{9,10},{10,1... | collective-permute-start | bytes 786440 | tf_op jit(solution)/shard_map/ppermute | solution.py:72
  294.8 17.8 %collective-permute-start.6 = (f32[256,256]{1,0:T(8,128)}, f32[256,256]{1,0:T(8,128)S(1)}, u32[]{:S(2)}, u32[]{:S(2)}) collective-permute-start(f32[256,256]{1,0:T(8,128)} %get-tuple-element.21), channel_id=1, source_target_pairs={{0,16},{1,17},{2,18},{3,19},{4,20},{5,21},{6,22},{7,23},{8,24},{9,... | collective-permute-start | bytes 786440 | tf_op jit(solution)/shard_map/ppermute | solution.py:72
  296.0 1.7 copy-start.2
  297.8 3.4 %copy-start.5 = (s32[4,2,2]{0,2,1:T(2,128)S(1)}, s32[4,2,2]{0,2,1:T(2,128)}, u32[]{:S(2)}) copy-start(s32[4,2,2]{0,2,1:T(2,128)} %param.16) | copy-start | bytes 196
  297.8 15.4 %copy-start.3 = (f32[256,256]{1,0:T(8,128)S(1)}, f32[256,256]{1,0:T(8,128)}, u32[]{:S(2)}) copy-start(f32[256,256]{1,0:T(8,128)} %param.18) | copy-start | bytes 786436
  297.8 15.4 %copy-start.4 = (bf16[256,256]{1,0:T(8,128)(2,1)S(1)}, bf16[256,256]{1,0:T(8,128)(2,1)}, u32[]{:S(2)}) copy-start(bf16[256,256]{1,0:T(8,128)(2,1)} %param.17) | copy-start | bytes 393220

commit v2 on v0

v2 whole, which is shorter than its diff:
```python
import functools

import jax
import jax.numpy as jnp
from jax import lax
from jax.experimental import pallas as pl
from jax.experimental.pallas import tpu as pltpu
from jax.sharding import PartitionSpec as P

BS = 128
KB = 98
WB = 2
STEPS = 4
MAXB = 78
N_ROW = 8
N_COL = 16
AXES = ("row", "col")
GROUP = 8
LANES = 128
KERNEL_VMEM = 8 * 1024 * 1024
STORED = MAXB * BS
TABLE_AT = STORED + BS
TABLE = 16
PACKED = TABLE_AT + TABLE


def left_near(i, j):
    if i % 2 == 1:
        return i - 1, j + 1
    return i - 1, j + 3 if j % 4 == 0 else j - 1


def right_near(i, j):
    if i % 2 == 1:
        return i + 1, j - 1
    return i + 1, j + 1 if j % 4 == 2 else j - 3


def left_far(i, j):
    if i % 2 == 1:
        return i - 2, j + 4 if j % 4 == 3 else j
    return None


def right_far(i, j):
    if i % 2 == 1:
        return i + 2, j if j % 4 == 3 else j - 4
    return None


def home_two(i, j):
    if i % 2 == 1:
        return i + 1, j - 1 if j % 4 == 3 else j + 3
    return i + 1, j + 1


def home_three(i, j):
    if i % 2 == 1:
        return i + 2, j - 1 if j % 4 == 3 else j + 3
    return i, j + 1


def home_one(i, j):
    if i % 2 == 1:
        return i + 1, j if j % 4 == 3 else j + 4
    return i + 1, j


def move(value, target):
    pairs = []
    for i in range(N_ROW):
        for j in range(N_COL):
            to = target(i, j)
            if to is not None:
                pairs.append((i * N_COL + j, (to[0] % N_ROW) * N_COL + to[1] % N_COL))
    return lax.ppermute(value, AXES, pairs)


def gather_blocks_kernel(
    left_ids_ref, right_ids_ref, left_ref, right_ref, left_out, right_out, left_ids, right_ids, id_sems, sems
):
    id_copies = [
        pltpu.make_async_copy(source, target, id_sems.at[n])
        for n, (source, target) in enumerate(
            ((left_ids_ref, left_ids), (right_ids_ref, right_ids))
        )
    ]
    for copy in id_copies:
        copy.start()
    row = lax.broadcasted_iota(jnp.int32, (8, LANES), 0)
    lane = lax.broadcasted_iota(jnp.int32, (8, LANES), 1)
    sides = ((left_ids, left_ref, left_out, KB), (right_ids, right_ref, right_out, WB))
    tables = []
    for side, (ids, panel_ref, out_ref, across) in enumerate(sides):
        id_copies[side].wait()

        def start(n, table):
            place = ids[0, 0, n]
            r, k = place // across, place % across
            pltpu.make_async_copy(
                panel_ref.at[
                    pl.ds(pl.multiple_of(jnp.minimum(r, WB * KB // across - 1) * BS, BS), BS),
                    pl.ds(pl.multiple_of(k * BS, BS), BS),
                ],
                out_ref.at[pl.ds(pl.multiple_of(n * BS, BS), BS), :],
                sems.at[side],
            ).start()
            outer, inner = (r, k) if across == KB else (k, r)
            return jnp.where((row == outer) & (lane == inner), n, table)

        tables.append(
            lax.fori_loop(0, MAXB, start, jnp.full((8, LANES), MAXB, jnp.int32), unroll=13)
        )
    for (_, _, out_ref, _), table in zip(sides, tables):
        out_ref[pl.ds(STORED, BS), :] = jnp.zeros((BS, BS), out_ref.dtype)
        both = jnp.concatenate([table, table], axis=0).astype(jnp.float32)
        out_ref[pl.ds(TABLE_AT, TABLE), :] = both.astype(out_ref.dtype)
    for side, (_, _, out_ref, _) in enumerate(sides):
        blocks = out_ref.at[pl.ds(0, STORED), :]
        pltpu.make_async_copy(blocks, blocks, sems.at[side]).wait()


def gather_blocks(left, right, left_ids, right_ids):
    any_space = pl.BlockSpec(memory_space=pl.ANY)
    return pl.pallas_call(
        gather_blocks_kernel,
        out_shape=[pltpu.VMEM((PACKED, BS), left.dtype)] * 2,
        in_specs=[any_space] * 4,
        out_specs=[pl.BlockSpec(memory_space=pltpu.VMEM)] * 2,
        scratch_shapes=[
            pltpu.SMEM(left_ids.shape, jnp.int32),
            pltpu.SMEM(right_ids.shape, jnp.int32),
            pltpu.SemaphoreType.DMA((2,)),
            pltpu.SemaphoreType.DMA((2,)),
        ],
        compiler_params=pltpu.CompilerParams(vmem_limit_bytes=KERNEL_VMEM),
        cost_estimate=pl.CostEstimate(
            flops=0, bytes_accessed=4 * PACKED * BS * 2, transcendentals=0
        ),
    )(
        left_ids,
        right_ids,
        pltpu.with_memory_space_constraint(left, pltpu.HBM),
        pltpu.with_memory_space_constraint(right, pltpu.HBM),
    )


def slot_words(left, right):
    both = (jnp.minimum(left[0:1], left[1:2]) < MAXB) & (jnp.minimum(right[0:1], right[1:2]) < MAXB)
    slots = (left[0:1], left[1:2], right[0:1], right[1:2])
    word = sum(slot << (8 * n) for n, slot in enumerate(slots))
    return jnp.where(both, word, -1)


def multiply(left_ref, right_ref, words, chosen, out_ref):
    def choose(k, count):
        word = words[k]
        chosen[count] = word
        return count + (word >= 0).astype(jnp.int32)

    count = lax.fori_loop(0, KB, choose, 0, unroll=14)
    nothing = MAXB * 0x01010101
    for q in range(GROUP - 1):
        chosen[count + q] = nothing
    out_ref[...] = jnp.zeros(out_ref.shape, out_ref.dtype)

    def block(ref, word, n):
        slot = lax.shift_right_logical(word, 8 * n) & 0xFF
        return ref[pl.ds(pl.multiple_of(slot * BS, BS), BS), :]

    def step(t, carry):
        words = [chosen[t * GROUP + q] for q in range(GROUP)]
        left = jnp.concatenate(
            [
                jnp.concatenate([block(left_ref, word, r) for word in words], axis=1)
                for r in range(WB)
            ],
            axis=0,
        )
        right = jnp.concatenate(
            [
                jnp.concatenate([block(right_ref, word, WB + c) for word in words], axis=0)
                for c in range(WB)
            ],
            axis=1,
        )
        out_ref[...] += jnp.dot(left, right, preferred_element_type=jnp.float32)
        return carry

    lax.fori_loop(0, (count + GROUP - 1) // GROUP, step, 0)


def table_in(ref):
    return ref[pl.ds(TABLE_AT, TABLE), :].astype(jnp.float32).astype(jnp.int32)


def to_scalars(rows, held, words, sem):
    rows = rows + [rows[0]] * (8 - len(rows))
    held[...] = jnp.concatenate(rows, axis=0)
    copy = pltpu.make_async_copy(held, words, sem)
    copy.start()
    copy.wait()


def masked(filter_ref, step, value):
    rows = []
    for r in range(WB):
        row = []
        for c in range(WB):
            block = value[r * BS : (r + 1) * BS, c * BS : (c + 1) * BS]
            row.append(jnp.where(filter_ref[step, r, c] == 1, block, 0.0))
        rows.append(jnp.concatenate(row, axis=1))
    return jnp.concatenate(rows, axis=0)


def base_kernel(filter_ref, left_ref, right_ref, before_ref, out_ref, product, held, words, chosen, sem):
    to_scalars([slot_words(table_in(left_ref), table_in(right_ref))], held, words, sem)
    multiply(left_ref, right_ref, words.at[0], chosen, product)
    out_ref[...] = 2.0 * masked(filter_ref, 0, product[...]) - before_ref[...].astype(jnp.float32)


def products_kernel(
    left_near_ref,
    right_near_ref,
    left_far_ref,
    right_far_ref,
    left_own_ref,
    right_own_ref,
    two_ref,
    three_ref,
    one_ref,
    held,
    words,
    chosen,
    sem,
):
    odd = lax.axis_index("row") % 2 == 1
    left_near, right_near = table_in(left_near_ref), table_in(right_near_ref)
    left_other = jnp.where(odd, table_in(left_far_ref), table_in(left_own_ref))
    right_other = jnp.where(odd, table_in(right_far_ref), table_in(right_own_ref))
    to_scalars(
        [
            slot_words(left_near, right_near),
            slot_words(left_other, right_near),
            slot_words(left_near, right_other),
        ],
        held,
        words,
        sem,
    )
    multiply(left_near_ref, right_near_ref, words.at[0], chosen, two_ref)

    @pl.when(odd)
    def _():
        multiply(left_far_ref, right_near_ref, words.at[1], chosen, three_ref)
        multiply(left_near_ref, right_far_ref, words.at[2], chosen, one_ref)

    @pl.when(jnp.logical_not(odd))
    def _():
        multiply(left_own_ref, right_near_ref, words.at[1], chosen, three_ref)
        multiply(left_near_ref, right_own_ref, words.at[2], chosen, one_ref)


def final_kernel(
    filter_ref, coefficient_ref, base_ref, two_ref, three_ref, one_ref, density_ref, term_out, density_out
):
    odd = lax.axis_index("row") % 2
    total = (
        masked(filter_ref, 2, two_ref[...])
        + masked(filter_ref, 1 + 2 * odd, three_ref[...])
        + masked(filter_ref, 3 - 2 * odd, one_ref[...])
    )
    term_next = (2.0 * total + base_ref[...]).astype(jnp.bfloat16)
    term_out[...] = term_next
    density_out[...] = density_ref[...] + coefficient_ref[0] * term_next.astype(jnp.float32)


IN_VMEM = pl.BlockSpec(memory_space=pltpu.VMEM)
IN_SMEM = pl.BlockSpec(memory_space=pltpu.SMEM)
PANEL = (WB * BS, WB * BS)
RESULT = jax.ShapeDtypeStruct(PANEL, jnp.float32)
LISTS = [
    pltpu.VMEM((8, LANES), jnp.int32),
    pltpu.SMEM((8, LANES), jnp.int32),
    pltpu.SMEM((LANES,), jnp.int32),
    pltpu.SemaphoreType.DMA,
]


def run_kernel(kernel, in_specs, out_shape, scratch_shapes, products, *args):
    return pl.pallas_call(
        kernel,
        out_shape=out_shape,
        in_specs=in_specs,
        out_specs=[IN_VMEM] * len(out_shape),
        scratch_shapes=scratch_shapes,
        compiler_params=pltpu.CompilerParams(vmem_limit_bytes=KERNEL_VMEM),
        cost_estimate=pl.CostEstimate(
            flops=products * 2 * WB * WB * BS * BS * BS * 40,
            bytes_accessed=4 * len(out_shape) * WB * WB * BS * BS,
            transcendentals=0,
        ),
    )(*args)


def per_device(
    hamiltonian,
    term_now,
    hamiltonian_ids,
    term_ids,
    product_filter,
    term_before,
    density_in,
    coefficient,
):
    left_own, right_own = gather_blocks(hamiltonian, term_now, hamiltonian_ids, term_ids)
    left_n = move(left_own, left_near)
    right_n = move(right_own, right_near)
    left_f = move(left_own, left_far)
    right_f = move(right_own, right_far)

    def in_vmem(panel):
        return pltpu.with_memory_space_constraint(panel, pltpu.VMEM)

    two, three, one = run_kernel(
        products_kernel,
        [IN_VMEM] * 6,
        [RESULT] * 3,
        LISTS,
        3,
        *[in_vmem(panel) for panel in (left_n, right_n, left_f, right_f, left_own, right_own)],
    )
    two, three, one = move(two, home_two), move(three, home_three), move(one, home_one)
    (base,) = run_kernel(
        base_kernel,
        [IN_SMEM] + [IN_VMEM] * 3,
        [RESULT],
        [pltpu.VMEM(PANEL, jnp.float32)] + LISTS,
        1,
        product_filter,
        in_vmem(left_own),
        in_vmem(right_own),
        term_before,
    )
    term_next, density_out = run_kernel(
        final_kernel,
        [IN_SMEM] * 2 + [IN_VMEM] * 5,
        [
            jax.ShapeDtypeStruct(term_before.shape, jnp.bfloat16),
            jax.ShapeDtypeStruct(density_in.shape, jnp.float32),
        ],
        [],
        0,
        product_filter,
        coefficient,
        base,
        two,
        three,
        one,
        density_in,
    )
    return (term_next, density_out)


def solution(mesh):
    return jax.shard_map(
        per_device,
        mesh=mesh,
        in_specs=(
            P("row", "col"),
            P("row", "col"),
            P("row", "col", None),
            P("row", "col", None),
            P(None, "row", "col"),
            P("row", "col"),
            P("row", "col"),
            P(),
        ),
        out_specs=(P("row", "col"), P("row", "col")),
        check_vma=False,
    )
```

time: 465 us -> 103 us (0.22)
  waiting for transfers between devices: 356 us -> 67 us
  other arithmetic: 57 us -> 0 us
  matrix products: 26.1 us -> 0 us
  local copies, waits for them, and re-layouts: 18.6 us -> 3.14 us
  Pallas kernels: 0 us -> 13.7 us
  starting transfers between devices: 5.23 us -> 17.5 us
    ppermute x12 -> x7, waiting for transfers between devices: 356 us -> 67 us  [move(): return lax.ppermute(value, AXES, pairs)]
    select_n x8 -> x0, other arithmetic: 55.1 us -> none  [masked_panel(): jnp.where(keep, blocks, jnp.zeros((), panel.dtype)).reshape(height, breadth)]
    dot_general x4 -> x0, matrix products: 26.1 us -> none  [step_product(): jnp.dot(left_side, right_side, preferred_element_type=jnp.float32)]
    pallas_call x0 -> x4, Pallas kernels: none -> 13.7 us  [the longest x3 7.72 us: run_kernel(): pl.pallas_call(kernel, out_shape=out_shape, in_specs=in_specs, out_specs=...]
    ppermute x12 -> x7, starting transfers between devices: 5.23 us -> 17.5 us  [move(): return lax.ppermute(value, AXES, pairs)]
    broadcast_in_dim x20 -> x0, local copies, waits for them, and re-layouts: 8.9 us -> none  [masked_panel(): jnp.where(keep, blocks, jnp.zeros((), panel.dtype)).reshape(height, breadth)]
    unnamed x19 -> x15, local copies, waits for them, and re-layouts: 9.45 us -> 3.14 us
  transfers between devices with their start and end apart: 12 -> 7, of which waited for: 5 -> 5; matrix products, arithmetic and copies ran while one was open for 19% -> 0% of each run, Pallas kernels for 0% -> 2%
where the time goes in v2:
time: 103 us
  waiting for transfers between devices  67 us (65%)
  starting transfers between devices  17.5 us (17%)
  Pallas kernels  13.7 us (13%)
  local copies, waits for them, and re-layouts  3.14 us (3%)
  between operations  1.37 us (1%)
    ppermute x7, waiting for transfers between devices, move(): return lax.ppermute(value, AXES, pairs)  67 us
    ppermute x7, starting transfers between devices, move(): return lax.ppermute(value, AXES, pairs)  17.5 us
    pallas_call x3, Pallas kernels, run_kernel(): pl.pallas_call(kernel, out_shape=out_shape, in_specs=in_specs, out_specs=...  7.72 us
    pallas_call x1, Pallas kernels, gather_blocks(): pl.pallas_call(gather_blocks_kernel, out_shape=[pltpu.VMEM((PACKED, BS),...  5.96 us
    unnamed x15, local copies, waits for them, and re-layouts  3.14 us
  transfers between devices with their start and end apart: 7, of which 5 were waited for; matrix products, arithmetic and copies ran while one was open for 0% of the time, Pallas kernels for 2%

profile of v2, /device:TPU:0, one launch (start us, length us, event | category | flops | bytes accessed | tf_op | source)
XLA Modules:
  0.0 102.7 jit_solution(4391282968927482480)
XLA Ops:
  0.6 0.0 copy-start.4
  0.6 0.6 copy-done.4
  1.3 0.7 copy-done.5
  1.9 6.0 %shard_map.95 = (bf16[10128,128]{1,0:T(8,128)(2,1)S(1)}, bf16[10128,128]{1,0:T(8,128)(2,1)S(1)}) custom-call(s32[1,1,78]{2,1,0:T(1,128)S(1)} %copy-done.4, s32[1,1,78]{2,1,0:T(1,128)S(1)} %copy-done.5, bf16[256,12544]{1,0:T(8,128)(2,1)} %left_ref.1, bf16[12544,256]{1,0:T(8,128)(2,1)} %right_ref.1), custom_call_target="tpu_custom_call" | custom-call | bytes 10371072 | tf_op jit(solution)/shard_map/pallas_call | solution.py:125
  7.9 3.2 %collective-permute-start = (bf16[10128,128]{1,0:T(8,128)(2,1)S(1)}, bf16[10128,128]{1,0:T(8,128)(2,1)S(1)}, u32[]{:S(2)}, u32[]{:S(2)}) collective-permute-start(bf16[10128,128]{1,0:T(8,128)(2,1)S(1)} %get-tuple-element.7.left_ref.left_own_ref), channel_id=1, source_target_pairs={{0,115},{1,112},{2,113},{3,114},{4,119},{5,116},{6,117},{7,118},{8... | collective-permute-start | bytes 7778312 | tf_op jit(solution)/shard_map/ppermute | solution.py:76
  11.1 2.7 %collective-permute-start.1 = (bf16[10128,128]{1,0:T(8,128)(2,1)S(1)}, bf16[10128,128]{1,0:T(8,128)(2,1)S(1)}, u32[]{:S(2)}, u32[]{:S(2)}) collective-permute-start(bf16[10128,128]{1,0:T(8,128)(2,1)S(1)} %get-tuple-element.8.right_ref.right_own_ref), channel_id=1, source_target_pairs={{0,29},{1,30},{2,19},{3,16},{4,17},{5,18},{6,23},{7,20},{8,21},{9,... | collective-permute-start | bytes 7778312 | tf_op jit(solution)/shard_map/ppermute | solution.py:76
  13.8 0.8 collective-permute-start.2
  14.7 0.8 collective-permute-start.3
  15.5 51.6 %collective-permute-done.left_near_ref = bf16[10128,128]{1,0:T(8,128)(2,1)S(1)} collective-permute-done((bf16[10128,128]{1,0:T(8,128)(2,1)S(1)}, bf16[10128,128]{1,0:T(8,128)(2,1)S(1)}, u32[]{:S(2)}, u32[]{:S(2)}) %collective-permute-start) | collective-permute-done | bytes 2592800 | tf_op jit(solution)/shard_map/ppermute | solution.py:76
  67.1 2.1 %collective-permute-done.1.right_near_ref = bf16[10128,128]{1,0:T(8,128)(2,1)S(1)} collective-permute-done((bf16[10128,128]{1,0:T(8,128)(2,1)S(1)}, bf16[10128,128]{1,0:T(8,128)(2,1)S(1)}, u32[]{:S(2)}, u32[]{:S(2)}) %collective-permute-start.1) | collective-permute-done | bytes 2592800 | tf_op jit(solution)/shard_map/ppermute | solution.py:76
  69.2 0.0 collective-permute-done.2.left_far_ref
  69.2 0.0 collective-permute-done.3.right_far_ref
  69.2 4.2 %shard_map.97 = (f32[256,256]{1,0:T(8,128)}, f32[256,256]{1,0:T(8,128)}, f32[256,256]{1,0:T(8,128)}) custom-call(bf16[10128,128]{1,0:T(8,128)(2,1)S(1)} %collective-permute-done.left_near_ref, bf16[10128,128]{1,0:T(8,128)(2,1)S(1)} %collective-permute-done.1.right_near_ref, bf16[10128,128]{1,0:T(8,128)(2,1)S(1)} %collective-permute-done.2.left_far_ref, ...), custom_call_target="tpu_custom_call" | custom-call | flops 2013265920 | bytes 786432 | tf_op jit(solution)/shard_map/pallas_call | solution.py:291
  73.3 0.0 copy-done
  73.4 7.8 %collective-permute-start.4 = (f32[256,256]{1,0:T(8,128)}, f32[256,256]{1,0:T(8,128)S(1)}, u32[]{:S(2)}, u32[]{:S(2)}) collective-permute-start(f32[256,256]{1,0:T(8,128)} %get-tuple-element.9), channel_id=1, source_target_pairs={{0,17},{1,18},{2,19},{3,20},{4,21},{5,22},{6,23},{7,24},{8,25},{9,... | collective-permute-start | bytes 786440 | tf_op jit(solution)/shard_map/ppermute | solution.py:76
  81.2 1.7 %collective-permute-start.5 = (f32[256,256]{1,0:T(8,128)}, f32[256,256]{1,0:T(8,128)S(1)}, u32[]{:S(2)}, u32[]{:S(2)}) collective-permute-start(f32[256,256]{1,0:T(8,128)} %get-tuple-element.10), channel_id=1, source_target_pairs={{0,1},{1,2},{2,3},{3,4},{4,5},{5,6},{6,7},{7,8},{8,9},{9,10},{10,1... | collective-permute-start | bytes 786440 | tf_op jit(solution)/shard_map/ppermute | solution.py:76
  82.9 0.4 collective-permute-start.6
  83.3 0.1 copy.11.filter_ref
  84.1 1.7 %copy-done.1 = bf16[10128,128]{1,0:T(8,128)(2,1)S(1)} copy-done((bf16[10128,128]{1,0:T(8,128)(2,1)S(1)}, bf16[10128,128]{1,0:T(8,128)(2,1)}, u32[]{:S(2)}) %copy-start.1) | copy-done | bytes 2592792
  85.8 2.1 %shard_map.96.base_ref = f32[256,256]{1,0:T(8,128)S(1)} custom-call(s32[4,2,2]{2,1,0:T(2,128)S(1)} %copy.11.filter_ref, bf16[10128,128]{1,0:T(8,128)(2,1)S(1)} %get-tuple-element.7.left_ref.left_own_ref, bf16[10128,128]{1,0:T(8,128)(2,1)S(1)} %copy-done.1, bf16[256,256]{1,0:T(8,128)(2,1)S(1)} %copy-done.3), custom_call_target="tpu_custom_call" | custom-call | flops 671088640 | bytes 262144 | tf_op jit(solution)/shard_map/pallas_call | solution.py:291
  87.9 2.5 %collective-permute-done.4.two_ref = f32[256,256]{1,0:T(8,128)S(1)} collective-permute-done((f32[256,256]{1,0:T(8,128)}, f32[256,256]{1,0:T(8,128)S(1)}, u32[]{:S(2)}, u32[]{:S(2)}) %collective-permute-start.4) | collective-permute-done | bytes 262176 | tf_op jit(solution)/shard_map/ppermute | solution.py:76
  90.4 10.7 %collective-permute-done.5.three_ref = f32[256,256]{1,0:T(8,128)S(1)} collective-permute-done((f32[256,256]{1,0:T(8,128)}, f32[256,256]{1,0:T(8,128)S(1)}, u32[]{:S(2)}, u32[]{:S(2)}) %collective-permute-start.5) | collective-permute-done | bytes 262176 | tf_op jit(solution)/shard_map/ppermute | solution.py:76
  101.0 0.2 collective-permute-done.6.one_ref
  101.3 1.4 %shard_map.98 = (bf16[256,256]{1,0:T(8,128)(2,1)}, f32[256,256]{1,0:T(8,128)}) custom-call(s32[4,2,2]{2,1,0:T(2,128)S(1)} %copy.11.filter_ref, f32[1]{0:T(128)S(6)} %copy.12.coefficient_ref, f32[256,256]{1,0:T(8,128)S(1)} %shard_map.96.base_ref, f32[256,256]{1,0:T(8,128)S(1)} %collective-permute-done.4.two_ref, ...), custom_call_target="tpu_custom_call" | custom-call | bytes 524288 | tf_op jit(solution)/shard_map/pallas_call | solution.py:291
  (9 shorter events, 0.0 us)
Async XLA Ops:
  0.6 0.7 copy-start.4
  1.3 0.7 copy-start.5
  7.9 65.4 %copy-start = (bf16[10128,128]{1,0:T(8,128)(2,1)}, bf16[10128,128]{1,0:T(8,128)(2,1)S(1)}, u32[]{:S(2)}) copy-start(bf16[10128,128]{1,0:T(8,128)(2,1)S(1)} %get-tuple-element.8.right_ref.right_own_ref) | copy-start | bytes 7778308
  7.9 59.1 %collective-permute-start = (bf16[10128,128]{1,0:T(8,128)(2,1)S(1)}, bf16[10128,128]{1,0:T(8,128)(2,1)S(1)}, u32[]{:S(2)}, u32[]{:S(2)}) collective-permute-start(bf16[10128,128]{1,0:T(8,128)(2,1)S(1)} %get-tuple-element.7.left_ref.left_own_ref), channel_id=1, source_target_pairs={{0,115},{1,112},{2,113},{3,114},{4,119},{5,116},{6,117},{7,118},{8... | collective-permute-start | bytes 7778312 | tf_op jit(solution)/shard_map/ppermute | solution.py:76
  11.1 72.1 %copy-start.6 = (s32[4,2,2]{0,2,1:T(2,128)S(1)}, s32[4,2,2]{0,2,1:T(2,128)}, u32[]{:S(2)}) copy-start(s32[4,2,2]{0,2,1:T(2,128)} %param.12) | copy-start | bytes 196
  11.1 72.9 %copy-start.3 = (bf16[256,256]{1,0:T(8,128)(2,1)S(1)}, bf16[256,256]{1,0:T(8,128)(2,1)}, u32[]{:S(2)}) copy-start(bf16[256,256]{1,0:T(8,128)(2,1)} %before_ref.1) | copy-start | bytes 393220
  11.1 58.0 %collective-permute-start.1 = (bf16[10128,128]{1,0:T(8,128)(2,1)S(1)}, bf16[10128,128]{1,0:T(8,128)(2,1)S(1)}, u32[]{:S(2)}, u32[]{:S(2)}) collective-permute-start(bf16[10128,128]{1,0:T(8,128)(2,1)S(1)} %get-tuple-element.8.right_ref.right_own_ref), channel_id=1, source_target_pairs={{0,29},{1,30},{2,19},{3,16},{4,17},{5,18},{6,23},{7,20},{8,21},{9,... | collective-permute-start | bytes 7778312 | tf_op jit(solution)/shard_map/ppermute | solution.py:76
  13.8 55.3 %collective-permute-start.2 = (bf16[10128,128]{1,0:T(8,128)(2,1)S(1)}, bf16[10128,128]{1,0:T(8,128)(2,1)S(1)}, u32[]{:S(2)}, u32[]{:S(2)}) collective-permute-start(bf16[10128,128]{1,0:T(8,128)(2,1)S(1)} %get-tuple-element.7.left_ref.left_own_ref), channel_id=1, source_target_pairs={{16,112},{17,113},{18,114},{19,119},{20,116},{21,117},{22,118},{23... | collective-permute-start | bytes 7778312 | tf_op jit(solution)/shard_map/ppermute | solution.py:76
  14.7 54.5 %collective-permute-start.3 = (bf16[10128,128]{1,0:T(8,128)(2,1)S(1)}, bf16[10128,128]{1,0:T(8,128)(2,1)S(1)}, u32[]{:S(2)}, u32[]{:S(2)}) collective-permute-start(bf16[10128,128]{1,0:T(8,128)(2,1)S(1)} %get-tuple-element.8.right_ref.right_own_ref), channel_id=1, source_target_pairs={{16,60},{17,61},{18,62},{19,51},{20,48},{21,49},{22,50},{23,55},{2... | collective-permute-start | bytes 7778312 | tf_op jit(solution)/shard_map/ppermute | solution.py:76
  73.4 17.0 %collective-permute-start.4 = (f32[256,256]{1,0:T(8,128)}, f32[256,256]{1,0:T(8,128)S(1)}, u32[]{:S(2)}, u32[]{:S(2)}) collective-permute-start(f32[256,256]{1,0:T(8,128)} %get-tuple-element.9), channel_id=1, source_target_pairs={{0,17},{1,18},{2,19},{3,20},{4,21},{5,22},{6,23},{7,24},{8,25},{9,... | collective-permute-start | bytes 786440 | tf_op jit(solution)/shard_map/ppermute | solution.py:76
  81.2 19.9 %collective-permute-start.5 = (f32[256,256]{1,0:T(8,128)}, f32[256,256]{1,0:T(8,128)S(1)}, u32[]{:S(2)}, u32[]{:S(2)}) collective-permute-start(f32[256,256]{1,0:T(8,128)} %get-tuple-element.10), channel_id=1, source_target_pairs={{0,1},{1,2},{2,3},{3,4},{4,5},{5,6},{6,7},{7,8},{8,9},{9,10},{10,1... | collective-permute-start | bytes 786440 | tf_op jit(solution)/shard_map/ppermute | solution.py:76
  82.9 18.4 %collective-permute-start.6 = (f32[256,256]{1,0:T(8,128)}, f32[256,256]{1,0:T(8,128)S(1)}, u32[]{:S(2)}, u32[]{:S(2)}) collective-permute-start(f32[256,256]{1,0:T(8,128)} %get-tuple-element.11), channel_id=1, source_target_pairs={{0,16},{1,17},{2,18},{3,19},{4,20},{5,21},{6,22},{7,23},{8,24},{9,... | collective-permute-start | bytes 786440 | tf_op jit(solution)/shard_map/ppermute | solution.py:76
  84.0 1.7 %copy-start.1 = (bf16[10128,128]{1,0:T(8,128)(2,1)S(1)}, bf16[10128,128]{1,0:T(8,128)(2,1)}, u32[]{:S(2)}) copy-start(bf16[10128,128]{1,0:T(8,128)(2,1)} %copy-done) | copy-start | bytes 7778308
  85.8 15.5 %copy-start.2 = (f32[256,256]{1,0:T(8,128)S(1)}, f32[256,256]{1,0:T(8,128)}, u32[]{:S(2)}) copy-start(f32[256,256]{1,0:T(8,128)} %density_ref.1) | copy-start | bytes 786436

commit v3 on v2

--- a/solution.py
+++ b/solution.py
@@ -15,7 +15,7 @@
 N_ROW = 8
 N_COL = 16
 AXES = ("row", "col")
-GROUP = 8
+GROUP = 16
 LANES = 128
 KERNEL_VMEM = 8 * 1024 * 1024
 STORED = MAXB * BS
@@ -27,42 +27,42 @@
 def left_near(i, j):
     if i % 2 == 1:
         return i - 1, j + 1
-    return i - 1, j + 3 if j % 4 == 0 else j - 1
+    return i - 1, j - 1 if j % 4 == 1 else j + 3
 
 
 def right_near(i, j):
     if i % 2 == 1:
         return i + 1, j - 1
-    return i + 1, j + 1 if j % 4 == 2 else j - 3
+    return i + 1, j - 3 if j % 4 == 3 else j + 1
 
 
 def left_far(i, j):
     if i % 2 == 1:
-        return i - 2, j + 4 if j % 4 == 3 else j
+        return i - 2, j if j % 4 == 0 else j + 4
     return None
 
 
 def right_far(i, j):
     if i % 2 == 1:
-        return i + 2, j if j % 4 == 3 else j - 4
+        return i + 2, j - 4 if j % 4 == 0 else j
     return None
 
 
 def home_two(i, j):
     if i % 2 == 1:
-        return i + 1, j - 1 if j % 4 == 3 else j + 3
+        return i + 1, j + 3 if j % 4 == 0 else j - 1
     return i + 1, j + 1
 
 
 def home_three(i, j):
     if i % 2 == 1:
-        return i + 2, j - 1 if j % 4 == 3 else j + 3
+        return i + 2, j + 3 if j % 4 == 0 else j - 1
     return i, j + 1
 
 
 def home_one(i, j):
     if i % 2 == 1:
-        return i + 1, j if j % 4 == 3 else j + 4
+        return i + 1, j + 4 if j % 4 == 0 else j
     return i + 1, j
 
 
@@ -97,10 +97,11 @@
         def start(n, table):
             place = ids[0, 0, n]
             r, k = place // across, place % across
+            read = jnp.where(place < WB * KB, place, n)
             pltpu.make_async_copy(
                 panel_ref.at[
-                    pl.ds(pl.multiple_of(jnp.minimum(r, WB * KB // across - 1) * BS, BS), BS),
-                    pl.ds(pl.multiple_of(k * BS, BS), BS),
+                    pl.ds(pl.multiple_of(read // across * BS, BS), BS),
+                    pl.ds(pl.multiple_of(read % across * BS, BS), BS),
                 ],
                 out_ref.at[pl.ds(pl.multiple_of(n * BS, BS), BS), :],
                 sems.at[side],
@@ -219,6 +220,11 @@
     out_ref[...] = 2.0 * masked(filter_ref, 0, product[...]) - before_ref[...].astype(jnp.float32)
 
 
+def send_product(left_ref, right_ref, words, chosen, product, out_ref):
+    multiply(left_ref, right_ref, words, chosen, product)
+    out_ref[...] = product[...].astype(out_ref.dtype)
+
+
 def products_kernel(
     left_near_ref,
     right_near_ref,
@@ -229,6 +235,7 @@
     two_ref,
     three_ref,
     one_ref,
+    product,
     held,
     words,
     chosen,
@@ -248,17 +255,17 @@
         words,
         sem,
     )
-    multiply(left_near_ref, right_near_ref, words.at[0], chosen, two_ref)
+    send_product(left_near_ref, right_near_ref, words.at[0], chosen, product, two_ref)
 
     @pl.when(odd)
     def _():
-        multiply(left_far_ref, right_near_ref, words.at[1], chosen, three_ref)
-        multiply(left_near_ref, right_far_ref, words.at[2], chosen, one_ref)
+        send_product(left_far_ref, right_near_ref, words.at[1], chosen, product, three_ref)
+        send_product(left_near_ref, right_far_ref, words.at[2], chosen, product, one_ref)
 
     @pl.when(jnp.logical_not(odd))
     def _():
-        multiply(left_own_ref, right_near_ref, words.at[1], chosen, three_ref)
-        multiply(left_near_ref, right_own_ref, words.at[2], chosen, one_ref)
+        send_product(left_own_ref, right_near_ref, words.at[1], chosen, product, three_ref)
+        send_product(left_near_ref, right_own_ref, words.at[2], chosen, product, one_ref)
 
 
 def final_kernel(
@@ -266,9 +273,9 @@
 ):
     odd = lax.axis_index("row") % 2
     total = (
-        masked(filter_ref, 2, two_ref[...])
-        + masked(filter_ref, 1 + 2 * odd, three_ref[...])
-        + masked(filter_ref, 3 - 2 * odd, one_ref[...])
+        masked(filter_ref, 2, two_ref[...].astype(jnp.float32))
+        + masked(filter_ref, 1 + 2 * odd, three_ref[...].astype(jnp.float32))
+        + masked(filter_ref, 3 - 2 * odd, one_ref[...].astype(jnp.float32))
     )
     term_next = (2.0 * total + base_ref[...]).astype(jnp.bfloat16)
     term_out[...] = term_next
@@ -315,9 +322,9 @@
 ):
     left_own, right_own = gather_blocks(hamiltonian, term_now, hamiltonian_ids, term_ids)
     left_n = move(left_own, left_near)
+    right_f = move(right_own, right_far)
     right_n = move(right_own, right_near)
     left_f = move(left_own, left_far)
-    right_f = move(right_own, right_far)
 
     def in_vmem(panel):
         return pltpu.with_memory_space_constraint(panel, pltpu.VMEM)
@@ -325,8 +332,8 @@
     two, three, one = run_kernel(
         products_kernel,
         [IN_VMEM] * 6,
-        [RESULT] * 3,
-        LISTS,
+        [jax.ShapeDtypeStruct(PANEL, jnp.bfloat16)] * 3,
+        [pltpu.VMEM(PANEL, jnp.float32)] + LISTS,
         3,
         *[in_vmem(panel) for panel in (left_n, right_n, left_f, right_f, left_own, right_own)],
     )

time: 103 us -> 91.9 us (0.89)
  waiting for transfers between devices: 67 us -> 59.3 us
  Pallas kernels: 13.7 us -> 10.6 us
    ppermute x7, waiting for transfers between devices: 67 us -> 59.3 us  [move(): return lax.ppermute(value, AXES, pairs)]
    pallas_call x1, Pallas kernels: 5.96 us -> 3.99 us  [gather_blocks(): pl.pallas_call(gather_blocks_kernel, out_shape=[pltpu.VMEM((PACKED, BS),...]
    pallas_call x3, Pallas kernels: 7.72 us -> 6.65 us  [run_kernel(): pl.pallas_call(kernel, out_shape=out_shape, in_specs=in_specs, out_specs=...]
  transfers between devices with their start and end apart: 7 -> 7, of which waited for: 5 -> 3; matrix products, arithmetic and copies ran while one was open for 0% -> 0% of each run, Pallas kernels for 2% -> 3%
where the time goes in v3:
time: 91.9 us; the launch traced here: 91.7 us
  waiting for transfers between devices  59.3 us (65%)
  starting transfers between devices  17.3 us (19%)
  Pallas kernels  10.6 us (12%)
  local copies, waits for them, and re-layouts  3.14 us (3%)
  between operations  1.38 us (2%)
    ppermute x7, waiting for transfers between devices, move(): return lax.ppermute(value, AXES, pairs)  59.3 us
    ppermute x7, starting transfers between devices, move(): return lax.ppermute(value, AXES, pairs)  17.3 us
    pallas_call x3, Pallas kernels, run_kernel(): pl.pallas_call(kernel, out_shape=out_shape, in_specs=in_specs, out_specs=...  6.65 us
    pallas_call x1, Pallas kernels, gather_blocks(): pl.pallas_call(gather_blocks_kernel, out_shape=[pltpu.VMEM((PACKED, BS),...  3.99 us
    unnamed x15, local copies, waits for them, and re-layouts  3.14 us
  transfers between devices with their start and end apart: 7, of which 3 were waited for; matrix products, arithmetic and copies ran while one was open for 0% of the time, Pallas kernels for 3%

profile of v3, /device:TPU:0, one launch (start us, length us, event | category | flops | bytes accessed | tf_op | source)
XLA Modules:
  0.0 91.7 jit_solution(7653792235672651003)
XLA Ops:
  0.6 0.0 copy-start.4
  0.6 0.6 copy-done.4
  1.3 0.7 copy-done.5
  1.9 4.0 %shard_map.95 = (bf16[10128,128]{1,0:T(8,128)(2,1)S(1)}, bf16[10128,128]{1,0:T(8,128)(2,1)S(1)}) custom-call(s32[1,1,78]{2,1,0:T(1,128)S(1)} %copy-done.4, s32[1,1,78]{2,1,0:T(1,128)S(1)} %copy-done.5, bf16[256,12544]{1,0:T(8,128)(2,1)} %left_ref.1, bf16[12544,256]{1,0:T(8,128)(2,1)} %right_ref.1), custom_call_target="tpu_custom_call" | custom-call | bytes 10371072 | tf_op jit(solution)/shard_map/pallas_call | solution.py:126
  6.0 4.8 %collective-permute-start = (bf16[10128,128]{1,0:T(8,128)(2,1)S(1)}, bf16[10128,128]{1,0:T(8,128)(2,1)S(1)}, u32[]{:S(2)}, u32[]{:S(2)}) collective-permute-start(bf16[10128,128]{1,0:T(8,128)(2,1)S(1)} %get-tuple-element.7.left_ref.left_own_ref), channel_id=1, source_target_pairs={{0,115},{1,112},{2,117},{3,118},{4,119},{5,116},{6,121},{7,122},{8... | collective-permute-start | bytes 7778312 | tf_op jit(solution)/shard_map/ppermute | solution.py:76
  10.8 0.0 collective-permute-start.1
  10.8 0.9 %collective-permute-start.2 = (bf16[10128,128]{1,0:T(8,128)(2,1)S(1)}, bf16[10128,128]{1,0:T(8,128)(2,1)S(1)}, u32[]{:S(2)}, u32[]{:S(2)}) collective-permute-start(bf16[10128,128]{1,0:T(8,128)(2,1)S(1)} %get-tuple-element.7.left_ref.left_own_ref), channel_id=1, source_target_pairs={{16,112},{17,117},{18,118},{19,119},{20,116},{21,121},{22,122},{23... | collective-permute-start | bytes 7778312 | tf_op jit(solution)/shard_map/ppermute | solution.py:76
  11.7 0.8 collective-permute-start.3
  12.6 53.4 %collective-permute-done.left_near_ref = bf16[10128,128]{1,0:T(8,128)(2,1)S(1)} collective-permute-done((bf16[10128,128]{1,0:T(8,128)(2,1)S(1)}, bf16[10128,128]{1,0:T(8,128)(2,1)S(1)}, u32[]{:S(2)}, u32[]{:S(2)}) %collective-permute-start) | collective-permute-done | bytes 2592800 | tf_op jit(solution)/shard_map/ppermute | solution.py:76
  66.0 1.4 %collective-permute-done.1.right_near_ref = bf16[10128,128]{1,0:T(8,128)(2,1)S(1)} collective-permute-done((bf16[10128,128]{1,0:T(8,128)(2,1)S(1)}, bf16[10128,128]{1,0:T(8,128)(2,1)S(1)}, u32[]{:S(2)}, u32[]{:S(2)}) %collective-permute-start.1) | collective-permute-done | bytes 2592800 | tf_op jit(solution)/shard_map/ppermute | solution.py:76
  67.4 0.0 collective-permute-done.2.left_far_ref
  67.4 0.0 collective-permute-done.3.right_far_ref
  67.4 2.8 %shard_map.97 = (bf16[256,256]{1,0:T(8,128)(2,1)S(1)}, bf16[256,256]{1,0:T(8,128)(2,1)S(1)}, bf16[256,256]{1,0:T(8,128)(2,1)S(1)}) custom-call(bf16[10128,128]{1,0:T(8,128)(2,1)S(1)} %collective-permute-done.left_near_ref, bf16[10128,128]{1,0:T(8,128)(2,1)S(1)} %collective-permute-done.1.right_near_ref, ...), custom_call_target="tpu_custom_call" | custom-call | flops 2013265920 | bytes 786432 | tf_op jit(solution)/shard_map/pallas_call | solution.py:298
  70.2 8.2 %collective-permute-start.4 = (bf16[256,256]{1,0:T(8,128)(2,1)S(1)}, bf16[256,256]{1,0:T(8,128)(2,1)S(1)}, u32[]{:S(2)}, u32[]{:S(2)}) collective-permute-start(bf16[256,256]{1,0:T(8,128)(2,1)S(1)} %get-tuple-element.9), channel_id=1, source_target_pairs={{0,17},{1,18},{2,19},{3,20},{4,21},{5,22},{6,23},{7,24},{8,25},{9,... | collective-permute-start | bytes 393224 | tf_op jit(solution)/shard_map/ppermute | solution.py:76
  78.4 1.1 %collective-permute-start.5 = (bf16[256,256]{1,0:T(8,128)(2,1)S(1)}, bf16[256,256]{1,0:T(8,128)(2,1)S(1)}, u32[]{:S(2)}, u32[]{:S(2)}) collective-permute-start(bf16[256,256]{1,0:T(8,128)(2,1)S(1)} %get-tuple-element.10), channel_id=1, source_target_pairs={{0,1},{1,2},{2,3},{3,4},{4,5},{5,6},{6,7},{7,8},{8,9},{9,10},{10,1... | collective-permute-start | bytes 393224 | tf_op jit(solution)/shard_map/ppermute | solution.py:76
  79.6 1.4 %collective-permute-start.6 = (bf16[256,256]{1,0:T(8,128)(2,1)S(1)}, bf16[256,256]{1,0:T(8,128)(2,1)S(1)}, u32[]{:S(2)}, u32[]{:S(2)}) collective-permute-start(bf16[256,256]{1,0:T(8,128)(2,1)S(1)} %get-tuple-element.11), channel_id=1, source_target_pairs={{0,16},{1,17},{2,18},{3,19},{4,20},{5,21},{6,22},{7,23},{8,24},{9,... | collective-permute-start | bytes 393224 | tf_op jit(solution)/shard_map/ppermute | solution.py:76
  80.9 0.0 copy-done.6
  80.9 0.1 copy.11.filter_ref
  81.7 1.7 %copy-done.1 = bf16[10128,128]{1,0:T(8,128)(2,1)S(1)} copy-done((bf16[10128,128]{1,0:T(8,128)(2,1)S(1)}, bf16[10128,128]{1,0:T(8,128)(2,1)}, u32[]{:S(2)}) %copy-start.1) | copy-done | bytes 2592792
  83.4 2.4 %shard_map.96.base_ref = f32[256,256]{1,0:T(8,128)S(1)} custom-call(s32[4,2,2]{2,1,0:T(2,128)S(1)} %copy.11.filter_ref, bf16[10128,128]{1,0:T(8,128)(2,1)S(1)} %get-tuple-element.7.left_ref.left_own_ref, bf16[10128,128]{1,0:T(8,128)(2,1)S(1)} %copy-done.1, bf16[256,256]{1,0:T(8,128)(2,1)S(1)} %copy-done.3), custom_call_target="tpu_custom_call" | custom-call | flops 671088640 | bytes 262144 | tf_op jit(solution)/shard_map/pallas_call | solution.py:298
  85.8 0.0 collective-permute-done.4.two_ref
  85.8 4.4 %collective-permute-done.5.three_ref = bf16[256,256]{1,0:T(8,128)(2,1)S(1)} collective-permute-done((bf16[256,256]{1,0:T(8,128)(2,1)S(1)}, bf16[256,256]{1,0:T(8,128)(2,1)S(1)}, u32[]{:S(2)}, u32[]{:S(2)}) %collective-permute-start.5) | collective-permute-done | bytes 131104 | tf_op jit(solution)/shard_map/ppermute | solution.py:76
  90.3 0.0 collective-permute-done.6.one_ref
  90.3 1.5 %shard_map.98 = (bf16[256,256]{1,0:T(8,128)(2,1)}, f32[256,256]{1,0:T(8,128)}) custom-call(s32[4,2,2]{2,1,0:T(2,128)S(1)} %copy.11.filter_ref, f32[1]{0:T(128)S(6)} %copy.12.coefficient_ref, f32[256,256]{1,0:T(8,128)S(1)} %shard_map.96.base_ref, bf16[256,256]{1,0:T(8,128)(2,1)S(1)} %collective-permute-done.4.two_ref, ...), custom_call_target="tpu_custom_call" | custom-call | bytes 524288 | tf_op jit(solution)/shard_map/pallas_call | solution.py:298
  (9 shorter events, 0.0 us)
Async XLA Ops:
  0.6 0.7 copy-start.4
  1.3 0.7 copy-start.5
  5.9 64.3 %copy-start = (bf16[10128,128]{1,0:T(8,128)(2,1)}, bf16[10128,128]{1,0:T(8,128)(2,1)S(1)}, u32[]{:S(2)}) copy-start(bf16[10128,128]{1,0:T(8,128)(2,1)S(1)} %get-tuple-element.8.right_ref.right_own_ref) | copy-start | bytes 7778308
  6.0 60.0 %collective-permute-start = (bf16[10128,128]{1,0:T(8,128)(2,1)S(1)}, bf16[10128,128]{1,0:T(8,128)(2,1)S(1)}, u32[]{:S(2)}, u32[]{:S(2)}) collective-permute-start(bf16[10128,128]{1,0:T(8,128)(2,1)S(1)} %get-tuple-element.7.left_ref.left_own_ref), channel_id=1, source_target_pairs={{0,115},{1,112},{2,117},{3,118},{4,119},{5,116},{6,121},{7,122},{8... | collective-permute-start | bytes 7778312 | tf_op jit(solution)/shard_map/ppermute | solution.py:76
  10.8 70.2 %copy-start.6 = (s32[4,2,2]{0,2,1:T(2,128)S(1)}, s32[4,2,2]{0,2,1:T(2,128)}, u32[]{:S(2)}) copy-start(s32[4,2,2]{0,2,1:T(2,128)} %param.12) | copy-start | bytes 196
  10.8 70.9 %copy-start.3 = (bf16[256,256]{1,0:T(8,128)(2,1)S(1)}, bf16[256,256]{1,0:T(8,128)(2,1)}, u32[]{:S(2)}) copy-start(bf16[256,256]{1,0:T(8,128)(2,1)} %before_ref.1) | copy-start | bytes 393220
  10.8 56.6 %collective-permute-start.1 = (bf16[10128,128]{1,0:T(8,128)(2,1)S(1)}, bf16[10128,128]{1,0:T(8,128)(2,1)S(1)}, u32[]{:S(2)}, u32[]{:S(2)}) collective-permute-start(bf16[10128,128]{1,0:T(8,128)(2,1)S(1)} %get-tuple-element.8.right_ref.right_own_ref), channel_id=1, source_target_pairs={{0,17},{1,18},{2,19},{3,16},{4,21},{5,22},{6,23},{7,20},{8,25},{9,... | collective-permute-start | bytes 7778312 | tf_op jit(solution)/shard_map/ppermute | solution.py:76
  10.8 56.6 %collective-permute-start.2 = (bf16[10128,128]{1,0:T(8,128)(2,1)S(1)}, bf16[10128,128]{1,0:T(8,128)(2,1)S(1)}, u32[]{:S(2)}, u32[]{:S(2)}) collective-permute-start(bf16[10128,128]{1,0:T(8,128)(2,1)S(1)} %get-tuple-element.7.left_ref.left_own_ref), channel_id=1, source_target_pairs={{16,112},{17,117},{18,118},{19,119},{20,116},{21,121},{22,122},{23... | collective-permute-start | bytes 7778312 | tf_op jit(solution)/shard_map/ppermute | solution.py:76
  11.7 55.7 %collective-permute-start.3 = (bf16[10128,128]{1,0:T(8,128)(2,1)S(1)}, bf16[10128,128]{1,0:T(8,128)(2,1)S(1)}, u32[]{:S(2)}, u32[]{:S(2)}) collective-permute-start(bf16[10128,128]{1,0:T(8,128)(2,1)S(1)} %get-tuple-element.8.right_ref.right_own_ref), channel_id=1, source_target_pairs={{16,60},{17,49},{18,50},{19,51},{20,48},{21,53},{22,54},{23,55},{2... | collective-permute-start | bytes 7778312 | tf_op jit(solution)/shard_map/ppermute | solution.py:76
  70.2 15.6 %collective-permute-start.4 = (bf16[256,256]{1,0:T(8,128)(2,1)S(1)}, bf16[256,256]{1,0:T(8,128)(2,1)S(1)}, u32[]{:S(2)}, u32[]{:S(2)}) collective-permute-start(bf16[256,256]{1,0:T(8,128)(2,1)S(1)} %get-tuple-element.9), channel_id=1, source_target_pairs={{0,17},{1,18},{2,19},{3,20},{4,21},{5,22},{6,23},{7,24},{8,25},{9,... | collective-permute-start | bytes 393224 | tf_op jit(solution)/shard_map/ppermute | solution.py:76
  78.4 11.8 %collective-permute-start.5 = (bf16[256,256]{1,0:T(8,128)(2,1)S(1)}, bf16[256,256]{1,0:T(8,128)(2,1)S(1)}, u32[]{:S(2)}, u32[]{:S(2)}) collective-permute-start(bf16[256,256]{1,0:T(8,128)(2,1)S(1)} %get-tuple-element.10), channel_id=1, source_target_pairs={{0,1},{1,2},{2,3},{3,4},{4,5},{5,6},{6,7},{7,8},{8,9},{9,10},{10,1... | collective-permute-start | bytes 393224 | tf_op jit(solution)/shard_map/ppermute | solution.py:76
  79.6 10.7 %collective-permute-start.6 = (bf16[256,256]{1,0:T(8,128)(2,1)S(1)}, bf16[256,256]{1,0:T(8,128)(2,1)S(1)}, u32[]{:S(2)}, u32[]{:S(2)}) collective-permute-start(bf16[256,256]{1,0:T(8,128)(2,1)S(1)} %get-tuple-element.11), channel_id=1, source_target_pairs={{0,16},{1,17},{2,18},{3,19},{4,20},{5,21},{6,22},{7,23},{8,24},{9,... | collective-permute-start | bytes 393224 | tf_op jit(solution)/shard_map/ppermute | solution.py:76
  81.7 1.7 %copy-start.1 = (bf16[10128,128]{1,0:T(8,128)(2,1)S(1)}, bf16[10128,128]{1,0:T(8,128)(2,1)}, u32[]{:S(2)}) copy-start(bf16[10128,128]{1,0:T(8,128)(2,1)} %copy-done) | copy-start | bytes 7778308
  83.4 6.9 %copy-start.2 = (f32[256,256]{1,0:T(8,128)S(1)}, f32[256,256]{1,0:T(8,128)}, u32[]{:S(2)}) copy-start(f32[256,256]{1,0:T(8,128)} %density_ref.1) | copy-start | bytes 786436

commit v4 on v3

--- a/solution.py
+++ b/solution.py
@@ -17,7 +17,7 @@
 AXES = ("row", "col")
 GROUP = 16
 LANES = 128
-KERNEL_VMEM = 8 * 1024 * 1024
+KERNEL_VMEM = 4 * 1024 * 1024
 STORED = MAXB * BS
 TABLE_AT = STORED + BS
 TABLE = 16
@@ -76,73 +76,55 @@
     return lax.ppermute(value, AXES, pairs)
 
 
-def gather_blocks_kernel(
-    left_ids_ref, right_ids_ref, left_ref, right_ref, left_out, right_out, left_ids, right_ids, id_sems, sems
-):
-    id_copies = [
-        pltpu.make_async_copy(source, target, id_sems.at[n])
-        for n, (source, target) in enumerate(
-            ((left_ids_ref, left_ids), (right_ids_ref, right_ids))
-        )
-    ]
-    for copy in id_copies:
-        copy.start()
+def gather_blocks_kernel(across, ids_ref, panel_ref, out_ref, ids, id_sem, sem):
+    id_copy = pltpu.make_async_copy(ids_ref, ids, id_sem)
+    id_copy.start()
     row = lax.broadcasted_iota(jnp.int32, (8, LANES), 0)
     lane = lax.broadcasted_iota(jnp.int32, (8, LANES), 1)
-    sides = ((left_ids, left_ref, left_out, KB), (right_ids, right_ref, right_out, WB))
-    tables = []
-    for side, (ids, panel_ref, out_ref, across) in enumerate(sides):
-        id_copies[side].wait()
-
-        def start(n, table):
-            place = ids[0, 0, n]
-            r, k = place // across, place % across
-            read = jnp.where(place < WB * KB, place, n)
-            pltpu.make_async_copy(
-                panel_ref.at[
-                    pl.ds(pl.multiple_of(read // across * BS, BS), BS),
-                    pl.ds(pl.multiple_of(read % across * BS, BS), BS),
-                ],
-                out_ref.at[pl.ds(pl.multiple_of(n * BS, BS), BS), :],
-                sems.at[side],
-            ).start()
-            outer, inner = (r, k) if across == KB else (k, r)
-            return jnp.where((row == outer) & (lane == inner), n, table)
-
-        tables.append(
-            lax.fori_loop(0, MAXB, start, jnp.full((8, LANES), MAXB, jnp.int32), unroll=13)
-        )
-    for (_, _, out_ref, _), table in zip(sides, tables):
-        out_ref[pl.ds(STORED, BS), :] = jnp.zeros((BS, BS), out_ref.dtype)
-        both = jnp.concatenate([table, table], axis=0).astype(jnp.float32)
-        out_ref[pl.ds(TABLE_AT, TABLE), :] = both.astype(out_ref.dtype)
-    for side, (_, _, out_ref, _) in enumerate(sides):
-        blocks = out_ref.at[pl.ds(0, STORED), :]
-        pltpu.make_async_copy(blocks, blocks, sems.at[side]).wait()
-
-
-def gather_blocks(left, right, left_ids, right_ids):
+    out_ref[pl.ds(STORED, BS), :] = jnp.zeros((BS, BS), out_ref.dtype)
+    id_copy.wait()
+
+    def start(n, table):
+        place = ids[0, 0, n]
+        r, k = place // across, place % across
+        read = jnp.where(place < WB * KB, place, n)
+        pltpu.make_async_copy(
+            panel_ref.at[
+                pl.ds(pl.multiple_of(read // across * BS, BS), BS),
+                pl.ds(pl.multiple_of(read % across * BS, BS), BS),
+            ],
+            out_ref.at[pl.ds(pl.multiple_of(n * BS, BS), BS), :],
+            sem,
+        ).start()
+        outer, inner = (r, k) if across == KB else (k, r)
+        return jnp.where((row == outer) & (lane == inner), n, table)
+
+    table = lax.fori_loop(0, MAXB, start, jnp.full((8, LANES), MAXB, jnp.int32), unroll=13)
+    both = jnp.concatenate([table, table], axis=0).astype(jnp.float32)
+    out_ref[pl.ds(TABLE_AT, TABLE), :] = both.astype(out_ref.dtype)
+    blocks = out_ref.at[pl.ds(0, STORED), :]
+    pltpu.make_async_copy(blocks, blocks, sem).wait()
+
+
+def gather_blocks(panel, ids, across):
     any_space = pl.BlockSpec(memory_space=pl.ANY)
     return pl.pallas_call(
-        gather_blocks_kernel,
-        out_shape=[pltpu.VMEM((PACKED, BS), left.dtype)] * 2,
-        in_specs=[any_space] * 4,
-        out_specs=[pl.BlockSpec(memory_space=pltpu.VMEM)] * 2,
+        functools.partial(gather_blocks_kernel, across),
+        out_shape=pltpu.VMEM((PACKED, BS), panel.dtype),
+        in_specs=[any_space] * 2,
+        out_specs=pl.BlockSpec(memory_space=pltpu.VMEM),
         scratch_shapes=[
-            pltpu.SMEM(left_ids.shape, jnp.int32),
-            pltpu.SMEM(right_ids.shape, jnp.int32),
-            pltpu.SemaphoreType.DMA((2,)),
-            pltpu.SemaphoreType.DMA((2,)),
+            pltpu.SMEM(ids.shape, jnp.int32),
+            pltpu.SemaphoreType.DMA,
+            pltpu.SemaphoreType.DMA,
         ],
         compiler_params=pltpu.CompilerParams(vmem_limit_bytes=KERNEL_VMEM),
         cost_estimate=pl.CostEstimate(
-            flops=0, bytes_accessed=4 * PACKED * BS * 2, transcendentals=0
+            flops=0, bytes_accessed=2 * PACKED * BS * 2, transcendentals=0
         ),
     )(
-        left_ids,
-        right_ids,
-        pltpu.with_memory_space_constraint(left, pltpu.HBM),
-        pltpu.with_memory_space_constraint(right, pltpu.HBM),
+        pltpu.with_memory_space_constraint(ids, pltpu.HBM),
+        pltpu.with_memory_space_constraint(panel, pltpu.HBM),
     )
 
 
@@ -214,10 +196,11 @@
     return jnp.concatenate(rows, axis=0)
 
 
-def base_kernel(filter_ref, left_ref, right_ref, before_ref, out_ref, product, held, words, chosen, sem):
-    to_scalars([slot_words(table_in(left_ref), table_in(right_ref))], held, words, sem)
-    multiply(left_ref, right_ref, words.at[0], chosen, product)
-    out_ref[...] = 2.0 * masked(filter_ref, 0, product[...]) - before_ref[...].astype(jnp.float32)
+def base_kernel(filter_ref, own_ref, one_ref, before_ref, out_ref):
+    odd = lax.axis_index("row") % 2
+    one = masked(filter_ref, 3 - 2 * odd, one_ref[...].astype(jnp.float32))
+    total = masked(filter_ref, 0, own_ref[...]) + one
+    out_ref[...] = 2.0 * total - before_ref[...].astype(jnp.float32)
 
 
 def send_product(left_ref, right_ref, words, chosen, product, out_ref):
@@ -225,15 +208,16 @@
     out_ref[...] = product[...].astype(out_ref.dtype)
 
 
-def products_kernel(
+def own_kernel(left_near_ref, left_ref, right_ref, own_ref, held, words, chosen, sem):
+    to_scalars([slot_words(table_in(left_ref), table_in(right_ref))], held, words, sem)
+    multiply(left_ref, right_ref, words.at[0], chosen, own_ref)
+
+
+def early_kernel(
+    own_ref,
     left_near_ref,
-    right_near_ref,
-    left_far_ref,
     right_far_ref,
-    left_own_ref,
     right_own_ref,
-    two_ref,
-    three_ref,
     one_ref,
     product,
     held,
@@ -242,15 +226,37 @@
     sem,
 ):
     odd = lax.axis_index("row") % 2 == 1
-    left_near, right_near = table_in(left_near_ref), table_in(right_near_ref)
+    right_other = jnp.where(odd, table_in(right_far_ref), table_in(right_own_ref))
+    to_scalars([slot_words(table_in(left_near_ref), right_other)], held, words, sem)
+
+    @pl.when(odd)
+    def _():
+        send_product(left_near_ref, right_far_ref, words.at[0], chosen, product, one_ref)
+
+    @pl.when(jnp.logical_not(odd))
+    def _():
+        send_product(left_near_ref, right_own_ref, words.at[0], chosen, product, one_ref)
+
+
+def late_kernel(
+    one_ref,
+    left_near_ref,
+    right_near_ref,
+    left_far_ref,
+    left_own_ref,
+    two_ref,
+    three_ref,
+    product,
+    held,
+    words,
+    chosen,
+    sem,
+):
+    odd = lax.axis_index("row") % 2 == 1
+    right_near = table_in(right_near_ref)
     left_other = jnp.where(odd, table_in(left_far_ref), table_in(left_own_ref))
-    right_other = jnp.where(odd, table_in(right_far_ref), table_in(right_own_ref))
     to_scalars(
-        [
-            slot_words(left_near, right_near),
-            slot_words(left_other, right_near),
-            slot_words(left_near, right_other),
-        ],
+        [slot_words(table_in(left_near_ref), right_near), slot_words(left_other, right_near)],
         held,
         words,
         sem,
@@ -260,32 +266,30 @@
     @pl.when(odd)
     def _():
         send_product(left_far_ref, right_near_ref, words.at[1], chosen, product, three_ref)
-        send_product(left_near_ref, right_far_ref, words.at[2], chosen, product, one_ref)
 
     @pl.when(jnp.logical_not(odd))
     def _():
         send_product(left_own_ref, right_near_ref, words.at[1], chosen, product, three_ref)
-        send_product(left_near_ref, right_own_ref, words.at[2], chosen, product, one_ref)
 
 
 def final_kernel(
-    filter_ref, coefficient_ref, base_ref, two_ref, three_ref, one_ref, density_ref, term_out, density_out
+    filter_ref, coefficient_ref, base_ref, two_ref, three_ref, density_ref, term_out, density_out
 ):
     odd = lax.axis_index("row") % 2
-    total = (
-        masked(filter_ref, 2, two_ref[...].astype(jnp.float32))
-        + masked(filter_ref, 1 + 2 * odd, three_ref[...].astype(jnp.float32))
-        + masked(filter_ref, 3 - 2 * odd, one_ref[...].astype(jnp.float32))
-    )
+    two = masked(filter_ref, 2, two_ref[...].astype(jnp.float32))
+    three = masked(filter_ref, 1 + 2 * odd, three_ref[...].astype(jnp.float32))
+    total = two + three
     term_next = (2.0 * total + base_ref[...]).astype(jnp.bfloat16)
     term_out[...] = term_next
     density_out[...] = density_ref[...] + coefficient_ref[0] * term_next.astype(jnp.float32)
 
 
+ANYWHERE = pl.BlockSpec(memory_space=pl.ANY)
 IN_VMEM = pl.BlockSpec(memory_space=pltpu.VMEM)
 IN_SMEM = pl.BlockSpec(memory_space=pltpu.SMEM)
 PANEL = (WB * BS, WB * BS)
 RESULT = jax.ShapeDtypeStruct(PANEL, jnp.float32)
+SENT = jax.ShapeDtypeStruct(PANEL, jnp.bfloat16)
 LISTS = [
     pltpu.VMEM((8, LANES), jnp.int32),
     pltpu.SMEM((8, LANES), jnp.int32),
@@ -320,8 +324,9 @@
     density_in,
     coefficient,
 ):
-    left_own, right_own = gather_blocks(hamiltonian, term_now, hamiltonian_ids, term_ids)
+    left_own = gather_blocks(hamiltonian, hamiltonian_ids, KB)
     left_n = move(left_own, left_near)
+    right_own = gather_blocks(term_now, term_ids, WB)
     right_f = move(right_own, right_far)
     right_n = move(right_own, right_near)
     left_f = move(left_own, left_far)
@@ -329,29 +334,49 @@
     def in_vmem(panel):
         return pltpu.with_memory_space_constraint(panel, pltpu.VMEM)
 
-    two, three, one = run_kernel(
-        products_kernel,
-        [IN_VMEM] * 6,
-        [jax.ShapeDtypeStruct(PANEL, jnp.bfloat16)] * 3,
+    (own,) = run_kernel(
+        own_kernel,
+        [ANYWHERE] + [IN_VMEM] * 2,
+        [RESULT],
+        LISTS,
+        1,
+        left_n,
+        in_vmem(left_own),
+        in_vmem(right_own),
+    )
+    (one,) = run_kernel(
+        early_kernel,
+        [ANYWHERE] + [IN_VMEM] * 3,
+        [SENT],
         [pltpu.VMEM(PANEL, jnp.float32)] + LISTS,
-        3,
-        *[in_vmem(panel) for panel in (left_n, right_n, left_f, right_f, left_own, right_own)],
+        1,
+        own,
+        *[in_vmem(panel) for panel in (left_n, right_f, right_own)],
+    )
+    two, three = run_kernel(
+        late_kernel,
+        [ANYWHERE] + [IN_VMEM] * 4,
+        [SENT] * 2,
+        [pltpu.VMEM(PANEL, jnp.float32)] + LISTS,
+        2,
+        one,
+        *[in_vmem(panel) for panel in (left_n, right_n, left_f, left_own)],
     )
     two, three, one = move(two, home_two), move(three, home_three), move(one, home_one)
     (base,) = run_kernel(
         base_kernel,
         [IN_SMEM] + [IN_VMEM] * 3,
         [RESULT],
-        [pltpu.VMEM(PANEL, jnp.float32)] + LISTS,
-        1,
+        [],
+        0,
         product_filter,
-        in_vmem(left_own),
-        in_vmem(right_own),
+        own,
+        one,
         term_before,
     )
     term_next, density_out = run_kernel(
         final_kernel,
-        [IN_SMEM] * 2 + [IN_VMEM] * 5,
+        [IN_SMEM] * 2 + [IN_VMEM] * 4,
         [
             jax.ShapeDtypeStruct(term_before.shape, jnp.bfloat16),
             jax.ShapeDtypeStruct(density_in.shape, jnp.float32),
@@ -363,7 +388,6 @@
         base,
         two,
         three,
-        one,
         density_in,
     )
     return (term_next, density_out)

time: 91.9 us -> 86.6 us (0.942)
  waiting for transfers between devices: 59.3 us -> 52.7 us
  local copies, waits for them, and re-layouts: 3.14 us -> 0.12 us
  Pallas kernels: 10.6 us -> 12.9 us
  starting transfers between devices: 17.3 us -> 19.1 us
    ppermute x7, waiting for transfers between devices: 59.3 us -> 52.7 us  [move(): return lax.ppermute(value, AXES, pairs)]
    unnamed x15 -> x7, local copies, waits for them, and re-layouts: 3.14 us -> 0.12 us
    ppermute x7, starting transfers between devices: 17.3 us -> 19.1 us  [move(): return lax.ppermute(value, AXES, pairs)]
    pallas_call x1 -> x2, Pallas kernels: 3.99 us -> 5.62 us  [gather_blocks(): pl.pallas_call(functools.partial(gather_blocks_kernel, across), out_shape...]
    pallas_call x3 -> x5, Pallas kernels: 6.65 us -> 7.31 us  [run_kernel(): pl.pallas_call(kernel, out_shape=out_shape, in_specs=in_specs, out_specs=...]
  transfers between devices with their start and end apart: 7 -> 7, of which waited for: 3 -> 4; matrix products, arithmetic and copies ran while one was open for 0% -> 0% of each run, Pallas kernels for 3% -> 10%
where the time goes in v4:
time: 86.6 us; the launch traced here: 86.3 us
  waiting for transfers between devices  52.7 us (61%)
  starting transfers between devices  19.1 us (22%)
  Pallas kernels  12.9 us (15%)
  between operations  1.38 us (2%)
    ppermute x7, waiting for transfers between devices, move(): return lax.ppermute(value, AXES, pairs)  52.7 us
    ppermute x7, starting transfers between devices, move(): return lax.ppermute(value, AXES, pairs)  19.1 us
    pallas_call x5, Pallas kernels, run_kernel(): pl.pallas_call(kernel, out_shape=out_shape, in_specs=in_specs, out_specs=...  7.31 us
    pallas_call x2, Pallas kernels, gather_blocks(): pl.pallas_call(functools.partial(gather_blocks_kernel, across), out_shape...  5.62 us
  transfers between devices with their start and end apart: 7, of which 4 were waited for; matrix products, arithmetic and copies ran while one was open for 0% of the time, Pallas kernels for 10%

profile of v4, /device:TPU:0, one launch (start us, length us, event | category | flops | bytes accessed | tf_op | source)
XLA Modules:
  0.0 86.3 jit_solution(16942927212270743902)
XLA Ops:
  0.6 2.8 %shard_map.95.left_ref.left_own_ref = bf16[10128,128]{1,0:T(8,128)(2,1)S(1)} custom-call(s32[1,1,78]{2,1,0:T(1,128)} %ids_ref.2, bf16[256,12544]{1,0:T(8,128)(2,1)} %panel_ref.2), custom_call_target="tpu_custom_call" | custom-call | bytes 5185536 | tf_op jit(solution)/shard_map/pallas_call | solution.py:111
  3.5 4.8 %collective-permute-start = (bf16[10128,128]{1,0:T(8,128)(2,1)S(1)}, bf16[10128,128]{1,0:T(8,128)(2,1)S(1)}, u32[]{:S(2)}, u32[]{:S(2)}) collective-permute-start(bf16[10128,128]{1,0:T(8,128)(2,1)S(1)} %shard_map.95.left_ref.left_own_ref), channel_id=1, source_target_pairs={{0,115},{1,112},{2,117},{3,118},{4,119},{5,116},{6,121},{7,122},{8... | collective-permute-start | bytes 7778312 | tf_op jit(solution)/shard_map/ppermute | solution.py:76
  8.3 2.8 %shard_map.96.right_ref.right_own_ref = bf16[10128,128]{1,0:T(8,128)(2,1)S(1)} custom-call(s32[1,1,78]{2,1,0:T(1,128)} %ids_ref.3, bf16[12544,256]{1,0:T(8,128)(2,1)} %panel_ref.3), custom_call_target="tpu_custom_call" | custom-call | bytes 5185536 | tf_op jit(solution)/shard_map/pallas_call | solution.py:111
  11.1 0.8 collective-permute-start.1
  11.9 0.5 collective-permute-start.3
  12.4 0.8 collective-permute-start.4
  13.2 45.8 %collective-permute-done.left_near_ref = bf16[10128,128]{1,0:T(8,128)(2,1)S(1)} collective-permute-done((bf16[10128,128]{1,0:T(8,128)(2,1)S(1)}, bf16[10128,128]{1,0:T(8,128)(2,1)S(1)}, u32[]{:S(2)}, u32[]{:S(2)}) %collective-permute-start) | collective-permute-done | bytes 2592800 | tf_op jit(solution)/shard_map/ppermute | solution.py:76
  59.0 1.3 %shard_map.97.own_ref = f32[256,256]{1,0:T(8,128)S(1)} custom-call(bf16[10128,128]{1,0:T(8,128)(2,1)S(1)} %collective-permute-done.left_near_ref, bf16[10128,128]{1,0:T(8,128)(2,1)S(1)} %shard_map.95.left_ref.left_own_ref, bf16[10128,128]{1,0:T(8,128)(2,1)S(1)} %shard_map.96.right_ref.right_own_ref), custom_call_target="tpu_custom_call" | custom-call | flops 671088640 | bytes 262144 | tf_op jit(solution)/shard_map/pallas_call | solution.py:302
  60.4 0.0 collective-permute-done.1.right_far_ref
  60.4 1.4 %shard_map.98.one_ref = bf16[256,256]{1,0:T(8,128)(2,1)S(1)} custom-call(f32[256,256]{1,0:T(8,128)S(1)} %shard_map.97.own_ref, bf16[10128,128]{1,0:T(8,128)(2,1)S(1)} %collective-permute-done.left_near_ref, bf16[10128,128]{1,0:T(8,128)(2,1)S(1)} %collective-permute-done.1.right_far_ref, bf16[10128,128]{1,0:T(8,128)(2,1)S(1)} %shard_map.96.right_ref.right_own_ref), custom_call_target="tpu_custom_call" | custom-call | flops 671088640 | bytes 262144 | tf_op jit(solution)/shard_map/pallas_call | solution.py:302
  61.8 0.0 copy-start.2
  61.8 0.0 copy-start.1
  61.8 0.0 copy-start
  61.8 10.7 %collective-permute-start.2 = (bf16[256,256]{1,0:T(8,128)(2,1)S(1)}, bf16[256,256]{1,0:T(8,128)(2,1)S(1)}, u32[]{:S(2)}, u32[]{:S(2)}) collective-permute-start(bf16[256,256]{1,0:T(8,128)(2,1)S(1)} %shard_map.98.one_ref), channel_id=1, source_target_pairs={{0,16},{1,17},{2,18},{3,19},{4,20},{5,21},{6,22},{7,23},{8,24},{9,... | collective-permute-start | bytes 393224 | tf_op jit(solution)/shard_map/ppermute | solution.py:76
  72.5 0.0 collective-permute-done.3.right_near_ref
  72.5 2.5 %shard_map.100 = (bf16[256,256]{1,0:T(8,128)(2,1)S(1)}, bf16[256,256]{1,0:T(8,128)(2,1)S(1)}) custom-call(bf16[256,256]{1,0:T(8,128)(2,1)S(1)} %shard_map.98.one_ref, bf16[10128,128]{1,0:T(8,128)(2,1)S(1)} %collective-permute-done.left_near_ref, bf16[10128,128]{1,0:T(8,128)(2,1)S(1)} %collective-permute-done.3.right_near_ref, ...), custom_call_target="tpu_custom_call" | custom-call | flops 1342177280 | bytes 524288 | tf_op jit(solution)/shard_map/pallas_call | solution.py:302
  75.0 0.3 collective-permute-start.5
  75.3 1.2 %collective-permute-start.6 = (bf16[256,256]{1,0:T(8,128)(2,1)S(1)}, bf16[256,256]{1,0:T(8,128)(2,1)S(1)}, u32[]{:S(2)}, u32[]{:S(2)}) collective-permute-start(bf16[256,256]{1,0:T(8,128)(2,1)S(1)} %get-tuple-element.5), channel_id=1, source_target_pairs={{0,1},{1,2},{2,3},{3,4},{4,5},{5,6},{6,7},{7,8},{8,9},{9,10},{10,1... | collective-permute-start | bytes 393224 | tf_op jit(solution)/shard_map/ppermute | solution.py:76
  76.5 0.1 copy.11.filter_ref
  77.2 2.3 %collective-permute-done.2.one_ref = bf16[256,256]{1,0:T(8,128)(2,1)S(1)} collective-permute-done((bf16[256,256]{1,0:T(8,128)(2,1)S(1)}, bf16[256,256]{1,0:T(8,128)(2,1)S(1)}, u32[]{:S(2)}, u32[]{:S(2)}) %collective-permute-start.2) | collective-permute-done | bytes 131104 | tf_op jit(solution)/shard_map/ppermute | solution.py:76
  79.5 0.7 shard_map.99.base_ref
  80.2 1.4 %collective-permute-done.5.two_ref = bf16[256,256]{1,0:T(8,128)(2,1)S(1)} collective-permute-done((bf16[256,256]{1,0:T(8,128)(2,1)S(1)}, bf16[256,256]{1,0:T(8,128)(2,1)S(1)}, u32[]{:S(2)}, u32[]{:S(2)}) %collective-permute-start.5) | collective-permute-done | bytes 131104 | tf_op jit(solution)/shard_map/ppermute | solution.py:76
  81.6 3.3 %collective-permute-done.6.three_ref = bf16[256,256]{1,0:T(8,128)(2,1)S(1)} collective-permute-done((bf16[256,256]{1,0:T(8,128)(2,1)S(1)}, bf16[256,256]{1,0:T(8,128)(2,1)S(1)}, u32[]{:S(2)}, u32[]{:S(2)}) %collective-permute-start.6) | collective-permute-done | bytes 131104 | tf_op jit(solution)/shard_map/ppermute | solution.py:76
  84.8 1.4 %shard_map.101 = (bf16[256,256]{1,0:T(8,128)(2,1)}, f32[256,256]{1,0:T(8,128)}) custom-call(s32[4,2,2]{2,1,0:T(2,128)S(1)} %copy.11.filter_ref, f32[1]{0:T(128)S(6)} %copy.12.coefficient_ref, f32[256,256]{1,0:T(8,128)S(1)} %shard_map.99.base_ref, bf16[256,256]{1,0:T(8,128)(2,1)S(1)} %collective-permute-done.5.two_ref, ...), custom_call_target="tpu_custom_call" | custom-call | bytes 524288 | tf_op jit(solution)/shard_map/pallas_call | solution.py:302
  (4 shorter events, 0.0 us)
Async XLA Ops:
  3.5 55.6 %collective-permute-start = (bf16[10128,128]{1,0:T(8,128)(2,1)S(1)}, bf16[10128,128]{1,0:T(8,128)(2,1)S(1)}, u32[]{:S(2)}, u32[]{:S(2)}) collective-permute-start(bf16[10128,128]{1,0:T(8,128)(2,1)S(1)} %shard_map.95.left_ref.left_own_ref), channel_id=1, source_target_pairs={{0,115},{1,112},{2,117},{3,118},{4,119},{5,116},{6,121},{7,122},{8... | collective-permute-start | bytes 7778312 | tf_op jit(solution)/shard_map/ppermute | solution.py:76
  11.1 49.3 %collective-permute-start.1 = (bf16[10128,128]{1,0:T(8,128)(2,1)S(1)}, bf16[10128,128]{1,0:T(8,128)(2,1)S(1)}, u32[]{:S(2)}, u32[]{:S(2)}) collective-permute-start(bf16[10128,128]{1,0:T(8,128)(2,1)S(1)} %shard_map.96.right_ref.right_own_ref), channel_id=1, source_target_pairs={{16,60},{17,49},{18,50},{19,51},{20,48},{21,53},{22,54},{23,55},{2... | collective-permute-start | bytes 7778312 | tf_op jit(solution)/shard_map/ppermute | solution.py:76
  11.9 60.6 %collective-permute-start.3 = (bf16[10128,128]{1,0:T(8,128)(2,1)S(1)}, bf16[10128,128]{1,0:T(8,128)(2,1)S(1)}, u32[]{:S(2)}, u32[]{:S(2)}) collective-permute-start(bf16[10128,128]{1,0:T(8,128)(2,1)S(1)} %shard_map.96.right_ref.right_own_ref), channel_id=1, source_target_pairs={{0,17},{1,18},{2,19},{3,16},{4,21},{5,22},{6,23},{7,20},{8,25},{9,... | collective-permute-start | bytes 7778312 | tf_op jit(solution)/shard_map/ppermute | solution.py:76
  12.4 60.1 %collective-permute-start.4 = (bf16[10128,128]{1,0:T(8,128)(2,1)S(1)}, bf16[10128,128]{1,0:T(8,128)(2,1)S(1)}, u32[]{:S(2)}, u32[]{:S(2)}) collective-permute-start(bf16[10128,128]{1,0:T(8,128)(2,1)S(1)} %shard_map.95.left_ref.left_own_ref), channel_id=1, source_target_pairs={{16,112},{17,117},{18,118},{19,119},{20,116},{21,121},{22,122},{23... | collective-permute-start | bytes 7778312 | tf_op jit(solution)/shard_map/ppermute | solution.py:76
  61.8 14.7 %copy-start.2 = (s32[4,2,2]{0,2,1:T(2,128)S(1)}, s32[4,2,2]{0,2,1:T(2,128)}, u32[]{:S(2)}) copy-start(s32[4,2,2]{0,2,1:T(2,128)} %param.12) | copy-start | bytes 196
  61.8 17.7 %copy-start.1 = (bf16[256,256]{1,0:T(8,128)(2,1)S(1)}, bf16[256,256]{1,0:T(8,128)(2,1)}, u32[]{:S(2)}) copy-start(bf16[256,256]{1,0:T(8,128)(2,1)} %before_ref.1) | copy-start | bytes 393220
  61.8 23.0 %copy-start = (f32[256,256]{1,0:T(8,128)S(1)}, f32[256,256]{1,0:T(8,128)}, u32[]{:S(2)}) copy-start(f32[256,256]{1,0:T(8,128)} %density_ref.1) | copy-start | bytes 786436
  61.8 17.7 %collective-permute-start.2 = (bf16[256,256]{1,0:T(8,128)(2,1)S(1)}, bf16[256,256]{1,0:T(8,128)(2,1)S(1)}, u32[]{:S(2)}, u32[]{:S(2)}) collective-permute-start(bf16[256,256]{1,0:T(8,128)(2,1)S(1)} %shard_map.98.one_ref), channel_id=1, source_target_pairs={{0,16},{1,17},{2,18},{3,19},{4,20},{5,21},{6,22},{7,23},{8,24},{9,... | collective-permute-start | bytes 393224 | tf_op jit(solution)/shard_map/ppermute | solution.py:76
  75.0 6.6 %collective-permute-start.5 = (bf16[256,256]{1,0:T(8,128)(2,1)S(1)}, bf16[256,256]{1,0:T(8,128)(2,1)S(1)}, u32[]{:S(2)}, u32[]{:S(2)}) collective-permute-start(bf16[256,256]{1,0:T(8,128)(2,1)S(1)} %get-tuple-element.4), channel_id=1, source_target_pairs={{0,17},{1,18},{2,19},{3,20},{4,21},{5,22},{6,23},{7,24},{8,25},{9,... | collective-permute-start | bytes 393224 | tf_op jit(solution)/shard_map/ppermute | solution.py:76
  75.3 9.6 %collective-permute-start.6 = (bf16[256,256]{1,0:T(8,128)(2,1)S(1)}, bf16[256,256]{1,0:T(8,128)(2,1)S(1)}, u32[]{:S(2)}, u32[]{:S(2)}) collective-permute-start(bf16[256,256]{1,0:T(8,128)(2,1)S(1)} %get-tuple-element.5), channel_id=1, source_target_pairs={{0,1},{1,2},{2,3},{3,4},{4,5},{5,6},{6,7},{7,8},{8,9},{9,10},{10,1... | collective-permute-start | bytes 393224 | tf_op jit(solution)/shard_map/ppermute | solution.py:76

commit v5 on v4

--- a/solution.py
+++ b/solution.py
@@ -15,9 +15,9 @@
 N_ROW = 8
 N_COL = 16
 AXES = ("row", "col")
-GROUP = 16
+GROUP = 24
 LANES = 128
-KERNEL_VMEM = 4 * 1024 * 1024
+KERNEL_VMEM = 6 * 1024 * 1024
 STORED = MAXB * BS
 TABLE_AT = STORED + BS
 TABLE = 16
@@ -76,55 +76,73 @@
     return lax.ppermute(value, AXES, pairs)
 
 
-def gather_blocks_kernel(across, ids_ref, panel_ref, out_ref, ids, id_sem, sem):
-    id_copy = pltpu.make_async_copy(ids_ref, ids, id_sem)
-    id_copy.start()
+def gather_blocks_kernel(
+    left_ids_ref, right_ids_ref, left_ref, right_ref, left_out, right_out, left_ids, right_ids, id_sems, sems
+):
+    id_copies = [
+        pltpu.make_async_copy(source, target, id_sems.at[n])
+        for n, (source, target) in enumerate(
+            ((left_ids_ref, left_ids), (right_ids_ref, right_ids))
+        )
+    ]
+    for copy in id_copies:
+        copy.start()
     row = lax.broadcasted_iota(jnp.int32, (8, LANES), 0)
     lane = lax.broadcasted_iota(jnp.int32, (8, LANES), 1)
-    out_ref[pl.ds(STORED, BS), :] = jnp.zeros((BS, BS), out_ref.dtype)
-    id_copy.wait()
-
-    def start(n, table):
-        place = ids[0, 0, n]
-        r, k = place // across, place % across
-        read = jnp.where(place < WB * KB, place, n)
-        pltpu.make_async_copy(
-            panel_ref.at[
-                pl.ds(pl.multiple_of(read // across * BS, BS), BS),
-                pl.ds(pl.multiple_of(read % across * BS, BS), BS),
-            ],
-            out_ref.at[pl.ds(pl.multiple_of(n * BS, BS), BS), :],
-            sem,
-        ).start()
-        outer, inner = (r, k) if across == KB else (k, r)
-        return jnp.where((row == outer) & (lane == inner), n, table)
-
-    table = lax.fori_loop(0, MAXB, start, jnp.full((8, LANES), MAXB, jnp.int32), unroll=13)
-    both = jnp.concatenate([table, table], axis=0).astype(jnp.float32)
-    out_ref[pl.ds(TABLE_AT, TABLE), :] = both.astype(out_ref.dtype)
-    blocks = out_ref.at[pl.ds(0, STORED), :]
-    pltpu.make_async_copy(blocks, blocks, sem).wait()
-
-
-def gather_blocks(panel, ids, across):
+    sides = ((left_ids, left_ref, left_out, KB), (right_ids, right_ref, right_out, WB))
+    tables = []
+    for side, (ids, panel_ref, out_ref, across) in enumerate(sides):
+        id_copies[side].wait()
+
+        def start(n, table):
+            place = ids[0, 0, n]
+            r, k = place // across, place % across
+            read = jnp.where(place < WB * KB, place, n)
+            pltpu.make_async_copy(
+                panel_ref.at[
+                    pl.ds(pl.multiple_of(read // across * BS, BS), BS),
+                    pl.ds(pl.multiple_of(read % across * BS, BS), BS),
+                ],
+                out_ref.at[pl.ds(pl.multiple_of(n * BS, BS), BS), :],
+                sems.at[side],
+            ).start()
+            outer, inner = (r, k) if across == KB else (k, r)
+            return jnp.where((row == outer) & (lane == inner), n, table)
+
+        tables.append(
+            lax.fori_loop(0, MAXB, start, jnp.full((8, LANES), MAXB, jnp.int32), unroll=13)
+        )
+    for (_, _, out_ref, _), table in zip(sides, tables):
+        out_ref[pl.ds(STORED, BS), :] = jnp.zeros((BS, BS), out_ref.dtype)
+        both = jnp.concatenate([table, table], axis=0).astype(jnp.float32)
+        out_ref[pl.ds(TABLE_AT, TABLE), :] = both.astype(out_ref.dtype)
+    for side, (_, _, out_ref, _) in enumerate(sides):
+        blocks = out_ref.at[pl.ds(0, STORED), :]
+        pltpu.make_async_copy(blocks, blocks, sems.at[side]).wait()
+
+
+def gather_blocks(left, right, left_ids, right_ids):
     any_space = pl.BlockSpec(memory_space=pl.ANY)
     return pl.pallas_call(
-        functools.partial(gather_blocks_kernel, across),
-        out_shape=pltpu.VMEM((PACKED, BS), panel.dtype),
-        in_specs=[any_space] * 2,
-        out_specs=pl.BlockSpec(memory_space=pltpu.VMEM),
+        gather_blocks_kernel,
+        out_shape=[pltpu.VMEM((PACKED, BS), left.dtype)] * 2,
+        in_specs=[any_space] * 4,
+        out_specs=[pl.BlockSpec(memory_space=pltpu.VMEM)] * 2,
         scratch_shapes=[
-            pltpu.SMEM(ids.shape, jnp.int32),
-            pltpu.SemaphoreType.DMA,
-            pltpu.SemaphoreType.DMA,
+            pltpu.SMEM(left_ids.shape, jnp.int32),
+            pltpu.SMEM(right_ids.shape, jnp.int32),
+            pltpu.SemaphoreType.DMA((2,)),
+            pltpu.SemaphoreType.DMA((2,)),
         ],
         compiler_params=pltpu.CompilerParams(vmem_limit_bytes=KERNEL_VMEM),
         cost_estimate=pl.CostEstimate(
-            flops=0, bytes_accessed=2 * PACKED * BS * 2, transcendentals=0
+            flops=0, bytes_accessed=4 * PACKED * BS * 2, transcendentals=0
         ),
     )(
-        pltpu.with_memory_space_constraint(ids, pltpu.HBM),
-        pltpu.with_memory_space_constraint(panel, pltpu.HBM),
+        pltpu.with_memory_space_constraint(left_ids, pltpu.HBM),
+        pltpu.with_memory_space_constraint(right_ids, pltpu.HBM),
+        pltpu.with_memory_space_constraint(left, pltpu.HBM),
+        pltpu.with_memory_space_constraint(right, pltpu.HBM),
     )
 
 
@@ -208,7 +226,7 @@
     out_ref[...] = product[...].astype(out_ref.dtype)
 
 
-def own_kernel(left_near_ref, left_ref, right_ref, own_ref, held, words, chosen, sem):
+def own_kernel(left_ref, right_ref, own_ref, held, words, chosen, sem):
     to_scalars([slot_words(table_in(left_ref), table_in(right_ref))], held, words, sem)
     multiply(left_ref, right_ref, words.at[0], chosen, own_ref)
 
@@ -324,9 +342,8 @@
     density_in,
     coefficient,
 ):
-    left_own = gather_blocks(hamiltonian, hamiltonian_ids, KB)
+    left_own, right_own = gather_blocks(hamiltonian, term_now, hamiltonian_ids, term_ids)
     left_n = move(left_own, left_near)
-    right_own = gather_blocks(term_now, term_ids, WB)
     right_f = move(right_own, right_far)
     right_n = move(right_own, right_near)
     left_f = move(left_own, left_far)
@@ -336,11 +353,10 @@
 
     (own,) = run_kernel(
         own_kernel,
-        [ANYWHERE] + [IN_VMEM] * 2,
+        [IN_VMEM] * 2,
         [RESULT],
         LISTS,
         1,
-        left_n,
         in_vmem(left_own),
         in_vmem(right_own),
     )

time: 86.6 us -> 85 us (0.982)
  starting transfers between devices: 19.1 us -> 13.8 us
  waiting for transfers between devices: 52.7 us -> 57 us
  Pallas kernels: 12.9 us -> 11.6 us
    ppermute x7, starting transfers between devices: 19.1 us -> 13.8 us  [move(): return lax.ppermute(value, AXES, pairs)]
    ppermute x7, waiting for transfers between devices: 52.7 us -> 57 us  [move(): return lax.ppermute(value, AXES, pairs)]
    pallas_call x2 -> x1, Pallas kernels: 5.62 us -> 4.12 us  [gather_blocks(): pl.pallas_call(gather_blocks_kernel, out_shape=[pltpu.VMEM((PACKED, BS),...]
  transfers between devices with their start and end apart: 7 -> 7, of which waited for: 4 -> 4; matrix products, arithmetic and copies ran while one was open for 0% -> 0% of each run, Pallas kernels for 10% -> 7%
where the time goes in v5:
time: 85 us; the launch traced here: 83.8 us
  waiting for transfers between devices  57 us (67%)
  starting transfers between devices  13.8 us (16%)
  Pallas kernels  11.6 us (14%)
  between operations  1.37 us (2%)
    ppermute x7, waiting for transfers between devices, move(): return lax.ppermute(value, AXES, pairs)  57 us
    ppermute x7, starting transfers between devices, move(): return lax.ppermute(value, AXES, pairs)  13.8 us
    pallas_call x5, Pallas kernels, run_kernel(): pl.pallas_call(kernel, out_shape=out_shape, in_specs=in_specs, out_specs=...  7.46 us
    pallas_call x1, Pallas kernels, gather_blocks(): pl.pallas_call(gather_blocks_kernel, out_shape=[pltpu.VMEM((PACKED, BS),...  4.12 us
  transfers between devices with their start and end apart: 7, of which 4 were waited for; matrix products, arithmetic and copies ran while one was open for 0% of the time, Pallas kernels for 7%

profile of v5, /device:TPU:0, one launch (start us, length us, event | category | flops | bytes accessed | tf_op | source)
XLA Modules:
  0.0 83.8 jit_solution(12930049021646955315)
XLA Ops:
  0.6 4.1 %shard_map.95 = (bf16[10128,128]{1,0:T(8,128)(2,1)S(1)}, bf16[10128,128]{1,0:T(8,128)(2,1)S(1)}) custom-call(s32[1,1,78]{2,1,0:T(1,128)} %left_ids_ref.1, s32[1,1,78]{2,1,0:T(1,128)} %right_ids_ref.1, bf16[256,12544]{1,0:T(8,128)(2,1)} %left_ref.1, bf16[12544,256]{1,0:T(8,128)(2,1)} %right_ref.1), custom_call_target="tpu_custom_call" | custom-call | bytes 10371072 | tf_op jit(solution)/shard_map/pallas_call | solution.py:126
  4.8 4.8 %collective-permute-start = (bf16[10128,128]{1,0:T(8,128)(2,1)S(1)}, bf16[10128,128]{1,0:T(8,128)(2,1)S(1)}, u32[]{:S(2)}, u32[]{:S(2)}) collective-permute-start(bf16[10128,128]{1,0:T(8,128)(2,1)S(1)} %get-tuple-element.6.left_ref.left_own_ref), channel_id=1, source_target_pairs={{0,115},{1,112},{2,117},{3,118},{4,119},{5,116},{6,121},{7,122},{8... | collective-permute-start | bytes 7778312 | tf_op jit(solution)/shard_map/ppermute | solution.py:76
  9.6 0.8 collective-permute-start.1
  10.4 0.5 collective-permute-start.3
  10.9 0.8 collective-permute-start.4
  11.7 1.5 %shard_map.96.own_ref = f32[256,256]{1,0:T(8,128)S(1)} custom-call(bf16[10128,128]{1,0:T(8,128)(2,1)S(1)} %get-tuple-element.6.left_ref.left_own_ref, bf16[10128,128]{1,0:T(8,128)(2,1)S(1)} %get-tuple-element.7.right_ref.right_own_ref), custom_call_target="tpu_custom_call" | custom-call | flops 671088640 | bytes 262144 | tf_op jit(solution)/shard_map/pallas_call | solution.py:320
  13.2 49.9 %collective-permute-done.left_near_ref = bf16[10128,128]{1,0:T(8,128)(2,1)S(1)} collective-permute-done((bf16[10128,128]{1,0:T(8,128)(2,1)S(1)}, bf16[10128,128]{1,0:T(8,128)(2,1)S(1)}, u32[]{:S(2)}, u32[]{:S(2)}) %collective-permute-start) | collective-permute-done | bytes 2592800 | tf_op jit(solution)/shard_map/ppermute | solution.py:76
  63.1 0.0 collective-permute-done.1.right_far_ref
  63.1 1.5 %shard_map.97.one_ref = bf16[256,256]{1,0:T(8,128)(2,1)S(1)} custom-call(f32[256,256]{1,0:T(8,128)S(1)} %shard_map.96.own_ref, bf16[10128,128]{1,0:T(8,128)(2,1)S(1)} %collective-permute-done.left_near_ref, bf16[10128,128]{1,0:T(8,128)(2,1)S(1)} %collective-permute-done.1.right_far_ref, bf16[10128,128]{1,0:T(8,128)(2,1)S(1)} %get-tuple-element.7.right_ref.right_own_ref), custom_call_target="tpu_custom_call" | custom-call | flops 671088640 | bytes 262144 | tf_op jit(solution)/shard_map/pallas_call | solution.py:320
  64.6 0.0 copy-start.2
  64.6 0.0 copy-start.1
  64.7 0.0 copy-start
  64.7 6.0 %collective-permute-start.2 = (bf16[256,256]{1,0:T(8,128)(2,1)S(1)}, bf16[256,256]{1,0:T(8,128)(2,1)S(1)}, u32[]{:S(2)}, u32[]{:S(2)}) collective-permute-start(bf16[256,256]{1,0:T(8,128)(2,1)S(1)} %shard_map.97.one_ref), channel_id=1, source_target_pairs={{0,16},{1,17},{2,18},{3,19},{4,20},{5,21},{6,22},{7,23},{8,24},{9,... | collective-permute-start | bytes 393224 | tf_op jit(solution)/shard_map/ppermute | solution.py:76
  70.6 0.0 collective-permute-done.3.right_near_ref
  70.6 0.0 collective-permute-done.4.left_far_ref
  70.6 2.4 %shard_map.99 = (bf16[256,256]{1,0:T(8,128)(2,1)S(1)}, bf16[256,256]{1,0:T(8,128)(2,1)S(1)}) custom-call(bf16[256,256]{1,0:T(8,128)(2,1)S(1)} %shard_map.97.one_ref, bf16[10128,128]{1,0:T(8,128)(2,1)S(1)} %collective-permute-done.left_near_ref, bf16[10128,128]{1,0:T(8,128)(2,1)S(1)} %collective-permute-done.3.right_near_ref, ...), custom_call_target="tpu_custom_call" | custom-call | flops 1342177280 | bytes 524288 | tf_op jit(solution)/shard_map/pallas_call | solution.py:320
  73.0 0.1 collective-permute-start.5
  73.1 0.8 collective-permute-start.6
  73.9 0.1 copy.11.filter_ref
  74.6 3.0 %collective-permute-done.2.one_ref = bf16[256,256]{1,0:T(8,128)(2,1)S(1)} collective-permute-done((bf16[256,256]{1,0:T(8,128)(2,1)S(1)}, bf16[256,256]{1,0:T(8,128)(2,1)S(1)}, u32[]{:S(2)}, u32[]{:S(2)}) %collective-permute-start.2) | collective-permute-done | bytes 131104 | tf_op jit(solution)/shard_map/ppermute | solution.py:76
  77.7 0.7 shard_map.98.base_ref
  78.4 1.2 %collective-permute-done.5.two_ref = bf16[256,256]{1,0:T(8,128)(2,1)S(1)} collective-permute-done((bf16[256,256]{1,0:T(8,128)(2,1)S(1)}, bf16[256,256]{1,0:T(8,128)(2,1)S(1)}, u32[]{:S(2)}, u32[]{:S(2)}) %collective-permute-start.5) | collective-permute-done | bytes 131104 | tf_op jit(solution)/shard_map/ppermute | solution.py:76
  79.6 2.8 %collective-permute-done.6.three_ref = bf16[256,256]{1,0:T(8,128)(2,1)S(1)} collective-permute-done((bf16[256,256]{1,0:T(8,128)(2,1)S(1)}, bf16[256,256]{1,0:T(8,128)(2,1)S(1)}, u32[]{:S(2)}, u32[]{:S(2)}) %collective-permute-start.6) | collective-permute-done | bytes 131104 | tf_op jit(solution)/shard_map/ppermute | solution.py:76
  82.4 1.4 %shard_map.100 = (bf16[256,256]{1,0:T(8,128)(2,1)}, f32[256,256]{1,0:T(8,128)}) custom-call(s32[4,2,2]{2,1,0:T(2,128)S(1)} %copy.11.filter_ref, f32[1]{0:T(128)S(6)} %copy.12.coefficient_ref, f32[256,256]{1,0:T(8,128)S(1)} %shard_map.98.base_ref, bf16[256,256]{1,0:T(8,128)(2,1)S(1)} %collective-permute-done.5.two_ref, ...), custom_call_target="tpu_custom_call" | custom-call | bytes 524288 | tf_op jit(solution)/shard_map/pallas_call | solution.py:320
  (3 shorter events, 0.0 us)
Async XLA Ops:
  4.8 58.4 %collective-permute-start = (bf16[10128,128]{1,0:T(8,128)(2,1)S(1)}, bf16[10128,128]{1,0:T(8,128)(2,1)S(1)}, u32[]{:S(2)}, u32[]{:S(2)}) collective-permute-start(bf16[10128,128]{1,0:T(8,128)(2,1)S(1)} %get-tuple-element.6.left_ref.left_own_ref), channel_id=1, source_target_pairs={{0,115},{1,112},{2,117},{3,118},{4,119},{5,116},{6,121},{7,122},{8... | collective-permute-start | bytes 7778312 | tf_op jit(solution)/shard_map/ppermute | solution.py:76
  9.6 53.6 %collective-permute-start.1 = (bf16[10128,128]{1,0:T(8,128)(2,1)S(1)}, bf16[10128,128]{1,0:T(8,128)(2,1)S(1)}, u32[]{:S(2)}, u32[]{:S(2)}) collective-permute-start(bf16[10128,128]{1,0:T(8,128)(2,1)S(1)} %get-tuple-element.7.right_ref.right_own_ref), channel_id=1, source_target_pairs={{16,60},{17,49},{18,50},{19,51},{20,48},{21,53},{22,54},{23,55},{2... | collective-permute-start | bytes 7778312 | tf_op jit(solution)/shard_map/ppermute | solution.py:76
  10.4 60.2 %collective-permute-start.3 = (bf16[10128,128]{1,0:T(8,128)(2,1)S(1)}, bf16[10128,128]{1,0:T(8,128)(2,1)S(1)}, u32[]{:S(2)}, u32[]{:S(2)}) collective-permute-start(bf16[10128,128]{1,0:T(8,128)(2,1)S(1)} %get-tuple-element.7.right_ref.right_own_ref), channel_id=1, source_target_pairs={{0,17},{1,18},{2,19},{3,16},{4,21},{5,22},{6,23},{7,20},{8,25},{9,... | collective-permute-start | bytes 7778312 | tf_op jit(solution)/shard_map/ppermute | solution.py:76
  10.9 59.8 %collective-permute-start.4 = (bf16[10128,128]{1,0:T(8,128)(2,1)S(1)}, bf16[10128,128]{1,0:T(8,128)(2,1)S(1)}, u32[]{:S(2)}, u32[]{:S(2)}) collective-permute-start(bf16[10128,128]{1,0:T(8,128)(2,1)S(1)} %get-tuple-element.6.left_ref.left_own_ref), channel_id=1, source_target_pairs={{16,112},{17,117},{18,118},{19,119},{20,116},{21,121},{22,122},{23... | collective-permute-start | bytes 7778312 | tf_op jit(solution)/shard_map/ppermute | solution.py:76
  64.6 9.3 %copy-start.2 = (s32[4,2,2]{0,2,1:T(2,128)S(1)}, s32[4,2,2]{0,2,1:T(2,128)}, u32[]{:S(2)}) copy-start(s32[4,2,2]{0,2,1:T(2,128)} %param.12) | copy-start | bytes 196
  64.6 13.0 %copy-start.1 = (bf16[256,256]{1,0:T(8,128)(2,1)S(1)}, bf16[256,256]{1,0:T(8,128)(2,1)}, u32[]{:S(2)}) copy-start(bf16[256,256]{1,0:T(8,128)(2,1)} %before_ref.1) | copy-start | bytes 393220
  64.7 17.8 %copy-start = (f32[256,256]{1,0:T(8,128)S(1)}, f32[256,256]{1,0:T(8,128)}, u32[]{:S(2)}) copy-start(f32[256,256]{1,0:T(8,128)} %density_ref.1) | copy-start | bytes 786436
  64.7 13.0 %collective-permute-start.2 = (bf16[256,256]{1,0:T(8,128)(2,1)S(1)}, bf16[256,256]{1,0:T(8,128)(2,1)S(1)}, u32[]{:S(2)}, u32[]{:S(2)}) collective-permute-start(bf16[256,256]{1,0:T(8,128)(2,1)S(1)} %shard_map.97.one_ref), channel_id=1, source_target_pairs={{0,16},{1,17},{2,18},{3,19},{4,20},{5,21},{6,22},{7,23},{8,24},{9,... | collective-permute-start | bytes 393224 | tf_op jit(solution)/shard_map/ppermute | solution.py:76
  73.0 6.6 %collective-permute-start.5 = (bf16[256,256]{1,0:T(8,128)(2,1)S(1)}, bf16[256,256]{1,0:T(8,128)(2,1)S(1)}, u32[]{:S(2)}, u32[]{:S(2)}) collective-permute-start(bf16[256,256]{1,0:T(8,128)(2,1)S(1)} %get-tuple-element.8), channel_id=1, source_target_pairs={{0,17},{1,18},{2,19},{3,20},{4,21},{5,22},{6,23},{7,24},{8,25},{9,... | collective-permute-start | bytes 393224 | tf_op jit(solution)/shard_map/ppermute | solution.py:76
  73.1 9.3 %collective-permute-start.6 = (bf16[256,256]{1,0:T(8,128)(2,1)S(1)}, bf16[256,256]{1,0:T(8,128)(2,1)S(1)}, u32[]{:S(2)}, u32[]{:S(2)}) collective-permute-start(bf16[256,256]{1,0:T(8,128)(2,1)S(1)} %get-tuple-element.9), channel_id=1, source_target_pairs={{0,1},{1,2},{2,3},{3,4},{4,5},{5,6},{6,7},{7,8},{8,9},{9,10},{10,1... | collective-permute-start | bytes 393224 | tf_op jit(solution)/shard_map/ppermute | solution.py:76

commit v6 on v5

--- a/solution.py
+++ b/solution.py
@@ -97,15 +97,18 @@
         def start(n, table):
             place = ids[0, 0, n]
             r, k = place // across, place % across
-            read = jnp.where(place < WB * KB, place, n)
-            pltpu.make_async_copy(
-                panel_ref.at[
-                    pl.ds(pl.multiple_of(read // across * BS, BS), BS),
-                    pl.ds(pl.multiple_of(read % across * BS, BS), BS),
-                ],
-                out_ref.at[pl.ds(pl.multiple_of(n * BS, BS), BS), :],
-                sems.at[side],
-            ).start()
+            at = pl.ds(pl.multiple_of(n * BS, BS), BS)
+
+            @pl.when(place < WB * KB)
+            def _():
+                pltpu.make_async_copy(
+                    panel_ref.at[
+                        pl.ds(pl.multiple_of(r * BS, BS), BS), pl.ds(pl.multiple_of(k * BS, BS), BS)
+                    ],
+                    out_ref.at[at, :],
+                    sems.at[side],
+                ).start()
+
             outer, inner = (r, k) if across == KB else (k, r)
             return jnp.where((row == outer) & (lane == inner), n, table)
 
@@ -116,9 +119,17 @@
         out_ref[pl.ds(STORED, BS), :] = jnp.zeros((BS, BS), out_ref.dtype)
         both = jnp.concatenate([table, table], axis=0).astype(jnp.float32)
         out_ref[pl.ds(TABLE_AT, TABLE), :] = both.astype(out_ref.dtype)
-    for side, (_, _, out_ref, _) in enumerate(sides):
-        blocks = out_ref.at[pl.ds(0, STORED), :]
-        pltpu.make_async_copy(blocks, blocks, sems.at[side]).wait()
+    for side, (ids, _, out_ref, _) in enumerate(sides):
+
+        def finish(n, carry):
+            @pl.when(ids[0, 0, n] < WB * KB)
+            def _():
+                block = out_ref.at[pl.ds(0, BS), :]
+                pltpu.make_async_copy(block, block, sems.at[side]).wait()
+
+            return carry
+
+        lax.fori_loop(0, MAXB, finish, 0, unroll=13)
 
 
 def gather_blocks(left, right, left_ids, right_ids):

time: 85 us -> 85.1 us (level)
    pallas_call x5, Pallas kernels: 7.46 us -> 8.64 us  [run_kernel(): pl.pallas_call(kernel, out_shape=out_shape, in_specs=in_specs, out_specs=...]
    pallas_call x1, Pallas kernels: 4.12 us -> 3.15 us  [gather_blocks(): pl.pallas_call(gather_blocks_kernel, out_shape=[pltpu.VMEM((PACKED, BS),...]
  transfers between devices with their start and end apart: 7 -> 7, of which waited for: 4 -> 4; matrix products, arithmetic and copies ran while one was open for 0% -> 0% of each run, Pallas kernels for 7% -> 9%
where the time goes in v6:
time: 85.1 us; the launch traced here: 84.8 us
  waiting for transfers between devices  57.7 us (68%)
  starting transfers between devices  13.7 us (16%)
  Pallas kernels  11.8 us (14%)
  between operations  1.39 us (2%)
    ppermute x7, waiting for transfers between devices, move(): return lax.ppermute(value, AXES, pairs)  57.7 us
    ppermute x7, starting transfers between devices, move(): return lax.ppermute(value, AXES, pairs)  13.7 us
    pallas_call x5, Pallas kernels, run_kernel(): pl.pallas_call(kernel, out_shape=out_shape, in_specs=in_specs, out_specs=...  8.64 us
    pallas_call x1, Pallas kernels, gather_blocks(): pl.pallas_call(gather_blocks_kernel, out_shape=[pltpu.VMEM((PACKED, BS),...  3.15 us
  transfers between devices with their start and end apart: 7, of which 4 were waited for; matrix products, arithmetic and copies ran while one was open for 0% of the time, Pallas kernels for 9%

profile of v6, /device:TPU:0, one launch (start us, length us, event | category | flops | bytes accessed | tf_op | source)
XLA Modules:
  0.0 84.8 jit_solution(6347819165992281464)
XLA Ops:
  0.6 3.2 %shard_map.95 = (bf16[10128,128]{1,0:T(8,128)(2,1)S(1)}, bf16[10128,128]{1,0:T(8,128)(2,1)S(1)}) custom-call(s32[1,1,78]{2,1,0:T(1,128)} %left_ids_ref.1, s32[1,1,78]{2,1,0:T(1,128)} %right_ids_ref.1, bf16[256,12544]{1,0:T(8,128)(2,1)} %left_ref.1, bf16[12544,256]{1,0:T(8,128)(2,1)} %right_ref.1), custom_call_target="tpu_custom_call" | custom-call | bytes 10371072 | tf_op jit(solution)/shard_map/pallas_call | solution.py:137
  3.8 4.8 %collective-permute-start = (bf16[10128,128]{1,0:T(8,128)(2,1)S(1)}, bf16[10128,128]{1,0:T(8,128)(2,1)S(1)}, u32[]{:S(2)}, u32[]{:S(2)}) collective-permute-start(bf16[10128,128]{1,0:T(8,128)(2,1)S(1)} %get-tuple-element.6.left_ref.left_own_ref), channel_id=1, source_target_pairs={{0,115},{1,112},{2,117},{3,118},{4,119},{5,116},{6,121},{7,122},{8... | collective-permute-start | bytes 7778312 | tf_op jit(solution)/shard_map/ppermute | solution.py:76
  8.6 0.8 collective-permute-start.1
  9.4 0.5 collective-permute-start.3
  9.9 0.8 collective-permute-start.4
  10.7 2.1 %shard_map.96.own_ref = f32[256,256]{1,0:T(8,128)S(1)} custom-call(bf16[10128,128]{1,0:T(8,128)(2,1)S(1)} %get-tuple-element.6.left_ref.left_own_ref, bf16[10128,128]{1,0:T(8,128)(2,1)S(1)} %get-tuple-element.7.right_ref.right_own_ref), custom_call_target="tpu_custom_call" | custom-call | flops 671088640 | bytes 262144 | tf_op jit(solution)/shard_map/pallas_call | solution.py:331
  12.8 49.3 %collective-permute-done.left_near_ref = bf16[10128,128]{1,0:T(8,128)(2,1)S(1)} collective-permute-done((bf16[10128,128]{1,0:T(8,128)(2,1)S(1)}, bf16[10128,128]{1,0:T(8,128)(2,1)S(1)}, u32[]{:S(2)}, u32[]{:S(2)}) %collective-permute-start) | collective-permute-done | bytes 2592800 | tf_op jit(solution)/shard_map/ppermute | solution.py:76
  62.1 0.0 collective-permute-done.1.right_far_ref
  62.1 1.5 %shard_map.97.one_ref = bf16[256,256]{1,0:T(8,128)(2,1)S(1)} custom-call(f32[256,256]{1,0:T(8,128)S(1)} %shard_map.96.own_ref, bf16[10128,128]{1,0:T(8,128)(2,1)S(1)} %collective-permute-done.left_near_ref, bf16[10128,128]{1,0:T(8,128)(2,1)S(1)} %collective-permute-done.1.right_far_ref, bf16[10128,128]{1,0:T(8,128)(2,1)S(1)} %get-tuple-element.7.right_ref.right_own_ref), custom_call_target="tpu_custom_call" | custom-call | flops 671088640 | bytes 262144 | tf_op jit(solution)/shard_map/pallas_call | solution.py:331
  63.6 0.0 copy-start.2
  63.6 0.0 copy-start.1
  63.6 0.0 copy-start
  63.7 6.7 %collective-permute-start.2 = (bf16[256,256]{1,0:T(8,128)(2,1)S(1)}, bf16[256,256]{1,0:T(8,128)(2,1)S(1)}, u32[]{:S(2)}, u32[]{:S(2)}) collective-permute-start(bf16[256,256]{1,0:T(8,128)(2,1)S(1)} %shard_map.97.one_ref), channel_id=1, source_target_pairs={{0,16},{1,17},{2,18},{3,19},{4,20},{5,21},{6,22},{7,23},{8,24},{9,... | collective-permute-start | bytes 393224 | tf_op jit(solution)/shard_map/ppermute | solution.py:76
  70.4 0.0 collective-permute-done.3.right_near_ref
  70.4 0.0 collective-permute-done.4.left_far_ref
  70.4 2.9 %shard_map.99 = (bf16[256,256]{1,0:T(8,128)(2,1)S(1)}, bf16[256,256]{1,0:T(8,128)(2,1)S(1)}) custom-call(bf16[256,256]{1,0:T(8,128)(2,1)S(1)} %shard_map.97.one_ref, bf16[10128,128]{1,0:T(8,128)(2,1)S(1)} %collective-permute-done.left_near_ref, bf16[10128,128]{1,0:T(8,128)(2,1)S(1)} %collective-permute-done.3.right_near_ref, ...), custom_call_target="tpu_custom_call" | custom-call | flops 1342177280 | bytes 524288 | tf_op jit(solution)/shard_map/pallas_call | solution.py:331
  73.3 0.1 collective-permute-start.5
  73.4 0.1 collective-permute-start.6
  73.5 0.1 copy.11.filter_ref
  74.2 3.0 %collective-permute-done.2.one_ref = bf16[256,256]{1,0:T(8,128)(2,1)S(1)} collective-permute-done((bf16[256,256]{1,0:T(8,128)(2,1)S(1)}, bf16[256,256]{1,0:T(8,128)(2,1)S(1)}, u32[]{:S(2)}, u32[]{:S(2)}) %collective-permute-start.2) | collective-permute-done | bytes 131104 | tf_op jit(solution)/shard_map/ppermute | solution.py:76
  77.3 0.7 shard_map.98.base_ref
  78.0 1.9 %collective-permute-done.5.two_ref = bf16[256,256]{1,0:T(8,128)(2,1)S(1)} collective-permute-done((bf16[256,256]{1,0:T(8,128)(2,1)S(1)}, bf16[256,256]{1,0:T(8,128)(2,1)S(1)}, u32[]{:S(2)}, u32[]{:S(2)}) %collective-permute-start.5) | collective-permute-done | bytes 131104 | tf_op jit(solution)/shard_map/ppermute | solution.py:76
  79.9 3.5 %collective-permute-done.6.three_ref = bf16[256,256]{1,0:T(8,128)(2,1)S(1)} collective-permute-done((bf16[256,256]{1,0:T(8,128)(2,1)S(1)}, bf16[256,256]{1,0:T(8,128)(2,1)S(1)}, u32[]{:S(2)}, u32[]{:S(2)}) %collective-permute-start.6) | collective-permute-done | bytes 131104 | tf_op jit(solution)/shard_map/ppermute | solution.py:76
  83.3 1.4 %shard_map.100 = (bf16[256,256]{1,0:T(8,128)(2,1)}, f32[256,256]{1,0:T(8,128)}) custom-call(s32[4,2,2]{2,1,0:T(2,128)S(1)} %copy.11.filter_ref, f32[1]{0:T(128)S(6)} %copy.12.coefficient_ref, f32[256,256]{1,0:T(8,128)S(1)} %shard_map.98.base_ref, bf16[256,256]{1,0:T(8,128)(2,1)S(1)} %collective-permute-done.5.two_ref, ...), custom_call_target="tpu_custom_call" | custom-call | bytes 524288 | tf_op jit(solution)/shard_map/pallas_call | solution.py:331
  (3 shorter events, 0.0 us)
Async XLA Ops:
  3.8 58.3 %collective-permute-start = (bf16[10128,128]{1,0:T(8,128)(2,1)S(1)}, bf16[10128,128]{1,0:T(8,128)(2,1)S(1)}, u32[]{:S(2)}, u32[]{:S(2)}) collective-permute-start(bf16[10128,128]{1,0:T(8,128)(2,1)S(1)} %get-tuple-element.6.left_ref.left_own_ref), channel_id=1, source_target_pairs={{0,115},{1,112},{2,117},{3,118},{4,119},{5,116},{6,121},{7,122},{8... | collective-permute-start | bytes 7778312 | tf_op jit(solution)/shard_map/ppermute | solution.py:76
  8.6 53.6 %collective-permute-start.1 = (bf16[10128,128]{1,0:T(8,128)(2,1)S(1)}, bf16[10128,128]{1,0:T(8,128)(2,1)S(1)}, u32[]{:S(2)}, u32[]{:S(2)}) collective-permute-start(bf16[10128,128]{1,0:T(8,128)(2,1)S(1)} %get-tuple-element.7.right_ref.right_own_ref), channel_id=1, source_target_pairs={{16,60},{17,49},{18,50},{19,51},{20,48},{21,53},{22,54},{23,55},{2... | collective-permute-start | bytes 7778312 | tf_op jit(solution)/shard_map/ppermute | solution.py:76
  9.4 61.0 %collective-permute-start.3 = (bf16[10128,128]{1,0:T(8,128)(2,1)S(1)}, bf16[10128,128]{1,0:T(8,128)(2,1)S(1)}, u32[]{:S(2)}, u32[]{:S(2)}) collective-permute-start(bf16[10128,128]{1,0:T(8,128)(2,1)S(1)} %get-tuple-element.7.right_ref.right_own_ref), channel_id=1, source_target_pairs={{0,17},{1,18},{2,19},{3,16},{4,21},{5,22},{6,23},{7,20},{8,25},{9,... | collective-permute-start | bytes 7778312 | tf_op jit(solution)/shard_map/ppermute | solution.py:76
  9.9 60.5 %collective-permute-start.4 = (bf16[10128,128]{1,0:T(8,128)(2,1)S(1)}, bf16[10128,128]{1,0:T(8,128)(2,1)S(1)}, u32[]{:S(2)}, u32[]{:S(2)}) collective-permute-start(bf16[10128,128]{1,0:T(8,128)(2,1)S(1)} %get-tuple-element.6.left_ref.left_own_ref), channel_id=1, source_target_pairs={{16,112},{17,117},{18,118},{19,119},{20,116},{21,121},{22,122},{23... | collective-permute-start | bytes 7778312 | tf_op jit(solution)/shard_map/ppermute | solution.py:76
  63.6 9.9 %copy-start.2 = (s32[4,2,2]{0,2,1:T(2,128)S(1)}, s32[4,2,2]{0,2,1:T(2,128)}, u32[]{:S(2)}) copy-start(s32[4,2,2]{0,2,1:T(2,128)} %param.12) | copy-start | bytes 196
  63.6 13.7 %copy-start.1 = (bf16[256,256]{1,0:T(8,128)(2,1)S(1)}, bf16[256,256]{1,0:T(8,128)(2,1)}, u32[]{:S(2)}) copy-start(bf16[256,256]{1,0:T(8,128)(2,1)} %before_ref.1) | copy-start | bytes 393220
  63.6 19.7 %copy-start = (f32[256,256]{1,0:T(8,128)S(1)}, f32[256,256]{1,0:T(8,128)}, u32[]{:S(2)}) copy-start(f32[256,256]{1,0:T(8,128)} %density_ref.1) | copy-start | bytes 786436
  63.7 13.6 %collective-permute-start.2 = (bf16[256,256]{1,0:T(8,128)(2,1)S(1)}, bf16[256,256]{1,0:T(8,128)(2,1)S(1)}, u32[]{:S(2)}, u32[]{:S(2)}) collective-permute-start(bf16[256,256]{1,0:T(8,128)(2,1)S(1)} %shard_map.97.one_ref), channel_id=1, source_target_pairs={{0,16},{1,17},{2,18},{3,19},{4,20},{5,21},{6,22},{7,23},{8,24},{9,... | collective-permute-start | bytes 393224 | tf_op jit(solution)/shard_map/ppermute | solution.py:76
  73.3 6.6 %collective-permute-start.5 = (bf16[256,256]{1,0:T(8,128)(2,1)S(1)}, bf16[256,256]{1,0:T(8,128)(2,1)S(1)}, u32[]{:S(2)}, u32[]{:S(2)}) collective-permute-start(bf16[256,256]{1,0:T(8,128)(2,1)S(1)} %get-tuple-element.8), channel_id=1, source_target_pairs={{0,17},{1,18},{2,19},{3,20},{4,21},{5,22},{6,23},{7,24},{8,25},{9,... | collective-permute-start | bytes 393224 | tf_op jit(solution)/shard_map/ppermute | solution.py:76
  73.4 10.0 %collective-permute-start.6 = (bf16[256,256]{1,0:T(8,128)(2,1)S(1)}, bf16[256,256]{1,0:T(8,128)(2,1)S(1)}, u32[]{:S(2)}, u32[]{:S(2)}) collective-permute-start(bf16[256,256]{1,0:T(8,128)(2,1)S(1)} %get-tuple-element.9), channel_id=1, source_target_pairs={{0,1},{1,2},{2,3},{3,4},{4,5},{5,6},{6,7},{7,8},{8,9},{9,10},{10,1... | collective-permute-start | bytes 393224 | tf_op jit(solution)/shard_map/ppermute | solution.py:76

commit v7 on v6

--- a/solution.py
+++ b/solution.py
@@ -225,11 +225,17 @@
     return jnp.concatenate(rows, axis=0)
 
 
-def base_kernel(filter_ref, own_ref, one_ref, before_ref, out_ref):
+def base_kernel(
+    filter_ref, coefficient_ref, own_ref, one_ref, before_ref, out_ref, two_factor, three_factor, scale
+):
     odd = lax.axis_index("row") % 2
     one = masked(filter_ref, 3 - 2 * odd, one_ref[...].astype(jnp.float32))
     total = masked(filter_ref, 0, own_ref[...]) + one
     out_ref[...] = 2.0 * total - before_ref[...].astype(jnp.float32)
+    twos = jnp.full(PANEL, 2.0, jnp.float32)
+    two_factor[...] = masked(filter_ref, 2, twos)
+    three_factor[...] = masked(filter_ref, 1 + 2 * odd, twos)
+    scale[...] = jnp.full(scale.shape, coefficient_ref[0], jnp.float32)
 
 
 def send_product(left_ref, right_ref, words, chosen, product, out_ref):
@@ -302,15 +308,13 @@
 
 
 def final_kernel(
-    filter_ref, coefficient_ref, base_ref, two_ref, three_ref, density_ref, term_out, density_out
-):
-    odd = lax.axis_index("row") % 2
-    two = masked(filter_ref, 2, two_ref[...].astype(jnp.float32))
-    three = masked(filter_ref, 1 + 2 * odd, three_ref[...].astype(jnp.float32))
-    total = two + three
-    term_next = (2.0 * total + base_ref[...]).astype(jnp.bfloat16)
+    base_ref, two_factor, three_factor, scale, two_ref, three_ref, density_ref, term_out, density_out
+):
+    two = two_factor[...] * two_ref[...].astype(jnp.float32)
+    three = three_factor[...] * three_ref[...].astype(jnp.float32)
+    term_next = (base_ref[...] + (two + three)).astype(jnp.bfloat16)
     term_out[...] = term_next
-    density_out[...] = density_ref[...] + coefficient_ref[0] * term_next.astype(jnp.float32)
+    density_out[...] = density_ref[...] + scale[0:1, 0:1] * term_next.astype(jnp.float32)
 
 
 ANYWHERE = pl.BlockSpec(memory_space=pl.ANY)
@@ -390,29 +394,31 @@
         *[in_vmem(panel) for panel in (left_n, right_n, left_f, left_own)],
     )
     two, three, one = move(two, home_two), move(three, home_three), move(one, home_one)
-    (base,) = run_kernel(
+    base, two_factor, three_factor, scale = run_kernel(
         base_kernel,
-        [IN_SMEM] + [IN_VMEM] * 3,
-        [RESULT],
+        [IN_SMEM] * 2 + [IN_VMEM] * 3,
+        [RESULT] * 3 + [jax.ShapeDtypeStruct((8, LANES), jnp.float32)],
         [],
         0,
         product_filter,
+        coefficient,
         own,
         one,
         term_before,
     )
     term_next, density_out = run_kernel(
         final_kernel,
-        [IN_SMEM] * 2 + [IN_VMEM] * 4,
+        [IN_VMEM] * 7,
         [
             jax.ShapeDtypeStruct(term_before.shape, jnp.bfloat16),
             jax.ShapeDtypeStruct(density_in.shape, jnp.float32),
         ],
         [],
         0,
-        product_filter,
-        coefficient,
         base,
+        two_factor,
+        three_factor,
+        scale,
         two,
         three,
         density_in,

time: 85.1 us -> 83.2 us (0.978)
  Pallas kernels: 11.8 us -> 10.7 us
    pallas_call x5, Pallas kernels: 8.64 us -> 7.49 us  [run_kernel(): pl.pallas_call(kernel, out_shape=out_shape, in_specs=in_specs, out_specs=...]
  transfers between devices with their start and end apart: 7 -> 7, of which waited for: 4 -> 4; matrix products, arithmetic and copies ran while one was open for 0% -> 0% of each run, Pallas kernels for 9% -> 8%
where the time goes in v7:
time: 83.2 us; the launch traced here: 83.5 us
  waiting for transfers between devices  56.9 us (68%)
  starting transfers between devices  14.4 us (17%)
  Pallas kernels  10.7 us (13%)
  between operations  1.37 us (2%)
    ppermute x7, waiting for transfers between devices, move(): return lax.ppermute(value, AXES, pairs)  56.9 us
    ppermute x7, starting transfers between devices, move(): return lax.ppermute(value, AXES, pairs)  14.4 us
    pallas_call x5, Pallas kernels, run_kernel(): pl.pallas_call(kernel, out_shape=out_shape, in_specs=in_specs, out_specs=...  7.49 us
    pallas_call x1, Pallas kernels, gather_blocks(): pl.pallas_call(gather_blocks_kernel, out_shape=[pltpu.VMEM((PACKED, BS),...  3.17 us
  transfers between devices with their start and end apart: 7, of which 4 were waited for; matrix products, arithmetic and copies ran while one was open for 0% of the time, Pallas kernels for 8%

profile of v7, /device:TPU:0, one launch (start us, length us, event | category | flops | bytes accessed | tf_op | source)
XLA Modules:
  0.0 83.5 jit_solution(8876406537661834679)
XLA Ops:
  0.6 3.2 %shard_map.95 = (bf16[10128,128]{1,0:T(8,128)(2,1)S(1)}, bf16[10128,128]{1,0:T(8,128)(2,1)S(1)}) custom-call(s32[1,1,78]{2,1,0:T(1,128)} %left_ids_ref.1, s32[1,1,78]{2,1,0:T(1,128)} %right_ids_ref.1, bf16[256,12544]{1,0:T(8,128)(2,1)} %left_ref.1, bf16[12544,256]{1,0:T(8,128)(2,1)} %right_ref.1), custom_call_target="tpu_custom_call" | custom-call | bytes 10371072 | tf_op jit(solution)/shard_map/pallas_call | solution.py:137
  3.8 4.7 %collective-permute-start = (bf16[10128,128]{1,0:T(8,128)(2,1)S(1)}, bf16[10128,128]{1,0:T(8,128)(2,1)S(1)}, u32[]{:S(2)}, u32[]{:S(2)}) collective-permute-start(bf16[10128,128]{1,0:T(8,128)(2,1)S(1)} %get-tuple-element.10.left_ref.left_own_ref), channel_id=1, source_target_pairs={{0,115},{1,112},{2,117},{3,118},{4,119},{5,116},{6,121},{7,122},{8... | collective-permute-start | bytes 7778312 | tf_op jit(solution)/shard_map/ppermute | solution.py:76
  8.6 0.8 collective-permute-start.1
  9.4 0.5 collective-permute-start.3
  9.9 0.8 collective-permute-start.4
  10.7 1.5 %shard_map.96.own_ref = f32[256,256]{1,0:T(8,128)S(1)} custom-call(bf16[10128,128]{1,0:T(8,128)(2,1)S(1)} %get-tuple-element.10.left_ref.left_own_ref, bf16[10128,128]{1,0:T(8,128)(2,1)S(1)} %get-tuple-element.11.right_ref.right_own_ref), custom_call_target="tpu_custom_call" | custom-call | flops 671088640 | bytes 262144 | tf_op jit(solution)/shard_map/pallas_call | solution.py:335
  12.2 49.9 %collective-permute-done.left_near_ref = bf16[10128,128]{1,0:T(8,128)(2,1)S(1)} collective-permute-done((bf16[10128,128]{1,0:T(8,128)(2,1)S(1)}, bf16[10128,128]{1,0:T(8,128)(2,1)S(1)}, u32[]{:S(2)}, u32[]{:S(2)}) %collective-permute-start) | collective-permute-done | bytes 2592800 | tf_op jit(solution)/shard_map/ppermute | solution.py:76
  62.1 0.0 collective-permute-done.1.right_far_ref
  62.1 1.5 %shard_map.97.one_ref = bf16[256,256]{1,0:T(8,128)(2,1)S(1)} custom-call(f32[256,256]{1,0:T(8,128)S(1)} %shard_map.96.own_ref, bf16[10128,128]{1,0:T(8,128)(2,1)S(1)} %collective-permute-done.left_near_ref, bf16[10128,128]{1,0:T(8,128)(2,1)S(1)} %collective-permute-done.1.right_far_ref, bf16[10128,128]{1,0:T(8,128)(2,1)S(1)} %get-tuple-element.11.right_ref.right_own_ref), custom_call_target="tpu_custom_call" | custom-call | flops 671088640 | bytes 262144 | tf_op jit(solution)/shard_map/pallas_call | solution.py:335
  63.6 0.0 copy-start.2
  63.6 0.0 copy-start.1
  63.7 0.0 copy-start
  63.7 6.0 %collective-permute-start.2 = (bf16[256,256]{1,0:T(8,128)(2,1)S(1)}, bf16[256,256]{1,0:T(8,128)(2,1)S(1)}, u32[]{:S(2)}, u32[]{:S(2)}) collective-permute-start(bf16[256,256]{1,0:T(8,128)(2,1)S(1)} %shard_map.97.one_ref), channel_id=1, source_target_pairs={{0,16},{1,17},{2,18},{3,19},{4,20},{5,21},{6,22},{7,23},{8,24},{9,... | collective-permute-start | bytes 393224 | tf_op jit(solution)/shard_map/ppermute | solution.py:76
  69.6 0.0 collective-permute-done.3.right_near_ref
  69.6 0.0 collective-permute-done.4.left_far_ref
  69.6 3.0 %shard_map.99 = (bf16[256,256]{1,0:T(8,128)(2,1)S(1)}, bf16[256,256]{1,0:T(8,128)(2,1)S(1)}) custom-call(bf16[256,256]{1,0:T(8,128)(2,1)S(1)} %shard_map.97.one_ref, bf16[10128,128]{1,0:T(8,128)(2,1)S(1)} %collective-permute-done.left_near_ref, bf16[10128,128]{1,0:T(8,128)(2,1)S(1)} %collective-permute-done.3.right_near_ref, ...), custom_call_target="tpu_custom_call" | custom-call | flops 1342177280 | bytes 524288 | tf_op jit(solution)/shard_map/pallas_call | solution.py:335
  72.6 1.2 %collective-permute-start.5 = (bf16[256,256]{1,0:T(8,128)(2,1)S(1)}, bf16[256,256]{1,0:T(8,128)(2,1)S(1)}, u32[]{:S(2)}, u32[]{:S(2)}) collective-permute-start(bf16[256,256]{1,0:T(8,128)(2,1)S(1)} %get-tuple-element.16), channel_id=1, source_target_pairs={{0,17},{1,18},{2,19},{3,20},{4,21},{5,22},{6,23},{7,24},{8,25},{9,... | collective-permute-start | bytes 393224 | tf_op jit(solution)/shard_map/ppermute | solution.py:76
  73.8 0.4 collective-permute-start.6
  74.2 0.1 copy.10.filter_ref
  74.9 1.8 %collective-permute-done.2.one_ref = bf16[256,256]{1,0:T(8,128)(2,1)S(1)} collective-permute-done((bf16[256,256]{1,0:T(8,128)(2,1)S(1)}, bf16[256,256]{1,0:T(8,128)(2,1)S(1)}, u32[]{:S(2)}, u32[]{:S(2)}) %collective-permute-start.2) | collective-permute-done | bytes 131104 | tf_op jit(solution)/shard_map/ppermute | solution.py:76
  76.7 0.7 shard_map.98
  77.4 1.7 %collective-permute-done.5.two_ref = bf16[256,256]{1,0:T(8,128)(2,1)S(1)} collective-permute-done((bf16[256,256]{1,0:T(8,128)(2,1)S(1)}, bf16[256,256]{1,0:T(8,128)(2,1)S(1)}, u32[]{:S(2)}, u32[]{:S(2)}) %collective-permute-start.5) | collective-permute-done | bytes 131104 | tf_op jit(solution)/shard_map/ppermute | solution.py:76
  79.2 3.5 %collective-permute-done.6.three_ref = bf16[256,256]{1,0:T(8,128)(2,1)S(1)} collective-permute-done((bf16[256,256]{1,0:T(8,128)(2,1)S(1)}, bf16[256,256]{1,0:T(8,128)(2,1)S(1)}, u32[]{:S(2)}, u32[]{:S(2)}) %collective-permute-start.6) | collective-permute-done | bytes 131104 | tf_op jit(solution)/shard_map/ppermute | solution.py:76
  82.6 0.8 %shard_map.100 = (bf16[256,256]{1,0:T(8,128)(2,1)}, f32[256,256]{1,0:T(8,128)}) custom-call(f32[256,256]{1,0:T(8,128)S(1)} %get-tuple-element.12.base_ref, f32[256,256]{1,0:T(8,128)S(1)} %get-tuple-element.13.two_factor, f32[256,256]{1,0:T(8,128)S(1)} %get-tuple-element.14.three_factor, f32[8,128]{1,0:T(8,128)S(1)} %get-tuple-element.15.scale, ...), custom_call_target="tpu_custom_call" | custom-call | bytes 524288 | tf_op jit(solution)/shard_map/pallas_call | solution.py:335
  (3 shorter events, 0.0 us)
Async XLA Ops:
  3.8 58.3 %collective-permute-start = (bf16[10128,128]{1,0:T(8,128)(2,1)S(1)}, bf16[10128,128]{1,0:T(8,128)(2,1)S(1)}, u32[]{:S(2)}, u32[]{:S(2)}) collective-permute-start(bf16[10128,128]{1,0:T(8,128)(2,1)S(1)} %get-tuple-element.10.left_ref.left_own_ref), channel_id=1, source_target_pairs={{0,115},{1,112},{2,117},{3,118},{4,119},{5,116},{6,121},{7,122},{8... | collective-permute-start | bytes 7778312 | tf_op jit(solution)/shard_map/ppermute | solution.py:76
  8.6 53.6 %collective-permute-start.1 = (bf16[10128,128]{1,0:T(8,128)(2,1)S(1)}, bf16[10128,128]{1,0:T(8,128)(2,1)S(1)}, u32[]{:S(2)}, u32[]{:S(2)}) collective-permute-start(bf16[10128,128]{1,0:T(8,128)(2,1)S(1)} %get-tuple-element.11.right_ref.right_own_ref), channel_id=1, source_target_pairs={{16,60},{17,49},{18,50},{19,51},{20,48},{21,53},{22,54},{23,55},{2... | collective-permute-start | bytes 7778312 | tf_op jit(solution)/shard_map/ppermute | solution.py:76
  9.4 60.3 %collective-permute-start.3 = (bf16[10128,128]{1,0:T(8,128)(2,1)S(1)}, bf16[10128,128]{1,0:T(8,128)(2,1)S(1)}, u32[]{:S(2)}, u32[]{:S(2)}) collective-permute-start(bf16[10128,128]{1,0:T(8,128)(2,1)S(1)} %get-tuple-element.11.right_ref.right_own_ref), channel_id=1, source_target_pairs={{0,17},{1,18},{2,19},{3,16},{4,21},{5,22},{6,23},{7,20},{8,25},{9,... | collective-permute-start | bytes 7778312 | tf_op jit(solution)/shard_map/ppermute | solution.py:76
  9.9 59.8 %collective-permute-start.4 = (bf16[10128,128]{1,0:T(8,128)(2,1)S(1)}, bf16[10128,128]{1,0:T(8,128)(2,1)S(1)}, u32[]{:S(2)}, u32[]{:S(2)}) collective-permute-start(bf16[10128,128]{1,0:T(8,128)(2,1)S(1)} %get-tuple-element.10.left_ref.left_own_ref), channel_id=1, source_target_pairs={{16,112},{17,117},{18,118},{19,119},{20,116},{21,121},{22,122},{23... | collective-permute-start | bytes 7778312 | tf_op jit(solution)/shard_map/ppermute | solution.py:76
  63.6 10.5 %copy-start.2 = (s32[4,2,2]{0,2,1:T(2,128)S(1)}, s32[4,2,2]{0,2,1:T(2,128)}, u32[]{:S(2)}) copy-start(s32[4,2,2]{0,2,1:T(2,128)} %param.12) | copy-start | bytes 196
  63.6 13.1 %copy-start.1 = (bf16[256,256]{1,0:T(8,128)(2,1)S(1)}, bf16[256,256]{1,0:T(8,128)(2,1)}, u32[]{:S(2)}) copy-start(bf16[256,256]{1,0:T(8,128)(2,1)} %before_ref.1) | copy-start | bytes 393220
  63.7 19.0 %copy-start = (f32[256,256]{1,0:T(8,128)S(1)}, f32[256,256]{1,0:T(8,128)}, u32[]{:S(2)}) copy-start(f32[256,256]{1,0:T(8,128)} %density_ref.1) | copy-start | bytes 786436
  63.7 13.1 %collective-permute-start.2 = (bf16[256,256]{1,0:T(8,128)(2,1)S(1)}, bf16[256,256]{1,0:T(8,128)(2,1)S(1)}, u32[]{:S(2)}, u32[]{:S(2)}) collective-permute-start(bf16[256,256]{1,0:T(8,128)(2,1)S(1)} %shard_map.97.one_ref), channel_id=1, source_target_pairs={{0,16},{1,17},{2,18},{3,19},{4,20},{5,21},{6,22},{7,23},{8,24},{9,... | collective-permute-start | bytes 393224 | tf_op jit(solution)/shard_map/ppermute | solution.py:76
  72.6 6.6 %collective-permute-start.5 = (bf16[256,256]{1,0:T(8,128)(2,1)S(1)}, bf16[256,256]{1,0:T(8,128)(2,1)S(1)}, u32[]{:S(2)}, u32[]{:S(2)}) collective-permute-start(bf16[256,256]{1,0:T(8,128)(2,1)S(1)} %get-tuple-element.16), channel_id=1, source_target_pairs={{0,17},{1,18},{2,19},{3,20},{4,21},{5,22},{6,23},{7,24},{8,25},{9,... | collective-permute-start | bytes 393224 | tf_op jit(solution)/shard_map/ppermute | solution.py:76
  73.8 8.9 %collective-permute-start.6 = (bf16[256,256]{1,0:T(8,128)(2,1)S(1)}, bf16[256,256]{1,0:T(8,128)(2,1)S(1)}, u32[]{:S(2)}, u32[]{:S(2)}) collective-permute-start(bf16[256,256]{1,0:T(8,128)(2,1)S(1)} %get-tuple-element.17), channel_id=1, source_target_pairs={{0,1},{1,2},{2,3},{3,4},{4,5},{5,6},{6,7},{7,8},{8,9},{9,10},{10,1... | collective-permute-start | bytes 393224 | tf_op jit(solution)/shard_map/ppermute | solution.py:76

commit v8 on v7

--- a/solution.py
+++ b/solution.py
@@ -15,7 +15,7 @@
 N_ROW = 8
 N_COL = 16
 AXES = ("row", "col")
-GROUP = 24
+GROUP = 20
 LANES = 128
 KERNEL_VMEM = 6 * 1024 * 1024
 STORED = MAXB * BS

time: 83.2 us -> 83.4 us (level); the launches traced: 83.5 us -> 82 us
  waiting for transfers between devices: 56.9 us -> 55.7 us
    ppermute x7, waiting for transfers between devices: 56.9 us -> 55.7 us  [move(): return lax.ppermute(value, AXES, pairs)]
where the time goes in v8:
time: 83.4 us; the launch traced here: 82 us
  waiting for transfers between devices  55.7 us (67%)
  starting transfers between devices  14.1 us (17%)
  Pallas kernels  10.8 us (13%)
  between operations  1.37 us (2%)
    ppermute x7, waiting for transfers between devices, move(): return lax.ppermute(value, AXES, pairs)  55.7 us
    ppermute x7, starting transfers between devices, move(): return lax.ppermute(value, AXES, pairs)  14.1 us
    pallas_call x5, Pallas kernels, run_kernel(): pl.pallas_call(kernel, out_shape=out_shape, in_specs=in_specs, out_specs=...  7.67 us
    pallas_call x1, Pallas kernels, gather_blocks(): pl.pallas_call(gather_blocks_kernel, out_shape=[pltpu.VMEM((PACKED, BS),...  3.11 us
  transfers between devices with their start and end apart: 7, of which 4 were waited for; matrix products, arithmetic and copies ran while one was open for 0% of the time, Pallas kernels for 8%

profile of v8, /device:TPU:0, one launch (start us, length us, event | category | flops | bytes accessed | tf_op | source)
XLA Modules:
  0.0 82.0 jit_solution(14392546880253075032)
XLA Ops:
  0.6 3.1 %shard_map.95 = (bf16[10128,128]{1,0:T(8,128)(2,1)S(1)}, bf16[10128,128]{1,0:T(8,128)(2,1)S(1)}) custom-call(s32[1,1,78]{2,1,0:T(1,128)} %left_ids_ref.1, s32[1,1,78]{2,1,0:T(1,128)} %right_ids_ref.1, bf16[256,12544]{1,0:T(8,128)(2,1)} %left_ref.1, bf16[12544,256]{1,0:T(8,128)(2,1)} %right_ref.1), custom_call_target="tpu_custom_call" | custom-call | bytes 10371072 | tf_op jit(solution)/shard_map/pallas_call | solution.py:137
  3.8 4.9 %collective-permute-start = (bf16[10128,128]{1,0:T(8,128)(2,1)S(1)}, bf16[10128,128]{1,0:T(8,128)(2,1)S(1)}, u32[]{:S(2)}, u32[]{:S(2)}) collective-permute-start(bf16[10128,128]{1,0:T(8,128)(2,1)S(1)} %get-tuple-element.10.left_ref.left_own_ref), channel_id=1, source_target_pairs={{0,115},{1,112},{2,117},{3,118},{4,119},{5,116},{6,121},{7,122},{8... | collective-permute-start | bytes 7778312 | tf_op jit(solution)/shard_map/ppermute | solution.py:76
  8.6 0.8 collective-permute-start.1
  9.4 0.4 collective-permute-start.3
  9.9 0.8 collective-permute-start.4
  10.7 1.4 %shard_map.96.own_ref = f32[256,256]{1,0:T(8,128)S(1)} custom-call(bf16[10128,128]{1,0:T(8,128)(2,1)S(1)} %get-tuple-element.10.left_ref.left_own_ref, bf16[10128,128]{1,0:T(8,128)(2,1)S(1)} %get-tuple-element.11.right_ref.right_own_ref), custom_call_target="tpu_custom_call" | custom-call | flops 671088640 | bytes 262144 | tf_op jit(solution)/shard_map/pallas_call | solution.py:335
  12.1 50.1 %collective-permute-done.left_near_ref = bf16[10128,128]{1,0:T(8,128)(2,1)S(1)} collective-permute-done((bf16[10128,128]{1,0:T(8,128)(2,1)S(1)}, bf16[10128,128]{1,0:T(8,128)(2,1)S(1)}, u32[]{:S(2)}, u32[]{:S(2)}) %collective-permute-start) | collective-permute-done | bytes 2592800 | tf_op jit(solution)/shard_map/ppermute | solution.py:76
  62.2 0.0 collective-permute-done.1.right_far_ref
  62.2 2.0 %shard_map.97.one_ref = bf16[256,256]{1,0:T(8,128)(2,1)S(1)} custom-call(f32[256,256]{1,0:T(8,128)S(1)} %shard_map.96.own_ref, bf16[10128,128]{1,0:T(8,128)(2,1)S(1)} %collective-permute-done.left_near_ref, bf16[10128,128]{1,0:T(8,128)(2,1)S(1)} %collective-permute-done.1.right_far_ref, bf16[10128,128]{1,0:T(8,128)(2,1)S(1)} %get-tuple-element.11.right_ref.right_own_ref), custom_call_target="tpu_custom_call" | custom-call | flops 671088640 | bytes 262144 | tf_op jit(solution)/shard_map/pallas_call | solution.py:335
  64.2 0.0 copy-start.2
  64.2 0.0 copy-start.1
  64.2 0.0 copy-start
  64.2 5.3 %collective-permute-start.2 = (bf16[256,256]{1,0:T(8,128)(2,1)S(1)}, bf16[256,256]{1,0:T(8,128)(2,1)S(1)}, u32[]{:S(2)}, u32[]{:S(2)}) collective-permute-start(bf16[256,256]{1,0:T(8,128)(2,1)S(1)} %shard_map.97.one_ref), channel_id=1, source_target_pairs={{0,16},{1,17},{2,18},{3,19},{4,20},{5,21},{6,22},{7,23},{8,24},{9,... | collective-permute-start | bytes 393224 | tf_op jit(solution)/shard_map/ppermute | solution.py:76
  69.5 0.0 collective-permute-done.3.right_near_ref
  69.5 0.0 collective-permute-done.4.left_far_ref
  69.6 2.7 %shard_map.99 = (bf16[256,256]{1,0:T(8,128)(2,1)S(1)}, bf16[256,256]{1,0:T(8,128)(2,1)S(1)}) custom-call(bf16[256,256]{1,0:T(8,128)(2,1)S(1)} %shard_map.97.one_ref, bf16[10128,128]{1,0:T(8,128)(2,1)S(1)} %collective-permute-done.left_near_ref, bf16[10128,128]{1,0:T(8,128)(2,1)S(1)} %collective-permute-done.3.right_near_ref, ...), custom_call_target="tpu_custom_call" | custom-call | flops 1342177280 | bytes 524288 | tf_op jit(solution)/shard_map/pallas_call | solution.py:335
  72.3 0.4 collective-permute-start.5
  72.7 1.5 %collective-permute-start.6 = (bf16[256,256]{1,0:T(8,128)(2,1)S(1)}, bf16[256,256]{1,0:T(8,128)(2,1)S(1)}, u32[]{:S(2)}, u32[]{:S(2)}) collective-permute-start(bf16[256,256]{1,0:T(8,128)(2,1)S(1)} %get-tuple-element.17), channel_id=1, source_target_pairs={{0,1},{1,2},{2,3},{3,4},{4,5},{5,6},{6,7},{7,8},{8,9},{9,10},{10,1... | collective-permute-start | bytes 393224 | tf_op jit(solution)/shard_map/ppermute | solution.py:76
  74.2 0.1 copy.10.filter_ref
  74.9 1.7 %collective-permute-done.2.one_ref = bf16[256,256]{1,0:T(8,128)(2,1)S(1)} collective-permute-done((bf16[256,256]{1,0:T(8,128)(2,1)S(1)}, bf16[256,256]{1,0:T(8,128)(2,1)S(1)}, u32[]{:S(2)}, u32[]{:S(2)}) %collective-permute-start.2) | collective-permute-done | bytes 131104 | tf_op jit(solution)/shard_map/ppermute | solution.py:76
  76.6 0.7 shard_map.98
  77.4 1.5 %collective-permute-done.5.two_ref = bf16[256,256]{1,0:T(8,128)(2,1)S(1)} collective-permute-done((bf16[256,256]{1,0:T(8,128)(2,1)S(1)}, bf16[256,256]{1,0:T(8,128)(2,1)S(1)}, u32[]{:S(2)}, u32[]{:S(2)}) %collective-permute-start.5) | collective-permute-done | bytes 131104 | tf_op jit(solution)/shard_map/ppermute | solution.py:76
  78.9 2.3 %collective-permute-done.6.three_ref = bf16[256,256]{1,0:T(8,128)(2,1)S(1)} collective-permute-done((bf16[256,256]{1,0:T(8,128)(2,1)S(1)}, bf16[256,256]{1,0:T(8,128)(2,1)S(1)}, u32[]{:S(2)}, u32[]{:S(2)}) %collective-permute-start.6) | collective-permute-done | bytes 131104 | tf_op jit(solution)/shard_map/ppermute | solution.py:76
  81.2 0.8 %shard_map.100 = (bf16[256,256]{1,0:T(8,128)(2,1)}, f32[256,256]{1,0:T(8,128)}) custom-call(f32[256,256]{1,0:T(8,128)S(1)} %get-tuple-element.12.base_ref, f32[256,256]{1,0:T(8,128)S(1)} %get-tuple-element.13.two_factor, f32[256,256]{1,0:T(8,128)S(1)} %get-tuple-element.14.three_factor, f32[8,128]{1,0:T(8,128)S(1)} %get-tuple-element.15.scale, ...), custom_call_target="tpu_custom_call" | custom-call | bytes 524288 | tf_op jit(solution)/shard_map/pallas_call | solution.py:335
  (3 shorter events, 0.0 us)
Async XLA Ops:
  3.8 58.5 %collective-permute-start = (bf16[10128,128]{1,0:T(8,128)(2,1)S(1)}, bf16[10128,128]{1,0:T(8,128)(2,1)S(1)}, u32[]{:S(2)}, u32[]{:S(2)}) collective-permute-start(bf16[10128,128]{1,0:T(8,128)(2,1)S(1)} %get-tuple-element.10.left_ref.left_own_ref), channel_id=1, source_target_pairs={{0,115},{1,112},{2,117},{3,118},{4,119},{5,116},{6,121},{7,122},{8... | collective-permute-start | bytes 7778312 | tf_op jit(solution)/shard_map/ppermute | solution.py:76
  8.6 53.6 %collective-permute-start.1 = (bf16[10128,128]{1,0:T(8,128)(2,1)S(1)}, bf16[10128,128]{1,0:T(8,128)(2,1)S(1)}, u32[]{:S(2)}, u32[]{:S(2)}) collective-permute-start(bf16[10128,128]{1,0:T(8,128)(2,1)S(1)} %get-tuple-element.11.right_ref.right_own_ref), channel_id=1, source_target_pairs={{16,60},{17,49},{18,50},{19,51},{20,48},{21,53},{22,54},{23,55},{2... | collective-permute-start | bytes 7778312 | tf_op jit(solution)/shard_map/ppermute | solution.py:76
  9.4 60.1 %collective-permute-start.3 = (bf16[10128,128]{1,0:T(8,128)(2,1)S(1)}, bf16[10128,128]{1,0:T(8,128)(2,1)S(1)}, u32[]{:S(2)}, u32[]{:S(2)}) collective-permute-start(bf16[10128,128]{1,0:T(8,128)(2,1)S(1)} %get-tuple-element.11.right_ref.right_own_ref), channel_id=1, source_target_pairs={{0,17},{1,18},{2,19},{3,16},{4,21},{5,22},{6,23},{7,20},{8,25},{9,... | collective-permute-start | bytes 7778312 | tf_op jit(solution)/shard_map/ppermute | solution.py:76
  9.9 59.7 %collective-permute-start.4 = (bf16[10128,128]{1,0:T(8,128)(2,1)S(1)}, bf16[10128,128]{1,0:T(8,128)(2,1)S(1)}, u32[]{:S(2)}, u32[]{:S(2)}) collective-permute-start(bf16[10128,128]{1,0:T(8,128)(2,1)S(1)} %get-tuple-element.10.left_ref.left_own_ref), channel_id=1, source_target_pairs={{16,112},{17,117},{18,118},{19,119},{20,116},{21,121},{22,122},{23... | collective-permute-start | bytes 7778312 | tf_op jit(solution)/shard_map/ppermute | solution.py:76
  64.2 10.0 %copy-start.2 = (s32[4,2,2]{0,2,1:T(2,128)S(1)}, s32[4,2,2]{0,2,1:T(2,128)}, u32[]{:S(2)}) copy-start(s32[4,2,2]{0,2,1:T(2,128)} %param.12) | copy-start | bytes 196
  64.2 12.4 %copy-start.1 = (bf16[256,256]{1,0:T(8,128)(2,1)S(1)}, bf16[256,256]{1,0:T(8,128)(2,1)}, u32[]{:S(2)}) copy-start(bf16[256,256]{1,0:T(8,128)(2,1)} %before_ref.1) | copy-start | bytes 393220
  64.2 17.0 %copy-start = (f32[256,256]{1,0:T(8,128)S(1)}, f32[256,256]{1,0:T(8,128)}, u32[]{:S(2)}) copy-start(f32[256,256]{1,0:T(8,128)} %density_ref.1) | copy-start | bytes 786436
  64.2 12.4 %collective-permute-start.2 = (bf16[256,256]{1,0:T(8,128)(2,1)S(1)}, bf16[256,256]{1,0:T(8,128)(2,1)S(1)}, u32[]{:S(2)}, u32[]{:S(2)}) collective-permute-start(bf16[256,256]{1,0:T(8,128)(2,1)S(1)} %shard_map.97.one_ref), channel_id=1, source_target_pairs={{0,16},{1,17},{2,18},{3,19},{4,20},{5,21},{6,22},{7,23},{8,24},{9,... | collective-permute-start | bytes 393224 | tf_op jit(solution)/shard_map/ppermute | solution.py:76
  72.3 6.6 %collective-permute-start.5 = (bf16[256,256]{1,0:T(8,128)(2,1)S(1)}, bf16[256,256]{1,0:T(8,128)(2,1)S(1)}, u32[]{:S(2)}, u32[]{:S(2)}) collective-permute-start(bf16[256,256]{1,0:T(8,128)(2,1)S(1)} %get-tuple-element.16), channel_id=1, source_target_pairs={{0,17},{1,18},{2,19},{3,20},{4,21},{5,22},{6,23},{7,24},{8,25},{9,... | collective-permute-start | bytes 393224 | tf_op jit(solution)/shard_map/ppermute | solution.py:76
  72.7 8.5 %collective-permute-start.6 = (bf16[256,256]{1,0:T(8,128)(2,1)S(1)}, bf16[256,256]{1,0:T(8,128)(2,1)S(1)}, u32[]{:S(2)}, u32[]{:S(2)}) collective-permute-start(bf16[256,256]{1,0:T(8,128)(2,1)S(1)} %get-tuple-element.17), channel_id=1, source_target_pairs={{0,1},{1,2},{2,3},{3,4},{4,5},{5,6},{6,7},{7,8},{8,9},{9,10},{10,1... | collective-permute-start | bytes 393224 | tf_op jit(solution)/shard_map/ppermute | solution.py:76
